TPU v7x, 32 devices: a whole 2x2x4 slice. The times are simulated.
32 devices in a mesh: wide: 8 (over z, y), narrow: 4 (over x, core).
Axes of the slice: x: 2, y: 2, z: 4, core: 2. Of those that a mesh axis runs over, the one named last changes fastest.
Arguments:
- views: bfloat16 [192, 14, 14, 1024], P(('wide', 'narrow')), may hold values from -6 to 6
- partner: int32 [192], P(('wide', 'narrow')), may hold values from 0 to 191, as said below
- block1_params: bfloat16 [6029312], P(('wide', 'narrow')), may hold values from -0.1875 to 0.1875
- block2_params: bfloat16 [4456448], P(('wide', 'narrow')), may hold values from -0.125 to 0.125
- head_params: bfloat16 [4456448], P(('wide', 'narrow')), may hold values from -0.125 to 0.125
- norm_params: float32 [2, 10240], replicated, may hold values from -1 to 1.5, as said below
Outputs:
- loss: float32 [192], P(('wide', 'narrow'))
- views_grad: float32 [192, 14, 14, 1024], P(('wide', 'narrow'))
- block1_grad: float32 [6029312], P(('wide', 'narrow'))
- block2_grad: float32 [4456448], P(('wide', 'narrow'))
- head_grad: float32 [4456448], P(('wide', 'narrow'))
- norm_grad: float32 [2, 10240], replicated
Inputs may be any that keep to these rules, and one draw needn't show every extreme that they name: partner[partner[i]] = i and partner[i] != i: the views pair up into images, the pairing over all views drawn from the seed. `norm_params`: row 0 lies in 0.5 to 1.5, row 1 in -1 to 1.
All inputs are finite; a program needn't handle non-finite values.
Results may differ from a plain program's by a relative error of at most 0.018.
Values may be sent and summed in bfloat16 or wider, within the bound.
No kernel may reach another device: no remote copies, remote signals or barrier semaphores. Data moves between devices by JAX's collectives and lax.ppermute only.
A program may use at most 320 MiB of HBM per device.

v0:
```python
import jax
import jax.numpy as jnp
from jax import lax
from jax.sharding import PartitionSpec as P

C_IN = 1024
C_MID = 512
C_OUT = 2048
HEAD = 2048
EMBED = 128


TAU = 0.1
EPSILON = 1e-05
NORM_EPS = 1e-06
HIGHEST = lax.Precision.HIGHEST


def carve_flat(flat_params, shapes):
    pieces = []
    offset = 0
    for layout in shapes:
        length = layout[0] * layout[1]
        pieces.append(flat_params[offset : offset + length].reshape(layout))
        offset += length
    return pieces


def first_shapes():
    return [(C_IN, C_MID), (9 * C_MID, C_MID), (C_MID, C_OUT), (C_IN, C_OUT)]


def second_shapes():
    return [(C_OUT, C_MID), (9 * C_MID, C_MID), (C_MID, C_OUT)]


def head_shapes():
    return [(C_OUT, HEAD), (HEAD, EMBED)]


def split_norms(norm_params):
    widths = [C_MID, C_MID, C_OUT, C_OUT, C_MID, C_MID, C_OUT, HEAD]
    pieces = []
    offset = 0
    for span_width in widths:
        pieces.append(norm_params[:, offset : offset + span_width])
        offset += span_width
    return pieces


def patches(source, stride):
    padded = jnp.pad(source, ((0, 0), (1, 1), (1, 1), (0, 0)))
    out_side = source.shape[1] // stride
    stop_span = stride * (out_side - 1) + 1
    pieces = [
        padded[:, row_off : row_off + stop_span : stride, col_off : col_off + stop_span : stride, :]
        for row_off in range(3)
        for col_off in range(3)
    ]
    return jnp.concatenate(pieces, axis=-1)


def unpatch(patch_cot, layout, stride):
    base = jnp.zeros(layout, jnp.float32)
    _, pullback = jax.vjp(lambda source: patches(source, stride), base)
    return pullback(patch_cot)[0]


def spread_stride(strided_cot):
    count, half_rows, half_cols, channels = strided_cot.shape
    expanded = strided_cot[:, :, None, :, None, :]
    padded = jnp.pad(expanded, ((0, 0), (0, 0), (0, 1), (0, 0), (0, 1), (0, 0)))
    return padded.reshape(count, 2 * half_rows, 2 * half_cols, channels)


def weight_term(inputs, cotan, exact=None):
    left_rows = inputs.reshape(-1, inputs.shape[-1])
    right_rows = cotan.reshape(-1, cotan.shape[-1])
    return lax.dot_general(
        left_rows,
        right_rows,
        (((0,), (0,)), ((), ())),
        preferred_element_type=jnp.float32,
        precision=exact,
    )


def input_term(cotan, kernel, exact=None):
    return lax.dot_general(
        cotan,
        kernel,
        (((cotan.ndim - 1,), (1,)), ((), ())),
        preferred_element_type=jnp.float32,
        precision=exact,
    )


def silu_slope(values):
    logistic = jax.nn.sigmoid(values)
    return logistic * (1.0 + values * (1.0 - logistic))


def norm_stats(values, total_rows):
    flattened = values.reshape(-1, values.shape[-1])
    sums, squares = lax.psum(
        (jnp.sum(flattened, axis=0), jnp.sum(flattened * flattened, axis=0)), ("wide", "narrow")
    )
    center = sums / total_rows
    inv_std = lax.rsqrt(squares / total_rows - center * center + EPSILON)
    return (center, inv_std)


def norm_step(values, affine, total_rows, kept):
    stats = norm_stats(values, total_rows) if kept is None else kept
    normed = (values - stats[0]) * stats[1]
    return (normed, normed * affine[0] + affine[1], stats)


def norm_back(cotan, normed, stats, affine, total_rows):
    flat_cot = cotan.reshape(-1, cotan.shape[-1])
    flat_norm = normed.reshape(-1, normed.shape[-1])
    shift_grad, gain_grad = lax.psum(
        (jnp.sum(flat_cot, axis=0), jnp.sum(flat_cot * flat_norm, axis=0)), ("wide", "narrow")
    )
    raw_cot = (
        affine[0] * stats[1] * (cotan - shift_grad / total_rows - normed * gain_grad / total_rows)
    )
    return (raw_cot, jnp.stack([gain_grad, shift_grad]))


def block_one(inputs, kernels, norms, total_views, kept):
    w_reduce, w_spatial, w_expand, w_short = kernels
    kept = [None] * 4 if kept is None else kept
    wide_rows = total_views * inputs.shape[1] * inputs.shape[2]
    raw_one = jnp.dot(inputs, w_reduce, preferred_element_type=jnp.float32)
    normed_one, shifted_one, stat_one = norm_step(raw_one, norms[0], wide_rows, kept[0])
    act_one = jax.nn.silu(shifted_one).astype(jnp.bfloat16)
    columns_one = patches(act_one, 2)
    narrow_rows = total_views * columns_one.shape[1] * columns_one.shape[2]
    raw_two = jnp.dot(columns_one, w_spatial, preferred_element_type=jnp.float32)
    normed_two, shifted_two, stat_two = norm_step(raw_two, norms[1], narrow_rows, kept[1])
    act_two = jax.nn.silu(shifted_two).astype(jnp.bfloat16)
    raw_three = jnp.dot(act_two, w_expand, preferred_element_type=jnp.float32)
    normed_three, shifted_three, stat_three = norm_step(raw_three, norms[2], narrow_rows, kept[2])
    strided = inputs[:, ::2, ::2, :]
    raw_short = jnp.dot(strided, w_short, preferred_element_type=jnp.float32)
    normed_short, shifted_short, stat_short = norm_step(raw_short, norms[3], narrow_rows, kept[3])
    joined = shifted_three + shifted_short
    result = jax.nn.silu(joined).astype(jnp.bfloat16)
    record = {
        "normed_one": normed_one,
        "shifted_one": shifted_one,
        "act_one": act_one,
        "columns_one": columns_one,
        "normed_two": normed_two,
        "shifted_two": shifted_two,
        "act_two": act_two,
        "normed_three": normed_three,
        "strided": strided,
        "normed_short": normed_short,
        "joined": joined,
    }
    return (result, [stat_one, stat_two, stat_three, stat_short], record)


def block_one_back(inputs, kernels, norms, total_views, kept, result_cot):
    w_reduce, w_spatial, w_expand, w_short = kernels
    _, _, record = block_one(inputs, kernels, norms, total_views, kept)
    wide_rows = total_views * inputs.shape[1] * inputs.shape[2]
    narrow_rows = wide_rows // 4
    joined_cot = result_cot * silu_slope(record["joined"])
    three_cot, affine_three = norm_back(
        joined_cot, record["normed_three"], kept[2], norms[2], narrow_rows
    )
    short_cot, affine_short = norm_back(
        joined_cot, record["normed_short"], kept[3], norms[3], narrow_rows
    )
    low_three = three_cot.astype(jnp.bfloat16)
    low_short = short_cot.astype(jnp.bfloat16)
    grad_expand = weight_term(record["act_two"], low_three)
    grad_short = weight_term(record["strided"], low_short)
    act_two_cot = input_term(low_three, w_expand)
    strided_cot = input_term(low_short, w_short)
    two_cot, affine_two = norm_back(
        act_two_cot * silu_slope(record["shifted_two"]),
        record["normed_two"],
        kept[1],
        norms[1],
        narrow_rows,
    )
    low_two = two_cot.astype(jnp.bfloat16)
    grad_spatial = weight_term(record["columns_one"], low_two)
    act_one_cot = unpatch(input_term(low_two, w_spatial), record["act_one"].shape, 2)
    one_cot, affine_one = norm_back(
        act_one_cot * silu_slope(record["shifted_one"]),
        record["normed_one"],
        kept[0],
        norms[0],
        wide_rows,
    )
    low_one = one_cot.astype(jnp.bfloat16)
    grad_reduce = weight_term(inputs, low_one)
    inputs_cot = input_term(low_one, w_reduce) + spread_stride(strided_cot)
    flat_grads = jnp.concatenate(
        [
            grad_reduce.reshape(-1),
            grad_spatial.reshape(-1),
            grad_expand.reshape(-1),
            grad_short.reshape(-1),
        ]
    )
    return (inputs_cot, flat_grads, [affine_one, affine_two, affine_three, affine_short])


def block_two(inputs, kernels, norms, total_views, kept):
    w_narrow, w_middle, w_widen = kernels
    kept = [None] * 3 if kept is None else kept
    cell_rows = total_views * inputs.shape[1] * inputs.shape[2]
    raw_one = jnp.dot(inputs, w_narrow, preferred_element_type=jnp.float32)
    normed_one, shifted_one, stat_one = norm_step(raw_one, norms[0], cell_rows, kept[0])
    act_one = jax.nn.silu(shifted_one).astype(jnp.bfloat16)
    columns_one = patches(act_one, 1)
    raw_two = jnp.dot(columns_one, w_middle, preferred_element_type=jnp.float32)
    normed_two, shifted_two, stat_two = norm_step(raw_two, norms[1], cell_rows, kept[1])
    act_two = jax.nn.silu(shifted_two).astype(jnp.bfloat16)
    raw_three = jnp.dot(act_two, w_widen, preferred_element_type=jnp.float32)
    normed_three, shifted_three, stat_three = norm_step(raw_three, norms[2], cell_rows, kept[2])
    joined = shifted_three + inputs.astype(jnp.float32)
    result = jax.nn.silu(joined)
    record = {
        "normed_one": normed_one,
        "shifted_one": shifted_one,
        "act_one": act_one,
        "columns_one": columns_one,
        "normed_two": normed_two,
        "shifted_two": shifted_two,
        "act_two": act_two,
        "normed_three": normed_three,
        "joined": joined,
    }
    return (result, [stat_one, stat_two, stat_three], record)


def block_two_back(inputs, kernels, norms, total_views, kept, result_cot):
    w_narrow, w_middle, w_widen = kernels
    _, _, record = block_two(inputs, kernels, norms, total_views, kept)
    cell_rows = total_views * inputs.shape[1] * inputs.shape[2]
    joined_cot = result_cot * silu_slope(record["joined"])
    three_cot, affine_three = norm_back(
        joined_cot, record["normed_three"], kept[2], norms[2], cell_rows
    )
    low_three = three_cot.astype(jnp.bfloat16)
    grad_widen = weight_term(record["act_two"], low_three)
    act_two_cot = input_term(low_three, w_widen)
    two_cot, affine_two = norm_back(
        act_two_cot * silu_slope(record["shifted_two"]),
        record["normed_two"],
        kept[1],
        norms[1],
        cell_rows,
    )
    low_two = two_cot.astype(jnp.bfloat16)
    grad_middle = weight_term(record["columns_one"], low_two)
    act_one_cot = unpatch(input_term(low_two, w_middle), record["act_one"].shape, 1)
    one_cot, affine_one = norm_back(
        act_one_cot * silu_slope(record["shifted_one"]),
        record["normed_one"],
        kept[0],
        norms[0],
        cell_rows,
    )
    low_one = one_cot.astype(jnp.bfloat16)
    grad_narrow = weight_term(inputs, low_one)
    inputs_cot = joined_cot + input_term(low_one, w_narrow)
    flat_grads = jnp.concatenate(
        [grad_narrow.reshape(-1), grad_middle.reshape(-1), grad_widen.reshape(-1)]
    )
    return (inputs_cot, flat_grads, [affine_one, affine_two, affine_three])


def head_run(pooled, kernels, affine, total_views):
    w_hidden, w_embed = kernels
    raw_hidden = jnp.dot(
        pooled, w_hidden.astype(jnp.float32), preferred_element_type=jnp.float32, precision=HIGHEST
    )
    normed, shifted, stats = norm_step(raw_hidden, affine, total_views, None)
    hidden = jax.nn.silu(shifted)
    embed = jnp.dot(
        hidden, w_embed.astype(jnp.float32), preferred_element_type=jnp.float32, precision=HIGHEST
    )
    return (embed, stats, {"normed": normed, "shifted": shifted, "hidden": hidden})


def unit_norm(embed):
    return embed * lax.rsqrt(jnp.sum(embed * embed, axis=1, keepdims=True) + NORM_EPS)


def shards(views, partner, block1_params, block2_params, head_params, norm_params):
    views_dev = views.shape[0]
    wide_count = lax.axis_size("wide")
    narrow_count = lax.axis_size("narrow")
    total_views = views_dev * wide_count * narrow_count
    norms = split_norms(norm_params)
    first_flat = lax.all_gather(block1_params, ("wide", "narrow"), axis=0, tiled=True)
    second_flat, head_flat = (
        lax.all_gather(block2_params, ("wide", "narrow"), axis=0, tiled=True),
        lax.all_gather(head_params, ("wide", "narrow"), axis=0, tiled=True),
    )
    first_kernels = carve_flat(first_flat, first_shapes())
    second_kernels = carve_flat(second_flat, second_shapes())
    head_kernels = carve_flat(head_flat, head_shapes())
    result_one, stats_one, _ = block_one(views, first_kernels, norms[0:4], total_views, None)
    result_two, stats_two, _ = block_two(result_one, second_kernels, norms[4:7], total_views, None)
    pooled = jnp.mean(result_two, axis=(1, 2))
    embed, head_stats, head_record = head_run(pooled, head_kernels, norms[7], total_views)
    unit = unit_norm(embed).astype(jnp.bfloat16)
    device = lax.axis_index(("wide", "narrow"))
    own_ids = device * views_dev + jnp.arange(views_dev, dtype=jnp.int32)
    column = lax.all_gather(unit, "wide", axis=0, tiled=True)
    block_rows = column.shape[0]

    def piece_scores(piece):
        place = jnp.arange(piece.shape[0], dtype=jnp.int32)
        cycle_pos = place // block_rows
        within = place % block_rows
        cand_ids = (within // views_dev * narrow_count + cycle_pos) * views_dev + within % views_dev
        scores = (
            lax.dot_general(
                unit, piece, (((1,), (1,)), ((), ())), preferred_element_type=jnp.float32
            )
            / TAU
        )
        scores = jnp.where(cand_ids[None, :] == own_ids[:, None], -1e30, scores)
        return (scores, cand_ids)

    run_max = jnp.full((views_dev,), -1e30, jnp.float32)
    scores, cand_ids = piece_scores(lax.all_gather(column, "narrow", axis=0, tiled=True))
    new_max = jnp.maximum(run_max, jnp.max(scores, axis=1))
    run_sum = jnp.sum(jnp.exp(scores - new_max[:, None]), axis=1)
    run_pos = jnp.sum(jnp.where(cand_ids[None, :] == partner[:, None], scores, 0.0), axis=1)
    run_max, run_sum, run_pos = (new_max, run_sum, run_pos)
    log_total = run_max + jnp.log(run_sum)
    loss = log_total - run_pos
    factor = 1.0 / (total_views * TAU)
    piece = lax.all_gather(column, "narrow", axis=0, tiled=True)
    scores, cand_ids = piece_scores(piece)
    weights = jnp.exp(scores - log_total[:, None]) - (cand_ids[None, :] == partner[:, None]).astype(
        jnp.float32
    )
    weights = weights * factor
    anchor_acc = jnp.dot(weights, piece, preferred_element_type=jnp.float32, precision=HIGHEST)
    term = lax.dot_general(
        weights,
        unit,
        (((0,), (0,)), ((), ())),
        preferred_element_type=jnp.float32,
        precision=HIGHEST,
    )
    cand_acc = term
    anchor_acc, cand_acc = (anchor_acc, cand_acc)
    ordered = (
        cand_acc.reshape(narrow_count, wide_count, views_dev, EMBED)
        .transpose(1, 0, 2, 3)
        .reshape(-1, EMBED)
    )
    returned = lax.psum_scatter(ordered, ("wide", "narrow"), scatter_dimension=0, tiled=True)
    unit_cot = anchor_acc + returned
    _, norm_pull = jax.vjp(unit_norm, embed)
    embed_cot = norm_pull(unit_cot)[0]
    second_back, head_back = (
        lax.all_gather(block2_params, ("wide", "narrow"), axis=0, tiled=True),
        lax.all_gather(head_params, ("wide", "narrow"), axis=0, tiled=True),
    )
    second_kernels = carve_flat(second_back, second_shapes())
    head_kernels = carve_flat(head_back, head_shapes())
    w_hidden, w_embed = head_kernels
    grad_embed = weight_term(head_record["hidden"], embed_cot, HIGHEST)
    hidden_cot = input_term(embed_cot, w_embed.astype(jnp.float32), HIGHEST)
    raw_hidden_cot, head_affine = norm_back(
        hidden_cot * silu_slope(head_record["shifted"]),
        head_record["normed"],
        head_stats,
        norms[7],
        total_views,
    )
    grad_hidden = weight_term(pooled, raw_hidden_cot, HIGHEST)
    pooled_cot = input_term(raw_hidden_cot, w_hidden.astype(jnp.float32), HIGHEST)
    cells = result_two.shape[1] * result_two.shape[2]
    result_two_cot = jnp.broadcast_to(pooled_cot[:, None, None, :] / cells, result_two.shape)
    result_one_cot, second_grads, second_affines = block_two_back(
        result_one, second_kernels, norms[4:7], total_views, stats_two, result_two_cot
    )
    head_grads = jnp.concatenate([grad_hidden.reshape(-1), grad_embed.reshape(-1)])
    second_out, head_out = (
        lax.psum_scatter(second_grads, ("wide", "narrow"), scatter_dimension=0, tiled=True),
        lax.psum_scatter(head_grads, ("wide", "narrow"), scatter_dimension=0, tiled=True),
    )
    first_back = lax.all_gather(block1_params, ("wide", "narrow"), axis=0, tiled=True)
    first_kernels = carve_flat(first_back, first_shapes())
    views_cot, first_grads, first_affines = block_one_back(
        views, first_kernels, norms[0:4], total_views, stats_one, result_one_cot
    )
    first_out = lax.psum_scatter(first_grads, ("wide", "narrow"), scatter_dimension=0, tiled=True)
    norm_grad = jnp.concatenate(first_affines + second_affines + [head_affine], axis=1)
    return (loss, views_cot, first_out, second_out, head_out, norm_grad)


def solution(mesh):
    return jax.shard_map(
        shards,
        mesh=mesh,
        in_specs=(
            P(("wide", "narrow"), None, None, None),
            P(("wide", "narrow")),
            P(("wide", "narrow")),
            P(("wide", "narrow")),
            P(("wide", "narrow")),
            P(),
        ),
        out_specs=(
            P(("wide", "narrow")),
            P(("wide", "narrow"), None, None, None),
            P(("wide", "narrow")),
            P(("wide", "narrow")),
            P(("wide", "narrow")),
            P(),
        ),
        check_vma=False,
    )
```

profile of v0, /device:TPU:0, one launch (start us, length us, event | category | flops | bytes accessed | tf_op | source)
XLA Modules:
  0.0 2452.7 jit_solution(7960711247684056632)
XLA Ops:
  13.0 21.5 slice.317
  35.0 58.1 %all-gather.9.cloned.1.call-done = bf16[4456448]{0:T(1024)(128)(2,1)} async-done(((bf16[139264]{0:T(1024)(128)(2,1)}), bf16[4456448]{0:T(1024)(128)(2,1)}) %all-gather.9.cloned.1.call-update) | async-done | bytes 8912912 | tf_op jit(solution)/shard_map/all_gather | solution.py:307
  100.3 13.3 slice.343
  113.7 60.5 %all-gather.7.cloned.1.call-done = bf16[4456448]{0:T(1024)(128)(2,1)} async-done(((bf16[139264]{0:T(1024)(128)(2,1)}), bf16[4456448]{0:T(1024)(128)(2,1)}) %all-gather.7.cloned.1.call-update) | async-done | bytes 8912912 | tf_op jit(solution)/shard_map/all_gather | solution.py:306
  198.7 70.8 %all-gather.5.cloned.1.call-done = bf16[6029312]{0:T(1024)(128)(2,1)} async-done(((bf16[188416]{0:T(1024)(128)(2,1)}), bf16[6029312]{0:T(1024)(128)(2,1)}) %all-gather.5.cloned.1.call-update) | async-done | bytes 12058640 | tf_op jit(solution)/shard_map/all_gather | solution.py:304
  275.9 39.3 %all-reduce.38 = (f32[512]{0:T(512)S(1)}, f32[512]{0:T(512)S(1)}) all-reduce(f32[512]{0:T(512)S(1)} %get-tuple-element.18, f32[512]{0:T(512)S(1)} %get-tuple-element.17), channel_id=1, replica_groups=mesh['wide'=8,'narrow'=4] {'wide','narrow'}, use_global_device_ids=true, to_apply=%region_3.0 | all-reduce | flops 1024 | bytes 8192 | tf_op jit(solution)/shard_map/psum | solution.py:105
  318.3 20.0 slice.300
  338.3 20.1 slice.301
  358.4 20.0 slice.302
  378.4 20.0 slice.303
  398.4 20.0 slice.304
  418.4 12.9 slice.305
  431.3 12.9 slice.306
  488.3 40.4 %all-reduce.37 = (f32[512]{0:T(512)S(1)}, f32[512]{0:T(512)S(1)}) all-reduce(f32[512]{0:T(512)S(1)} %get-tuple-element.32, f32[512]{0:T(512)S(1)} %get-tuple-element.31), channel_id=1, replica_groups=mesh['wide'=8,'narrow'=4] {'wide','narrow'}, use_global_device_ids=true, to_apply=%region_7.8 | all-reduce | flops 1024 | bytes 8192 | tf_op jit(solution)/shard_map/psum | solution.py:105
  534.6 40.2 %all-reduce.36 = (f32[2048]{0:T(1024)S(1)}, f32[2048]{0:T(1024)S(1)}, f32[2048]{0:T(1024)S(1)}, f32[2048]{0:T(1024)S(1)}) all-reduce(f32[2048]{0:T(1024)} %get-tuple-element.20, f32[2048]{0:T(1024)S(1)} %get-tuple-element.19, f32[2048]{0:T(1024)} %get-tuple-element.16, ...), channel_id=1, replica_groups=mesh['wide'=8,'narrow'=4] {'wide','narrow'}, use_global_device_ids=true, to_apply=%region_15.16 | all-reduce | flops 8192 | bytes 65536 | tf_op jit(solution)/shard_map/psum | solution.py:105
  580.8 40.5 %all-reduce.35 = (f32[512]{0:T(512)S(1)}, f32[512]{0:T(512)S(1)}) all-reduce(f32[512]{0:T(512)S(1)} %get-tuple-element.30, f32[512]{0:T(512)S(1)} %get-tuple-element.29), channel_id=1, replica_groups=mesh['wide'=8,'narrow'=4] {'wide','narrow'}, use_global_device_ids=true, to_apply=%region_19.20 | all-reduce | flops 1024 | bytes 8192 | tf_op jit(solution)/shard_map/psum | solution.py:105
  628.0 39.5 %all-reduce.34 = (f32[512]{0:T(512)S(1)}, f32[512]{0:T(512)S(1)}) all-reduce(f32[512]{0:T(512)S(1)} %get-tuple-element.28, f32[512]{0:T(512)S(1)} %get-tuple-element.27), channel_id=1, replica_groups=mesh['wide'=8,'narrow'=4] {'wide','narrow'}, use_global_device_ids=true, to_apply=%region_23.24 | all-reduce | flops 1024 | bytes 8192 | tf_op jit(solution)/shard_map/psum | solution.py:105
  671.5 41.0 %all-reduce.33 = (f32[2048]{0:T(1024)S(1)}, f32[2048]{0:T(1024)S(1)}) all-reduce(f32[2048]{0:T(1024)S(1)} %get-tuple-element.14, f32[2048]{0:T(1024)S(1)} %get-tuple-element.13), channel_id=1, replica_groups=mesh['wide'=8,'narrow'=4] {'wide','narrow'}, use_global_device_ids=true, to_apply=%region_27.28 | all-reduce | flops 4096 | bytes 32768 | tf_op jit(solution)/shard_map/psum | solution.py:105
  721.6 39.8 %all-reduce.32 = (f32[2048]{0:T(1024)}, f32[2048]{0:T(1024)}) all-reduce(f32[2048]{0:T(1024)S(1)} %get-tuple-element.36, f32[2048]{0:T(1024)S(1)} %get-tuple-element.35), channel_id=1, replica_groups=mesh['wide'=8,'narrow'=4] {'wide','narrow'}, use_global_device_ids=true, to_apply=%region_32.33 | all-reduce | flops 4096 | bytes 32768 | tf_op jit(solution)/shard_map/psum | solution.py:105
  764.8 26.7 %all-gather = bf16[8,6,128]{2,1,0:T(8,128)(2,1)} all-gather(bf16[1,6,128]{2,1,0:T(8,128)(2,1)S(1)} %fusion.145), channel_id=1, replica_groups=mesh['wide'=8,'narrow'=4] {'wide'}, dimensions={0}, use_global_device_ids=true | all-gather | bytes 13824 | tf_op jit(solution)/shard_map/all_gather | solution.py:319
  808.6 120.3 %all-reduce.43.cloned.1.call-done = f32[192,128]{1,0:T(8,128)} async-done(((f32[192,128]{1,0:T(8,128)}), f32[192,128]{1,0:T(8,128)}) %all-reduce.43.cloned.1.call-update) | async-done | bytes 98320
  933.6 41.4 %all-reduce.31 = (f32[2048]{0:T(1024)S(1)}, f32[2048]{0:T(1024)}) all-reduce(f32[2048]{0:T(1024)} %get-tuple-element.34, f32[2048]{0:T(1024)} %get-tuple-element.33), channel_id=1, replica_groups=mesh['wide'=8,'narrow'=4] {'wide','narrow'}, use_global_device_ids=true, to_apply=%region_42.43 | all-reduce | flops 4096 | bytes 32768 | tf_op jit(solution)/shard_map/psum | solution.py:122
  975.7 9.0 convolution_multiply_fusion
  988.7 41.1 %all-reduce.30 = (f32[2048]{0:T(1024)S(1)}, f32[2048]{0:T(1024)S(1)}) all-reduce(f32[2048]{0:T(1024)} %get-tuple-element.12, f32[2048]{0:T(1024)} %get-tuple-element.11), channel_id=1, replica_groups=mesh['wide'=8,'narrow'=4] {'wide','narrow'}, use_global_device_ids=true, to_apply=%region_46.47 | all-reduce | flops 4096 | bytes 32768 | tf_op jit(solution)/shard_map/psum | solution.py:122
  1034.2 40.1 %all-reduce.29 = (f32[512]{0:T(512)S(1)}, f32[512]{0:T(512)S(1)}) all-reduce(f32[512]{0:T(512)S(1)} %get-tuple-element.26, f32[512]{0:T(512)S(1)} %get-tuple-element.25), channel_id=1, replica_groups=mesh['wide'=8,'narrow'=4] {'wide','narrow'}, use_global_device_ids=true, to_apply=%region_50.51 | all-reduce | flops 1024 | bytes 8192 | tf_op jit(solution)/shard_map/psum | solution.py:122
  1083.0 40.0 %all-reduce.28 = (f32[512]{0:T(512)S(1)}, f32[512]{0:T(512)S(1)}) all-reduce(f32[512]{0:T(512)S(1)} %get-tuple-element.24, f32[512]{0:T(512)S(1)} %get-tuple-element.23), channel_id=1, replica_groups=mesh['wide'=8,'narrow'=4] {'wide','narrow'}, use_global_device_ids=true, to_apply=%region_54.55 | all-reduce | flops 1024 | bytes 8192 | tf_op jit(solution)/shard_map/psum | solution.py:122
  1132.6 40.1 %all-reduce.27 = (f32[2048]{0:T(1024)S(1)}, f32[2048]{0:T(1024)S(1)}) all-reduce(f32[2048]{0:T(1024)S(1)} %get-tuple-element.10, f32[2048]{0:T(1024)S(1)} %get-tuple-element.8), channel_id=1, replica_groups=mesh['wide'=8,'narrow'=4] {'wide','narrow'}, use_global_device_ids=true, to_apply=%region_56.57 | all-reduce | flops 4096 | bytes 32768 | tf_op jit(solution)/shard_map/psum | solution.py:122
  1182.4 40.4 %all-reduce.26 = (f32[512]{0:T(512)S(1)}, f32[512]{0:T(512)S(1)}) all-reduce(f32[512]{0:T(512)S(1)} %get-tuple-element.22, f32[512]{0:T(512)S(1)} %get-tuple-element.21), channel_id=1, replica_groups=mesh['wide'=8,'narrow'=4] {'wide','narrow'}, use_global_device_ids=true, to_apply=%region_62.63 | all-reduce | flops 1024 | bytes 8192 | tf_op jit(solution)/shard_map/psum | solution.py:122
  1253.5 16.3 convolution_bitcast_fusion.1
  1271.8 20.9 pad.135
  1292.7 14.4 pad.134
  1307.1 14.5 pad.92
  1321.7 14.6 pad.90
  1336.2 14.6 pad.91
  1350.8 14.5 pad.231
  1365.3 14.6 pad.230
  1379.9 14.5 pad.229
  1394.4 14.5 pad.228
  1422.6 40.0 %all-reduce.25 = (f32[2048]{0:T(1024)S(1)}, f32[512]{0:T(512)S(1)}, f32[512]{0:T(512)S(1)}) all-reduce(f32[2048]{0:T(1024)S(1)} %copy-done.141, f32[512]{0:T(512)S(1)} %get-tuple-element.7, f32[512]{0:T(512)S(1)} %get-tuple-element.6), channel_id=1, replica_groups=mesh['wide'=8,'narrow'=4] {'wide','narrow'}, use_global_device_ids=true, to_apply=%region_68.69 | all-reduce | flops 3072 | bytes 24576 | tf_op jit(solution)/shard_map/psum | solution.py:122
  1473.5 9.4 copy.21
  1482.9 8.9 copy.40
  1494.7 9.6 copy.38
  1517.9 9.7 copy.42
  1532.9 9.5 copy.44
  1542.4 11.2 pad_maximum_fusion.2
  1553.7 17.5 pad_maximum_fusion.1
  1571.2 25.8 %pad_maximum_fusion = f32[6029312]{0:T(1024)} fusion(f32[2097152]{0:T(1024)} %bitcast.194, f32[1048576]{0:T(1024)} %bitcast.195, f32[2359296]{0:T(1024)S(1)} %bitcast.189, f32[524288]{0:T(1024)S(1)} %bitcast.198), kind=kLoop, calls=%fused_computation.1 | loop fusion | flops 18087936 | bytes 48234496 | tf_op jit(solution)/shard_map/concatenate | solution.py:204
  1623.8 816.4 %all-reduce.45.cloned.1.call-done = (f32[6029312]{0:T(1024)}, f32[4456448]{0:T(1024)}, f32[4456448]{0:T(1024)}) async-done(((f32[6029312]{0:T(1024)}, f32[4456448]{0:T(1024)}, f32[4456448]{0:T(1024)}), (f32[6029312]{0:T(1024)}, f32[4456448]{0:T(1024)}, f32[4456448]{0:T(1024)})) %all-reduce.45.cloned.1.call-update) | async-done | bytes 59768848
  (501 shorter events, 295.4 us)
Async XLA Ops:
  7.2 86.0 %all-gather.9.cloned.1.call-start = ((), (), s32[]{:S(2)}) async-start(), calls=%async_computation.2 | async-start | bytes 9191424 | tf_op jit(solution)/shard_map/all_gather | solution.py:307
  7.9 166.3 %all-gather.7.cloned.1.call-start = ((), (), s32[]{:S(2)}) async-start(), calls=%async_computation.1 | async-start | bytes 9191424 | tf_op jit(solution)/shard_map/all_gather | solution.py:306
  8.6 260.8 %all-gather.5.cloned.1.call-start = ((), (), s32[]{:S(2)}) async-start(), calls=%async_computation | async-start | bytes 12435456 | tf_op jit(solution)/shard_map/all_gather | solution.py:304
  9.4 919.5 %all-reduce.43.cloned.1.call-start = ((), (), s32[]{:S(2)}) async-start(), calls=%async_computation.3 | async-start | bytes 196608
  10.9 564.5 %copy-start.75 = (f32[1,2048]{1,0:T(1,128)}, f32[1,2048]{1,0:T(1,128)S(1)}, u32[]{:S(2)}) copy-start(f32[1,2048]{1,0:T(1,128)S(1)} %get-tuple-element.102) | copy-start | bytes 24580
  10.9 564.5 %copy-start.77 = (f32[1,2048]{1,0:T(1,128)}, f32[1,2048]{1,0:T(1,128)S(1)}, u32[]{:S(2)}) copy-start(f32[1,2048]{1,0:T(1,128)S(1)} %get-tuple-element.104) | copy-start | bytes 24580
  10.9 564.5 %copy-start.102 = (f32[1,2048]{1,0:T(1,128)}, f32[1,2048]{1,0:T(1,128)S(1)}, u32[]{:S(2)}) copy-start(f32[1,2048]{1,0:T(1,128)S(1)} %get-tuple-element.101) | copy-start | bytes 24580
  10.9 564.5 %copy-start.104 = (f32[1,2048]{1,0:T(1,128)}, f32[1,2048]{1,0:T(1,128)S(1)}, u32[]{:S(2)}) copy-start(f32[1,2048]{1,0:T(1,128)S(1)} %get-tuple-element.103) | copy-start | bytes 24580
  10.9 702.2 %copy-start.67 = (f32[1,2048]{1,0:T(1,128)}, f32[1,2048]{1,0:T(1,128)S(1)}, u32[]{:S(2)}) copy-start(f32[1,2048]{1,0:T(1,128)S(1)} %get-tuple-element.99) | copy-start | bytes 24580
  11.0 919.7 %copy-start.79 = (f32[1,2048]{1,0:T(1,128)}, f32[1,2048]{1,0:T(1,128)S(1)}, u32[]{:S(2)}) copy-start(f32[1,2048]{1,0:T(1,128)S(1)} %get-tuple-element.98) | copy-start | bytes 24580
  12.4 303.4 %copy-start.108 = (f32[1,512]{1,0:T(1,128)}, f32[1,512]{1,0:T(1,128)S(1)}, u32[]{:S(2)}) copy-start(f32[1,512]{1,0:T(1,128)S(1)} %get-tuple-element.113) | copy-start | bytes 6148
  12.4 303.4 %copy-start.119 = (f32[1,512]{1,0:T(1,128)}, f32[1,512]{1,0:T(1,128)S(1)}, u32[]{:S(2)}) copy-start(f32[1,512]{1,0:T(1,128)S(1)} %get-tuple-element.112) | copy-start | bytes 6148
  12.4 516.9 %copy-start.145 = (f32[1,512]{1,0:T(1,128)}, f32[1,512]{1,0:T(1,128)S(1)}, u32[]{:S(2)}) copy-start(f32[1,512]{1,0:T(1,128)S(1)} %get-tuple-element.111) | copy-start | bytes 6148
  12.4 516.9 %copy-start.161 = (f32[1,512]{1,0:T(1,128)}, f32[1,512]{1,0:T(1,128)S(1)}, u32[]{:S(2)}) copy-start(f32[1,512]{1,0:T(1,128)S(1)} %get-tuple-element.110) | copy-start | bytes 6148
  12.4 610.0 %copy-start.87 = (f32[1,512]{1,0:T(1,128)}, f32[1,512]{1,0:T(1,128)S(1)}, u32[]{:S(2)}) copy-start(f32[1,512]{1,0:T(1,128)S(1)} %get-tuple-element.109) | copy-start | bytes 6148
  12.4 610.0 %copy-start.99 = (f32[1,512]{1,0:T(1,128)}, f32[1,512]{1,0:T(1,128)S(1)}, u32[]{:S(2)}) copy-start(f32[1,512]{1,0:T(1,128)S(1)} %get-tuple-element.108) | copy-start | bytes 6148
  275.9 42.4 %copy-start = (f32[6,14,14,512]{3,2,1,0:T(8,128)}, f32[6,14,14,512]{3,2,1,0:T(8,128)S(1)}, u32[]{:S(2)}) copy-start(f32[6,14,14,512]{3,2,1,0:T(8,128)S(1)} %get-tuple-element.139) | copy-start | bytes 7225348
  338.3 80.1 %copy-start.4 = (bf16[6,16,16,512]{3,2,1,0:T(8,128)(2,1)S(1)}, bf16[6,16,16,512]{3,2,1,0:T(8,128)(2,1)}, u32[]{:S(2)}) copy-start(bf16[6,16,16,512]{3,2,1,0:T(8,128)(2,1)} %pad.78) | copy-start | bytes 4718596
  481.7 93.7 %copy-start.11 = (f32[6,7,7,2048]{3,2,1,0:T(8,128)}, f32[6,7,7,2048]{3,2,1,0:T(8,128)S(1)}, u32[]{:S(2)}) copy-start(f32[6,7,7,2048]{3,2,1,0:T(8,128)S(1)} %get-tuple-element.138) | copy-start | bytes 7225348
  488.3 46.3 %copy-start.41 = (f32[6,7,7,512]{3,2,1,0:T(8,128)}, f32[6,7,7,512]{3,2,1,0:T(8,128)S(1)}, u32[]{:S(2)}) copy-start(f32[6,7,7,512]{3,2,1,0:T(8,128)S(1)} %get-tuple-element.140) | copy-start | bytes 1806340
  579.3 43.7 %slice-start.10 = ((s8[4718592]{0:T(1024)(128)(4,1)}), s8[524288]{0:T(1024)(128)(4,1)S(1)}, s32[]{:S(2)}) async-start(s8[4718592]{0:T(1024)(128)(4,1)} %bitcast.202), calls=%async_computation.15 | async-start | bytes 1048576
  624.0 43.5 %copy-start.143 = (f32[1,512]{1,0:T(1,128)S(1)}, f32[1,512]{1,0:T(1,128)}, u32[]{:S(2)}) copy-start(f32[1,512]{1,0:T(1,128)} %get-tuple-element.106) | copy-start | bytes 6148
  624.0 44.2 %copy-start.159 = (f32[1,512]{1,0:T(1,128)S(1)}, f32[1,512]{1,0:T(1,128)}, u32[]{:S(2)}) copy-start(f32[1,512]{1,0:T(1,128)} %get-tuple-element.107) | copy-start | bytes 6148
  721.6 263.1 %copy-start.38 = (f32[6,2048]{1,0:T(8,128)}, f32[6,2048]{1,0:T(8,128)S(1)}, u32[]{:S(2)}) copy-start(f32[6,2048]{1,0:T(8,128)S(1)} %get-tuple-element.145) | copy-start | bytes 147460
  762.6 222.0 %copy-start.51 = (f32[2048]{0:T(1024)}, f32[2048]{0:T(1024)S(1)}, u32[]{:S(2)}) copy-start(f32[2048]{0:T(1024)S(1)} %get-tuple-element.121) | copy-start | bytes 24580
  762.6 222.1 %copy-start.53 = (f32[2048]{0:T(1024)}, f32[2048]{0:T(1024)S(1)}, u32[]{:S(2)}) copy-start(f32[2048]{0:T(1024)S(1)} %get-tuple-element.125) | copy-start | bytes 24580
  808.5 1631.7 %all-reduce.45.cloned.1.call-start = ((), (), s32[]{:S(2)}) async-start(), calls=%async_computation.4 | async-start | bytes 119537664
  1032.5 41.8 %copy-start.44 = (f32[6,7,7,512]{3,2,1,0:T(8,128)S(1)}, f32[6,7,7,512]{3,2,1,0:T(8,128)}, u32[]{:S(2)}) copy-start(f32[6,7,7,512]{3,2,1,0:T(8,128)} %get-tuple-element.143) | copy-start | bytes 1806340
  1032.5 41.8 %copy-start.140 = (f32[512]{0:T(512)S(1)}, f32[512]{0:T(512)}, u32[]{:S(2)}) copy-start(f32[512]{0:T(512)} %get-tuple-element.132) | copy-start | bytes 6148
  1081.2 42.3 %copy-start.135 = (f32[512]{0:T(512)S(1)}, f32[512]{0:T(512)}, u32[]{:S(2)}) copy-start(f32[512]{0:T(512)} %get-tuple-element.130) | copy-start | bytes 6148
  1081.2 43.6 %copy-start.12 = (f32[6,7,7,2048]{3,2,1,0:T(8,128)S(1)}, f32[6,7,7,2048]{3,2,1,0:T(8,128)}, u32[]{:S(2)}) copy-start(f32[6,7,7,2048]{3,2,1,0:T(8,128)} %copy-done.11) | copy-start | bytes 7225348
  1081.2 43.6 %copy-start.62 = (f32[2048]{0:T(1024)S(1)}, f32[2048]{0:T(1024)}, u32[]{:S(2)}) copy-start(f32[2048]{0:T(1024)} %copy-done.61) | copy-start | bytes 24580
  1081.2 43.6 %copy-start.65 = (f32[2048]{0:T(1024)S(1)}, f32[2048]{0:T(1024)}, u32[]{:S(2)}) copy-start(f32[2048]{0:T(1024)} %copy-done.64) | copy-start | bytes 24580
  1081.2 43.6 %copy-start.70 = (f32[2048]{0:T(1024)S(1)}, f32[2048]{0:T(1024)}, u32[]{:S(2)}) copy-start(f32[2048]{0:T(1024)} %copy-done.69) | copy-start | bytes 24580
  1081.2 43.6 %copy-start.72 = (f32[2048]{0:T(1024)S(1)}, f32[2048]{0:T(1024)}, u32[]{:S(2)}) copy-start(f32[2048]{0:T(1024)} %copy-done.71) | copy-start | bytes 24580
  1081.2 43.6 %copy-start.76 = (f32[1,2048]{1,0:T(1,128)S(1)}, f32[1,2048]{1,0:T(1,128)}, u32[]{:S(2)}) copy-start(f32[1,2048]{1,0:T(1,128)} %copy-done.75) | copy-start | bytes 24580
  1081.2 43.6 %copy-start.78 = (f32[1,2048]{1,0:T(1,128)S(1)}, f32[1,2048]{1,0:T(1,128)}, u32[]{:S(2)}) copy-start(f32[1,2048]{1,0:T(1,128)} %copy-done.77) | copy-start | bytes 24580
  1081.3 43.6 %copy-start.103 = (f32[1,2048]{1,0:T(1,128)S(1)}, f32[1,2048]{1,0:T(1,128)}, u32[]{:S(2)}) copy-start(f32[1,2048]{1,0:T(1,128)} %copy-done.102) | copy-start | bytes 24580
  1081.3 43.6 %copy-start.105 = (f32[1,2048]{1,0:T(1,128)S(1)}, f32[1,2048]{1,0:T(1,128)}, u32[]{:S(2)}) copy-start(f32[1,2048]{1,0:T(1,128)} %copy-done.104) | copy-start | bytes 24580
  1124.9 48.4 %copy-start.107 = (f32[2048]{0:T(1024)S(1)}, f32[2048]{0:T(1024)}, u32[]{:S(2)}) copy-start(f32[2048]{0:T(1024)} %get-tuple-element.158) | copy-start | bytes 24580
  1178.5 44.3 %copy-start.124 = (f32[512]{0:T(512)S(1)}, f32[512]{0:T(512)}, u32[]{:S(2)}) copy-start(f32[512]{0:T(512)} %get-tuple-element.128) | copy-start | bytes 6148
  1236.5 33.2 %slice-start.8 = ((s8[6193152]{0:T(1024)(128)(4,1)}), s8[4194304]{0:T(1024)(128)(4,1)S(1)}, s32[]{:S(2)}) async-start(s8[6193152]{0:T(1024)(128)(4,1)} %bitcast.200), calls=%async_computation.13 | async-start | bytes 8388608
  1240.4 29.4 %slice-start.9 = ((s8[6193152]{0:T(1024)(128)(4,1)}), s8[1998848]{0:T(1024)(128)(4,1)S(1)}, s32[]{:S(2)}) async-start(s8[6193152]{0:T(1024)(128)(4,1)} %bitcast.200), calls=%async_computation.14 | async-start | bytes 3997696
  1336.2 29.1 %copy-start.21 = (f32[6,7,7,512]{3,2,1,0:T(8,128)S(1)}, f32[6,7,7,512]{3,2,1,0:T(8,128)}, u32[]{:S(2)}) copy-start(f32[6,7,7,512]{3,2,1,0:T(8,128)} %get-tuple-element.83) | copy-start | bytes 1806340
  1416.1 46.6 %copy-start.63 = (f32[2048]{0:T(1024)S(1)}, f32[2048]{0:T(1024)}, u32[]{:S(2)}) copy-start(f32[2048]{0:T(1024)} %copy-done.61) | copy-start | bytes 24580
  1416.1 46.6 %copy-start.66 = (f32[2048]{0:T(1024)S(1)}, f32[2048]{0:T(1024)}, u32[]{:S(2)}) copy-start(f32[2048]{0:T(1024)} %copy-done.64) | copy-start | bytes 24580
  1416.1 46.6 %copy-start.74 = (f32[2048]{0:T(1024)S(1)}, f32[2048]{0:T(1024)}, u32[]{:S(2)}) copy-start(f32[2048]{0:T(1024)} %copy-done.73) | copy-start | bytes 24580
  1416.1 46.6 %copy-start.106 = (f32[2048]{0:T(1024)S(1)}, f32[2048]{0:T(1024)}, u32[]{:S(2)}) copy-start(f32[2048]{0:T(1024)} %get-tuple-element.114) | copy-start | bytes 24580
  (137 other events, 745.9 us)
Sparse Core Ops, SparseCore 0:
  10.8 82.2 all-gather.8
  96.0 78.1 all-gather.6
  177.0 92.4 all-gather.4
  808.6 120.1 all-reduce.42
  1597.1 843.0 all-reduce.44
where the time goes:
time: 2470 us; the launch traced here: 2450 us
  waiting for transfers between devices  1130 us (46%)
  blocking collectives  596 us (24%)
  local copies, waits for them, and re-layouts  475 us (19%)
  matrix products  135 us (5%)
  other arithmetic  102 us (4%)
    unnamed x7, waiting for transfers between devices  939 us
    psum x7, blocking collectives, norm_back(): lax.psum((jnp.sum(flat_cot, axis=0), jnp.sum(flat_cot * flat_norm, axis=0...  283 us
    psum x7, blocking collectives, norm_stats(): lax.psum((jnp.sum(flattened, axis=0), jnp.sum(flattened * flattened, axis...  281 us
    unnamed x388, local copies, waits for them, and re-layouts  133 us
    slice x9, local copies, waits for them, and re-layouts, patches(): padded[:, row_off:row_off + stop_span:stride, col_off:col_off + stop_span...  128 us
    slice x17, local copies, waits for them, and re-layouts, carve_flat(): pieces.append(flat_params[offset:offset + length].reshape(layout))  76.5 us
    all_gather x1, waiting for transfers between devices, shards(): lax.all_gather(block1_params, ('wide', 'narrow'), axis=0, tiled=True)  70.8 us
    all_gather x1, waiting for transfers between devices, shards(): lax.all_gather(block2_params, ('wide', 'narrow'), axis=0, tiled=True)  60.5 us
  transfers between devices with their start and end apart: 5, of which 5 were waited for; matrix products, arithmetic and copies ran while one was open for 4% of the time, Pallas kernels for 0%

commit v1 on v0

v1 whole, which is shorter than its diff:
```python
import jax
import jax.numpy as jnp
import numpy as np
from jax import lax
from jax.experimental import pallas as pl
from jax.experimental.pallas import tpu as pltpu
from jax.sharding import PartitionSpec as P

C_IN = 1024
C_MID = 512
C_OUT = 2048
HEAD = 2048
EMBED = 128

TAU = 0.1
EPSILON = 1e-05
NORM_EPS = 1e-06
HIGHEST = lax.Precision.HIGHEST
BOTH = ("wide", "narrow")
BF16 = jnp.bfloat16
F32 = jnp.float32
DIMS = ("NHWC", "HWIO", "NHWC")


def device_count():
    return lax.axis_size("wide") * lax.axis_size("narrow")


def swap(values, mask):
    return lax.ppermute(values, BOTH, [(i, i ^ mask) for i in range(device_count())])


def bit_groups_of(count):
    groups = [[1]]
    bit = 2
    while bit < count:
        if 2 * bit < count:
            groups.append([bit, 2 * bit, 3 * bit])
        else:
            groups.append([bit])
        bit *= 4
    return groups


def bit_groups():
    return bit_groups_of(device_count())


def all_sum(values):
    for masks in bit_groups():
        others = [swap(values, mask) for mask in masks]
        values = values + others[0]
        if len(others) == 3:
            values = values + (others[1] + others[2])
    return values


def reorder_kernel(device, source, target):
    groups = bit_groups_of(source.shape[0])
    for i in range(source.shape[0]):
        offset = jnp.bitwise_xor(device[0], i)
        place = jnp.int32(0)
        width = 0
        for masks in reversed(groups):
            bits = len(masks).bit_length()
            low = masks[0].bit_length() - 1
            place += ((offset >> low) & (2**bits - 1)) << width
            width += bits
        target[i] = source[place]


def all_blocks(values):
    gathered = values[None]
    for masks in reversed(bit_groups()):
        gathered = jnp.concatenate([gathered] + [swap(gathered, mask) for mask in masks], axis=0)
    return pl.pallas_call(
        reorder_kernel,
        out_shape=jax.ShapeDtypeStruct(gathered.shape, gathered.dtype),
        in_specs=[
            pl.BlockSpec(memory_space=pltpu.SMEM),
            pl.BlockSpec(memory_space=pltpu.VMEM),
        ],
        out_specs=pl.BlockSpec(memory_space=pltpu.VMEM),
        compiler_params=pltpu.CompilerParams(vmem_limit_bytes=48 << 20),
        cost_estimate=pl.CostEstimate(
            flops=0, bytes_accessed=8 * np.prod(gathered.shape).item(), transcendentals=0
        ),
    )(lax.axis_index(BOTH).reshape(1), gathered)


def copy_kernel(device, source, target):
    target[...] = source[...]


def add_kernel(device, *refs):
    ways = len(refs) // 3
    for way in range(ways):
        first, second, target = refs[2 * way], refs[2 * way + 1], refs[2 * ways + way]
        target[...] = (first[...].astype(F32) + second[...].astype(F32)).astype(BF16)


def copy_blocks(source, count, place):
    block = (1, *source.shape[1:])
    shape = (count, *source.shape[1:])
    return pl.pallas_call(
        copy_kernel,
        out_shape=jax.ShapeDtypeStruct(shape, source.dtype),
        grid_spec=pltpu.PrefetchScalarGridSpec(
            num_scalar_prefetch=1,
            grid=(count,),
            in_specs=[pl.BlockSpec(block, lambda i, device: (place(i, device[0]), 0, 0))],
            out_specs=pl.BlockSpec(block, lambda i, device: (i, 0, 0)),
        ),
        cost_estimate=pl.CostEstimate(
            flops=0, bytes_accessed=4 * np.prod(shape).item(), transcendentals=0
        ),
    )(lax.axis_index(BOTH).reshape(1), source)


def add_blocks(source, incoming, count, places):
    ways = len(places)
    block = (1, *source.shape[1:])

    def read(place):
        return pl.BlockSpec(block, lambda i, device: (place(i, device[0]), 0, 0))

    shape = jax.ShapeDtypeStruct((count, *source.shape[1:]), BF16)
    size = np.prod(shape.shape).item()
    return pl.pallas_call(
        add_kernel,
        out_shape=[shape] * ways,
        grid_spec=pltpu.PrefetchScalarGridSpec(
            num_scalar_prefetch=1,
            grid=(count,),
            in_specs=[read(place) for pair in places for place in pair],
            out_specs=[pl.BlockSpec(block, lambda i, device: (i, 0, 0))] * ways,
        ),
        compiler_params=pltpu.CompilerParams(vmem_limit_bytes=24 << 20),
        cost_estimate=pl.CostEstimate(
            flops=size * ways, bytes_accessed=6 * size * ways, transcendentals=0
        ),
    )(lax.axis_index(BOTH).reshape(1), *([source, incoming] * ways))


class ScatterSum:
    def __init__(self, data, base):
        self.count = device_count()
        self.base = base
        self.size = data.shape[0]
        self.width = self.size
        self.source = data
        self.incoming = None
        self.folded = False
        self.live = [True] * self.count
        self.stage = 0
        self.stages = self.count.bit_length() - 1
        self.crossed = self.size > 4

    def bit(self, device):
        if self.crossed and self.stage in (1, 2) and device & 1:
            return 3 - self.stage
        return self.stage

    def halves(self, other):
        stage, crossed = self.stage, self.crossed

        def place(i, device):
            core = device & 1
            if crossed and stage in (1, 2):
                bit = stage + core * (3 - 2 * stage)
            else:
                bit = stage
            value = ((device >> bit) & 1) ^ int(other)
            at = core if crossed and stage == 1 else 0
            return ((i >> at) << (at + 1)) | (value << at) | (i & ((1 << at) - 1))

        return place

    def within(self, place):
        if not self.folded:
            return place
        return lambda i, device: 2 * place(i, device) + (device & 1)

    def prepare(self):
        self.split = self.size > 1 << self.stage
        if self.split:
            self.width //= 2
            keep, send = self.halves(False), self.halves(True)
            if self.incoming is None:
                self.folded = True
                return copy_blocks(self.source, self.width, send)
            self.source, outgoing = add_blocks(
                self.source,
                self.incoming,
                self.width,
                [(self.within(keep), keep), (self.within(send), send)],
            )
            self.folded = False
            return outgoing

        def same(i, device):
            return i

        (self.source,) = add_blocks(
            self.source, self.incoming, self.width, [(self.within(same), same)]
        )
        self.folded = False
        return self.source

    def send(self, outgoing):
        pairs = []
        for device in range(self.count):
            bit = 1 << self.bit(device)
            if self.split:
                pairs.append((device, device ^ bit))
            elif self.live[device] and (device ^ self.base) & bit:
                pairs.append((device, device ^ bit))
                self.live[device] = False
        self.incoming = lax.ppermute(outgoing, BOTH, pairs)
        self.stage += 1

    def done(self):
        return self.stage == self.stages

    def result(self):
        return self.source[0].astype(F32) + self.incoming[0].astype(F32)


def step(groups, held):
    groups = [group for group in groups if not group.done()]
    outgoing = [group.prepare() for group in groups]
    held, outgoing = lax.optimization_barrier((held, outgoing))
    for group, array in zip(groups, outgoing):
        group.send(array)
    return held


def unflatten_kernel(order, source, target):
    for at in range(0, target.shape[0], 64):
        sorted_rows = jnp.dot(
            order[...], source[4 * at : 4 * at + 256, :], preferred_element_type=F32
        )
        for part in range(4):
            target[at : at + 64, part * C_MID : (part + 1) * C_MID] = sorted_rows[
                64 * part : 64 * part + 64, :
            ].astype(BF16)


def unflatten(flat, first, rows):
    tile = 256
    while first % (4 * tile):
        tile //= 2
    order = np.zeros((256, 256), np.float32)
    for row in range(256):
        order[row, 4 * (row % 64) + row // 64] = 1.0
    return pl.pallas_call(
        unflatten_kernel,
        out_shape=jax.ShapeDtypeStruct((rows, 4 * C_MID), BF16),
        grid=(rows // tile,),
        in_specs=[
            pl.BlockSpec((256, 256), lambda i: (0, 0)),
            pl.BlockSpec((4 * tile, C_MID), lambda i: (first // (4 * tile) + i, 0)),
        ],
        out_specs=pl.BlockSpec((tile, 4 * C_MID), lambda i: (i, 0)),
        compiler_params=pltpu.CompilerParams(vmem_limit_bytes=24 << 20),
        cost_estimate=pl.CostEstimate(
            flops=2048 * rows * C_MID, bytes_accessed=16 * rows * C_MID, transcendentals=0
        ),
    )(jnp.asarray(order, BF16), flat)


def flat_grad_kernel(inputs, cotan, target, scratch):
    rows = inputs.shape[1]
    grad = lax.dot_general(
        inputs[...], cotan[...], (((0,), (0,)), ((), ())), preferred_element_type=F32
    )
    for lane in range(4):
        for part in range(4):
            at = part * C_MID + lane * 128
            scratch[lane, pl.ds(part, rows, stride=4), :] = grad[:, at : at + 128]
        target[:, lane * 128 : (lane + 1) * 128] = scratch[lane].astype(BF16)


def flat_grad(inputs, cotan):
    inputs = inputs.reshape(-1, inputs.shape[-1])
    cotan = cotan.reshape(-1, cotan.shape[-1])
    count, depth = inputs.shape
    tile = 128
    return pl.pallas_call(
        flat_grad_kernel,
        out_shape=jax.ShapeDtypeStruct((4 * depth, C_MID), BF16),
        grid=(depth // tile,),
        in_specs=[
            pl.BlockSpec((count, tile), lambda i: (0, i)),
            pl.BlockSpec((count, 4 * C_MID), lambda i: (0, 0)),
        ],
        out_specs=pl.BlockSpec((4 * tile, C_MID), lambda i: (i, 0)),
        scratch_shapes=[pltpu.VMEM((4, 4 * tile, 128), F32)],
        compiler_params=pltpu.CompilerParams(vmem_limit_bytes=24 << 20),
        cost_estimate=pl.CostEstimate(
            flops=2 * count * depth * 4 * C_MID,
            bytes_accessed=2 * count * (depth + 4 * C_MID) + 8 * depth * C_MID,
            transcendentals=0,
        ),
    )(inputs, cotan)


def split_norms(norm_params):
    widths = [C_MID, C_MID, C_OUT, C_OUT, C_MID, C_MID, C_OUT, HEAD]
    pieces = []
    offset = 0
    for span_width in widths:
        pieces.append(norm_params[:, offset : offset + span_width])
        offset += span_width
    return pieces


def moments(values):
    rows = values.reshape(-1, values.shape[-1])
    return jnp.stack([jnp.sum(rows, axis=0), jnp.sum(rows * rows, axis=0)])


def stats_of(sums, total_rows):
    center = sums[0] / total_rows
    inv_std = lax.rsqrt(sums[1] / total_rows - center * center + EPSILON)
    return center, inv_std


def silu_slope(values):
    logistic = jax.nn.sigmoid(values)
    return logistic * (1.0 + values * (1.0 - logistic))


class Norm:
    def __init__(self, raw, sums, affine, total_rows):
        self.raw = raw
        self.affine = affine
        self.total_rows = total_rows
        self.center, self.inv_std = stats_of(sums, total_rows)

    def normed(self):
        return (self.raw - self.center) * self.inv_std

    def shifted(self):
        return self.normed() * self.affine[0] + self.affine[1]

    def partial_grads(self, cotan):
        rows = cotan.reshape(-1, cotan.shape[-1])
        normed = self.normed().reshape(-1, cotan.shape[-1])
        return jnp.stack([jnp.sum(rows * normed, axis=0), jnp.sum(rows, axis=0)])

    def pull(self, cotan, grads):
        return (
            self.affine[0]
            * self.inv_std
            * (cotan - grads[1] / self.total_rows - self.normed() * (grads[0] / self.total_rows))
        )


def times(values, kernel):
    return jnp.dot(values, kernel, preferred_element_type=F32)


def times_back(cotan, kernel):
    return lax.dot_general(
        cotan, kernel, (((cotan.ndim - 1,), (1,)), ((), ())), preferred_element_type=F32
    )


def kernel_grad(inputs, cotan):
    return lax.dot_general(
        inputs.reshape(-1, inputs.shape[-1]),
        cotan.reshape(-1, cotan.shape[-1]),
        (((0,), (0,)), ((), ())),
        preferred_element_type=F32,
    )


def conv(values, kernel, stride):
    taps = kernel.reshape(3, 3, C_MID, C_MID)
    return lax.conv_general_dilated(
        values,
        taps,
        (stride, stride),
        ((1, 1), (1, 1)),
        dimension_numbers=DIMS,
        preferred_element_type=F32,
    )


def conv_back(cotan, kernel, stride):
    taps = kernel.reshape(3, 3, C_MID, C_MID)[::-1, ::-1].transpose(0, 1, 3, 2)
    after = stride
    return lax.conv_general_dilated(
        cotan,
        taps,
        (1, 1),
        ((1, after), (1, after)),
        lhs_dilation=(stride, stride),
        dimension_numbers=DIMS,
        preferred_element_type=F32,
    )


def conv_kernel_grad(values, cotan, stride):
    after = 2 - stride
    grad = lax.conv_general_dilated(
        values,
        cotan,
        (1, 1),
        ((1, after), (1, after)),
        rhs_dilation=(stride, stride),
        dimension_numbers=("CHWN", "IHWO", "HWNC"),
        preferred_element_type=F32,
    )
    return grad.reshape(9 * C_MID, C_MID)


def exact_times(values, kernel, contract):
    high = lax.reduce_precision(values, 8, 7)
    low = values - high
    count = values.shape[0]
    terms = jnp.concatenate([high, low], axis=0).astype(BF16)
    product = lax.dot_general(
        terms, kernel, (((1,), (contract,)), ((), ())), preferred_element_type=F32
    )
    return product[:count] + product[count:]


def pad_side(values, size):
    return lax.pad(
        values,
        jnp.zeros((), values.dtype),
        ((0, 0, 0), (0, 0, 0), (0, size - values.shape[2], 0), (0, 0, 0)),
    )


def input_grad_kernel(cotan, kernel, strided, target, spread):
    side = target.shape[1]
    grad = lax.dot_general(
        cotan[0].reshape(-1, C_MID), kernel[...], (((1,), (1,)), ((), ())), preferred_element_type=F32
    )
    spread[...] = jnp.zeros_like(spread)
    for lane in range(C_IN // 128):
        for row in range(strided.shape[1]):
            spread[lane, pl.ds(32 * row, 8, stride=2), :] = strided[
                0, row, :, lane * 128 : (lane + 1) * 128
            ]
    for lane in range(C_IN // 128):
        total = grad[:, lane * 128 : (lane + 1) * 128] + spread[lane]
        target[0, :, :, lane * 128 : (lane + 1) * 128] = total.reshape(side, 16, 128)[:, :side, :]


def input_grad(cotan, kernel, strided):
    count, side = cotan.shape[:2]
    return pl.pallas_call(
        input_grad_kernel,
        out_shape=jax.ShapeDtypeStruct((count, side, side, C_IN), F32),
        grid=(count,),
        in_specs=[
            pl.BlockSpec((1, side, 16, C_MID), lambda i: (i, 0, 0, 0)),
            pl.BlockSpec((C_IN, C_MID), lambda i: (0, 0)),
            pl.BlockSpec((1, side // 2, 8, C_IN), lambda i: (i, 0, 0, 0)),
        ],
        out_specs=pl.BlockSpec((1, side, side, C_IN), lambda i: (i, 0, 0, 0)),
        scratch_shapes=[pltpu.VMEM((C_IN // 128, side * 16, 128), F32)],
        compiler_params=pltpu.CompilerParams(vmem_limit_bytes=24 << 20),
        cost_estimate=pl.CostEstimate(
            flops=2 * count * side * 16 * C_IN * C_MID,
            bytes_accessed=count * side * 16 * (2 * C_MID + 5 * C_IN),
            transcendentals=0,
        ),
    )(cotan, kernel, strided)


def unit_norm(embed):
    return embed * lax.rsqrt(jnp.sum(embed * embed, axis=1, keepdims=True) + NORM_EPS)


def contrast(unit, partner, total_views):
    ids = jnp.arange(total_views, dtype=jnp.int32)
    scores = (
        lax.dot_general(unit, unit, (((1,), (1,)), ((), ())), preferred_element_type=F32) / TAU
    )
    scores = jnp.where(ids[None, :] == ids[:, None], -1e30, scores)
    highest = jnp.max(scores, axis=1)
    log_total = highest + jnp.log(jnp.sum(jnp.exp(scores - highest[:, None]), axis=1))
    match = ids[None, :] == partner[:, None]
    loss = log_total - jnp.sum(jnp.where(match, scores, 0.0), axis=1)
    weights = (
        jnp.exp(scores - log_total[:, None])
        + jnp.exp(scores - log_total[None, :])
        - 2.0 * match.astype(F32)
    ) * (1.0 / (total_views * TAU))
    unit_cot = jnp.dot(weights, unit.astype(F32), preferred_element_type=F32, precision=HIGHEST)
    return loss, unit_cot


def head_kernel_grads(pooled, raw_cot, hidden, embed_cot, block):
    first = lax.axis_index(BOTH) * block
    split = C_OUT * HEAD
    rows = -(-block // HEAD)
    if block % HEAD:
        rows += 1
    row_at = first // HEAD
    padded = jnp.pad(pooled, ((0, 0), (0, rows)))
    left = lax.dynamic_slice_in_dim(padded, jnp.minimum(row_at, C_OUT), rows, axis=1)
    hidden_part = lax.dot_general(
        left, raw_cot, (((0,), (0,)), ((), ())), preferred_element_type=F32, precision=HIGHEST
    ).reshape(-1)
    if block % HEAD:
        hidden_part = lax.dynamic_slice_in_dim(hidden_part, first - row_at * HEAD, block)
    embed_rows = block // EMBED
    padded = jnp.pad(hidden, ((0, 0), (embed_rows, embed_rows)))
    at = jnp.clip((first - split) // EMBED + embed_rows, 0, HEAD + embed_rows)
    left = lax.dynamic_slice_in_dim(padded, at, embed_rows, axis=1)
    embed_part = lax.dot_general(
        left, embed_cot, (((0,), (0,)), ((), ())), preferred_element_type=F32, precision=HIGHEST
    ).reshape(-1)
    place = first + jnp.arange(block, dtype=jnp.int32)
    return jnp.where(place < split, hidden_part, embed_part)


def placed(rows, *pieces):
    flat = jnp.zeros((rows, C_MID), BF16)
    for at, piece in pieces:
        flat = lax.dynamic_update_slice(flat, piece.astype(BF16), (at, 0))
    return flat


def tied(*values):
    return lax.optimization_barrier(values)


def shards(views, partner, block1_params, block2_params, head_params, norm_params):
    views_dev = views.shape[0]
    count = device_count()
    total_views = views_dev * count
    device = lax.axis_index(BOTH)
    norms = split_norms(norm_params)

    def gather(flat):
        return lax.all_gather(flat.reshape(-1, C_MID), BOTH, axis=0, tiled=True)

    first = gather(block1_params)
    second = gather(block2_params)
    head = gather(head_params)
    strided = views[:, ::2, ::2, :]
    partners = all_blocks(partner[:, None]).reshape(-1)
    first, strided, partners = tied(first, strided, partners)
    w_reduce = first[:1024]
    w_spatial = first[1024:5632]

    side = views.shape[1]
    wide_rows = total_views * side * side
    half = side // 2
    rows = total_views * half * half

    raw_one = times(views, w_reduce)
    w_short = unflatten(first, 7680, C_IN)
    raw_short = times(strided, w_short)
    sums, raw_short = tied(all_sum(moments(raw_one)), raw_short)
    norm_one = Norm(raw_one, sums, norms[0], wide_rows)
    act_one = jax.nn.silu(norm_one.shifted()).astype(BF16)
    raw_two = conv(act_one, w_spatial, 2)
    w_expand = unflatten(first, 5632, C_MID)
    sums, w_expand = tied(all_sum(moments(raw_two)), w_expand)
    norm_two = Norm(raw_two, sums, norms[1], rows)
    act_two = jax.nn.silu(norm_two.shifted()).astype(BF16)
    raw_three = times(act_two, w_expand)
    sums = all_sum(jnp.concatenate([moments(raw_three), moments(raw_short)], axis=0))
    norm_three = Norm(raw_three, sums[:2], norms[2], rows)
    norm_short = Norm(raw_short, sums[2:], norms[3], rows)
    joined_one = norm_three.shifted() + norm_short.shifted()
    result_one = jax.nn.silu(joined_one).astype(BF16)

    w_narrow = second[:2048]
    w_middle = second[2048:6656]
    raw_five = times(result_one, w_narrow)
    w_widen = unflatten(second, 6656, C_MID)
    sums, w_widen = tied(all_sum(moments(raw_five)), w_widen)
    norm_five = Norm(raw_five, sums, norms[4], rows)
    act_three = jax.nn.silu(norm_five.shifted()).astype(BF16)
    raw_six = conv(act_three, w_middle, 1)
    norm_six = Norm(raw_six, all_sum(moments(raw_six)), norms[5], rows)
    act_four = jax.nn.silu(norm_six.shifted()).astype(BF16)
    raw_seven = times(act_four, w_widen)
    w_hidden = unflatten(head, 0, C_OUT)
    w_embed = head[4 * C_OUT :].reshape(HEAD, EMBED)
    sums, w_hidden, w_embed = tied(all_sum(moments(raw_seven)), w_hidden, w_embed)
    norm_seven = Norm(raw_seven, sums, norms[6], rows)
    joined_two = norm_seven.shifted() + result_one.astype(F32)
    pooled_own = jnp.mean(jax.nn.silu(joined_two), axis=(1, 2))

    pooled = all_blocks(pooled_own).reshape(total_views, C_OUT)
    raw_hidden = exact_times(pooled, w_hidden, 0)
    norm_head = Norm(raw_hidden, moments(raw_hidden), norms[7], total_views)
    shifted_head = norm_head.shifted()
    hidden = jax.nn.silu(shifted_head)
    embed = exact_times(hidden, w_embed, 0)
    losses, unit_cot = contrast(unit_norm(embed).astype(BF16), partners, total_views)
    _, norm_pull = jax.vjp(unit_norm, embed)
    embed_cot = norm_pull(unit_cot)[0]
    hidden_cot = exact_times(embed_cot, w_embed, 1) * silu_slope(shifted_head)
    grads_head = norm_head.partial_grads(hidden_cot)
    raw_hidden_cot = norm_head.pull(hidden_cot, grads_head)
    own_cot = lax.dynamic_slice_in_dim(raw_hidden_cot, device * views_dev, views_dev, axis=0)
    pooled_cot = exact_times(own_cot, w_hidden, 1)

    joined_cot = (pooled_cot / (half * half))[:, None, None, :] * silu_slope(joined_two)
    head_out = head_kernel_grads(pooled, raw_hidden_cot, hidden, embed_cot, head_params.shape[0])
    loss = lax.dynamic_slice_in_dim(losses, device * views_dev, views_dev)
    grads_seven, head_out, loss = tied(all_sum(norm_seven.partial_grads(joined_cot)), head_out, loss)
    low_seven = norm_seven.pull(joined_cot, grads_seven).astype(BF16)
    act_four_cot = times_back(low_seven, w_widen) * silu_slope(norm_six.shifted())
    grad_widen = flat_grad(act_four, low_seven)
    grads_six, grad_widen = tied(all_sum(norm_six.partial_grads(act_four_cot)), grad_widen)
    low_six = norm_six.pull(act_four_cot, grads_six).astype(BF16)
    act_three_cot = conv_back(low_six, w_middle, 1) * silu_slope(norm_five.shifted())
    grad_middle = conv_kernel_grad(act_three, low_six, 1).astype(BF16)
    grads_five, grad_middle = tied(all_sum(norm_five.partial_grads(act_three_cot)), grad_middle)
    low_five = norm_five.pull(act_three_cot, grads_five).astype(BF16)
    result_one_cot = joined_cot + times_back(low_five, w_narrow)
    grad_narrow = kernel_grad(result_one, low_five)

    joined_one_cot = result_one_cot * silu_slope(joined_one)
    grads_join = all_sum(
        jnp.concatenate(
            [
                norm_three.partial_grads(joined_one_cot),
                norm_short.partial_grads(joined_one_cot)[:1],
            ],
            axis=0,
        )
    )
    second_rows = second.shape[0] // count
    first_rows = first.shape[0] // count
    sum_second = ScatterSum(
        placed(second.shape[0], (0, grad_narrow), (2048, grad_middle), (6656, grad_widen)).reshape(
            count, second_rows, C_MID
        ),
        0,
    )
    grads_join = step([sum_second], grads_join)
    grads_three = grads_join[:2]
    grads_short = jnp.stack([grads_join[2], grads_join[1]])
    low_three = norm_three.pull(joined_one_cot, grads_three).astype(BF16)
    low_short = norm_short.pull(joined_one_cot, grads_short).astype(BF16)
    act_two_cot = times_back(low_three, w_expand) * silu_slope(norm_two.shifted())
    grad_expand = flat_grad(act_two, low_three)
    grad_short = flat_grad(strided, low_short)
    strided_cot = times_back(pad_side(low_short, 8), w_short)
    grads_two = all_sum(norm_two.partial_grads(act_two_cot))
    middle = count // 2 * first_rows
    sum_late = ScatterSum(
        placed(
            middle, (0, grad_expand[middle - 5632 :]), (7680 - middle, grad_short)
        ).reshape(count // 2, first_rows, C_MID),
        count // 2,
    )
    grads_two = step([sum_second, sum_late], grads_two)
    low_two = norm_two.pull(act_two_cot, grads_two).astype(BF16)
    act_one_cot = conv_back(low_two, w_spatial, 2) * silu_slope(norm_one.shifted())
    grad_spatial = conv_kernel_grad(act_one, low_two, 2)
    grads_one = all_sum(norm_one.partial_grads(act_one_cot))
    sum_early = ScatterSum(
        placed(
            middle, (1024, grad_spatial), (5632, grad_expand[: middle - 5632])
        ).reshape(count // 2, first_rows, C_MID),
        0,
    )
    grads_one = step([sum_second, sum_late, sum_early], grads_one)
    low_one = norm_one.pull(act_one_cot, grads_one).astype(BF16)
    grad_reduce = kernel_grad(views, low_one)
    reduce_blocks = count // 8
    sum_reduce = ScatterSum(
        placed(reduce_blocks * first_rows, (0, grad_reduce)).reshape(
            reduce_blocks, first_rows, C_MID
        ),
        0,
    )
    sums = [sum_reduce, sum_early, sum_late, sum_second]
    low_one = step(sums, low_one)
    views_cot = input_grad(pad_side(low_one, 16), w_reduce, strided_cot)
    while not all(group.done() for group in sums):
        step(sums, ())

    second_out = sum_second.result().reshape(-1)
    early = sum_early.result()
    early = early + jnp.where(device < reduce_blocks, sum_reduce.result(), 0.0)
    first_out = jnp.where(device < count // 2, early, sum_late.result()).reshape(-1)
    norm_grad = jnp.concatenate(
        [
            grads_one,
            grads_two,
            grads_three,
            grads_short,
            grads_five,
            grads_six,
            grads_seven,
            grads_head,
        ],
        axis=1,
    )
    return (loss, views_cot, first_out, second_out, head_out, norm_grad)


def solution(mesh):
    return jax.shard_map(
        shards,
        mesh=mesh,
        in_specs=(
            P(BOTH, None, None, None),
            P(BOTH),
            P(BOTH),
            P(BOTH),
            P(BOTH),
            P(),
        ),
        out_specs=(
            P(BOTH),
            P(BOTH, None, None, None),
            P(BOTH),
            P(BOTH),
            P(BOTH),
            P(),
        ),
        check_vma=False,
    )
```

time: 2470 us -> 712 us (0.29)
  waiting for transfers between devices: 1130 us -> 262 us
  blocking collectives: 596 us -> 0 us
  local copies, waits for them, and re-layouts: 475 us -> 96 us
  starting transfers between devices: 0.19 us -> 135 us
  Pallas kernels: 0 us -> 74.9 us
  other arithmetic: 102 us -> 38.3 us
  matrix products: 135 us -> 77.3 us
    unnamed x7 -> x3, waiting for transfers between devices: 939 us -> 0.05 us
    psum x14 -> x0, blocking collectives: 564 us -> none  [the longest x7 283 us: norm_back(): lax.psum((jnp.sum(flat_cot, axis=0), jnp.sum(flat_cot * flat_norm, axis=0...]
    slice x29 -> x9, local copies, waits for them, and re-layouts: 229 us -> 20.4 us  [the longest x1 18.3 us: shards(): strided = views[:, ::2, ::2, :]]
    ppermute x0 -> x118, waiting for transfers between devices: none -> 157 us  [the longest x20 81.6 us: send(): self.incoming = lax.ppermute(outgoing, BOTH, pairs)]
    ppermute x0 -> x118, starting transfers between devices: none -> 135 us  [the longest x98 115 us: swap(): lax.ppermute(values, BOTH, [(i, i ^ mask) for i in range(device_count())])]
    unnamed x388 -> x330, local copies, waits for them, and re-layouts: 133 us -> 41.5 us
    pad x7 -> x1, local copies, waits for them, and re-layouts: 85.4 us -> 0.2 us  [pad_side(): lax.pad(values, jnp.zeros((), values.dtype), ((0, 0, 0), (0, 0, 0), (0, s...]
    all_gather x3, waiting for transfers between devices: 189 us -> 104 us  [gather(): return lax.all_gather(flat.reshape(-1, C_MID), BOTH, axis=0, tiled=True)]
  transfers between devices with their start and end apart: 5 -> 121, of which waited for: 5 -> 59; matrix products, arithmetic and copies ran while one was open for 4% -> 17% of each run, Pallas kernels for 0% -> 9%
where the time goes in v1:
time: 712 us; the launch traced here: 700 us
  waiting for transfers between devices  262 us (37%)
  starting transfers between devices  135 us (19%)
  local copies, waits for them, and re-layouts  96 us (13%)
  matrix products  77.3 us (11%)
  Pallas kernels  74.9 us (11%)
  other arithmetic  38.3 us (5%)
  between operations  17.1 us (2%)
    ppermute x98, starting transfers between devices, swap(): lax.ppermute(values, BOTH, [(i, i ^ mask) for i in range(device_count())])  115 us
    all_gather x3, waiting for transfers between devices, gather(): return lax.all_gather(flat.reshape(-1, C_MID), BOTH, axis=0, tiled=True)  104 us
    ppermute x20, waiting for transfers between devices, send(): self.incoming = lax.ppermute(outgoing, BOTH, pairs)  81.6 us
    ppermute x98, waiting for transfers between devices, swap(): lax.ppermute(values, BOTH, [(i, i ^ mask) for i in range(device_count())])  75.9 us
    unnamed x330, local copies, waits for them, and re-layouts  41.5 us
    pallas_call x16, Pallas kernels, add_blocks(): pl.pallas_call(add_kernel, out_shape=[shape] * ways, grid_spec=pltpu.Pref...  27.1 us
    pallas_call x4, Pallas kernels, copy_blocks(): pl.pallas_call(copy_kernel, out_shape=jax.ShapeDtypeStruct(shape, source....  24.5 us
    ppermute x20, starting transfers between devices, send(): self.incoming = lax.ppermute(outgoing, BOTH, pairs)  19.3 us
  transfers between devices with their start and end apart: 121, of which 59 were waited for; matrix products, arithmetic and copies ran while one was open for 17% of the time, Pallas kernels for 9%

profile of v1, /device:TPU:0, one launch (start us, length us, event | category | flops | bytes accessed | tf_op | source)
XLA Modules:
  0.0 700.1 jit_solution(12425390651858555096)
XLA Ops:
  13.1 5.0 collective-permute-start.2
  19.8 2.9 collective-permute-done.1
  26.3 3.2 collective-permute-done.3
  29.6 18.3 %slice.230 = bf16[6,7,7,1024]{3,2,1,0:T(8,128)(2,1)S(1)} slice(bf16[6,14,14,1024]{3,2,1,0:T(8,128)(2,1)} %param.10), slice={[0:6:1], [0:14:2], [0:14:2], [0:1024:1]} | slice | bytes 1204224 | tf_op jit(solution)/shard_map/slice | solution.py:548
  49.4 58.4 %all-gather.4.cloned.1.call-done.source = bf16[11776,512]{1,0:T(8,128)(2,1)} async-done(((bf16[368,512]{1,0:T(8,128)(2,1)}), bf16[11776,512]{1,0:T(8,128)(2,1)}) %all-gather.4.cloned.1.call-update) | async-done | bytes 12058640 | tf_op jit(solution)/shard_map/all_gather | solution.py:543
  107.8 4.0 fusion.118
  128.6 4.6 fusion.122
  164.3 2.9 collective-permute-done.26
  169.3 20.3 %all-gather.6.cloned.1.call-done.source = bf16[8704,512]{1,0:T(8,128)(2,1)} async-done(((bf16[272,512]{1,0:T(8,128)(2,1)}), bf16[8704,512]{1,0:T(8,128)(2,1)}) %all-gather.6.cloned.1.call-update) | async-done | bytes 8912912 | tf_op jit(solution)/shard_map/all_gather | solution.py:543
  189.5 3.1 fusion.123
  204.8 3.6 copy-done.4
  213.2 3.3 fusion.121
  245.6 25.6 %all-gather.8.cloned.1.call-done.source = bf16[8704,512]{1,0:T(8,128)(2,1)} async-done(((bf16[272,512]{1,0:T(8,128)(2,1)}), bf16[8704,512]{1,0:T(8,128)(2,1)}) %all-gather.8.cloned.1.call-update) | async-done | bytes 8912912 | tf_op jit(solution)/shard_map/all_gather | solution.py:543
  271.2 3.5 copy-done.8
  274.8 3.5 shard_map.149
  278.3 3.2 copy-done.2
  300.4 10.9 %collective-permute-done.52 = f32[4,6,2048]{2,1,0:T(8,128)S(1)} collective-permute-done((f32[4,6,2048]{2,1,0:T(8,128)S(1)}, f32[4,6,2048]{2,1,0:T(8,128)S(1)}, u32[]{:S(2)}, u32[]{:S(2)}) %collective-permute-start.52) | collective-permute-done | bytes 196640 | tf_op jit(solution)/shard_map/ppermute | solution.py:30
  322.2 6.0 fusion.25
  338.5 3.4 multiply_reduce_fusion.2
  354.9 4.2 fusion
  380.2 5.7 multiply_reduce_fusion.11
  397.7 4.4 convolution_convert_fusion.1
  402.9 6.8 multiply_reduce_fusion.1
  411.7 7.4 %dynamic_update_slice.22 = bf16[8704,512]{1,0:T(8,128)(2,1)} pad(bf16[2048,512]{1,0:T(8,128)(2,1)S(1)} %bitcast_convert_fusion, bf16[]{:T(256)} %constant.151.clone.1), padding=0_6656x0_0 | pad | bytes 11010050 | tf_op jit(solution)/shard_map/dynamic_update_slice | solution.py:527
  431.6 10.5 %shard_map.152 = bf16[16,272,512]{2,1,0:T(8,128)(2,1)} custom-call(s32[1]{0:T(128)} %bitcast.device, bf16[32,272,512]{2,1,0:T(8,128)(2,1)} %bitcast.83.source.refs_0_.refs_2_), custom_call_target="tpu_custom_call" | custom-call | bytes 8912896 | tf_op jit(solution)/shard_map/pallas_call | solution.py:105
  442.6 5.8 multiply_convert_fusion
  448.8 5.8 multiply_reduce_fusion.10
  455.7 4.5 shard_map.155
  475.9 3.0 pad_maximum_fusion
  478.9 6.1 shard_map.156
  485.1 8.2 %shard_map.153 = (bf16[8,272,512]{2,1,0:T(8,128)(2,1)S(1)}, bf16[8,272,512]{2,1,0:T(8,128)(2,1)}) custom-call(s32[1]{0:T(128)} %bitcast.device, bf16[32,272,512]{2,1,0:T(8,128)(2,1)} %bitcast.83.source.refs_0_.refs_2_, bf16[16,272,512]{2,1,0:T(8,128)(2,1)} %collective-permute-done.91.refs_1_.refs_3_, bf16[32,272,512]{2,1,0:T(8,128)(2,1)} %bitcast.83.source.refs_0_.refs_2_, ...), custom_call_target="tpu_custom_call" | custom-call | flops 2228224 | bytes 13369344 | tf_op jit(solution)/shard_map/pallas_call | solution.py:129
  493.7 3.4 fusion.131
  497.2 3.7 fusion.7
  505.7 4.8 convolution_convert_fusion
  510.5 2.9 dynamic_update_slice.26
  513.4 15.7 %collective-permute-done.95 = f32[2,512]{1,0:T(2,128)S(1)} collective-permute-done((f32[2,512]{1,0:T(2,128)S(1)}, f32[2,512]{1,0:T(2,128)S(1)}, u32[]{:S(2)}, u32[]{:S(2)}) %collective-permute-start.95) | collective-permute-done | bytes 4128 | tf_op jit(solution)/shard_map/ppermute | solution.py:30
  535.2 6.1 shard_map.159
  542.9 3.7 shard_map.157
  565.7 13.7 %collective-permute-done.103.refs_1_.refs_3_ = bf16[4,272,512]{2,1,0:T(8,128)(2,1)} collective-permute-done((bf16[4,272,512]{2,1,0:T(8,128)(2,1)}, bf16[4,272,512]{2,1,0:T(8,128)(2,1)}, u32[]{:S(2)}, u32[]{:S(2)}) %collective-permute-start.103) | collective-permute-done | bytes 1114144 | tf_op jit(solution)/shard_map/ppermute | solution.py:219
  586.9 3.9 shard_map.161
  595.5 13.7 %collective-permute-done.107.refs_1_.refs_3_ = bf16[2,272,512]{2,1,0:T(8,128)(2,1)} collective-permute-done((bf16[2,272,512]{2,1,0:T(8,128)(2,1)}, bf16[2,272,512]{2,1,0:T(8,128)(2,1)}, u32[]{:S(2)}, u32[]{:S(2)}) %collective-permute-start.107) | collective-permute-done | bytes 557088 | tf_op jit(solution)/shard_map/ppermute | solution.py:219
  615.3 4.7 collective-permute-done.104.refs_1_.refs_3_
  626.1 9.9 %collective-permute-done.109.refs_1_ = bf16[1,368,512]{2,1,0:T(8,128)(2,1)S(1)} collective-permute-done((bf16[1,368,512]{2,1,0:T(8,128)(2,1)S(1)}, bf16[1,368,512]{2,1,0:T(8,128)(2,1)S(1)}, u32[]{:S(2)}, u32[]{:S(2)}) %collective-permute-start.109) | collective-permute-done | bytes 376864 | tf_op jit(solution)/shard_map/ppermute | solution.py:219
  638.0 10.7 %collective-permute-done.112.refs_1_ = bf16[1,368,512]{2,1,0:T(8,128)(2,1)S(1)} collective-permute-done((bf16[1,368,512]{2,1,0:T(8,128)(2,1)S(1)}, bf16[1,368,512]{2,1,0:T(8,128)(2,1)S(1)}, u32[]{:S(2)}, u32[]{:S(2)}) %collective-permute-start.112) | collective-permute-done | bytes 376864 | tf_op jit(solution)/shard_map/ppermute | solution.py:219
  656.7 14.5 %collective-permute-done.114.refs_1_ = bf16[1,368,512]{2,1,0:T(8,128)(2,1)S(1)} collective-permute-done((bf16[1,368,512]{2,1,0:T(8,128)(2,1)S(1)}, bf16[1,368,512]{2,1,0:T(8,128)(2,1)S(1)}, u32[]{:S(2)}, u32[]{:S(2)}) %collective-permute-start.114) | collective-permute-done | bytes 376864 | tf_op jit(solution)/shard_map/ppermute | solution.py:219
  672.6 4.8 shard_map.164
  678.4 5.5 collective-permute-done.113
  683.9 7.8 %collective-permute-done.115 = bf16[1,368,512]{2,1,0:T(8,128)(2,1)S(1)} collective-permute-done((bf16[1,368,512]{2,1,0:T(8,128)(2,1)S(1)}, bf16[1,368,512]{2,1,0:T(8,128)(2,1)S(1)}, u32[]{:S(2)}, u32[]{:S(2)}) %collective-permute-start.115) | collective-permute-done | bytes 376864 | tf_op jit(solution)/shard_map/ppermute | solution.py:219
  (731 shorter events, 295.3 us)
Async XLA Ops:
  7.2 100.7 %all-gather.4.cloned.1.call-start = ((), (), s32[]{:S(2)}) async-start(), calls=%async_computation | async-start | bytes 12435456 | tf_op jit(solution)/shard_map/all_gather | solution.py:543
  9.2 180.3 %all-gather.6.cloned.1.call-start = ((), (), s32[]{:S(2)}) async-start(), calls=%async_computation.1 | async-start | bytes 9191424 | tf_op jit(solution)/shard_map/all_gather | solution.py:543
  11.1 260.1 %all-gather.8.cloned.1.call-start = ((), (), s32[]{:S(2)}) async-start(), calls=%async_computation.2 | async-start | bytes 9191424 | tf_op jit(solution)/shard_map/all_gather | solution.py:543
  29.5 18.5 %collective-permute-start.6 = (s32[16,6,1]{2,1,0:T(8,128)S(1)}, s32[16,6,1]{2,1,0:T(8,128)S(1)}, u32[]{:S(2)}, u32[]{:S(2)}) collective-permute-start(s32[16,6,1]{2,1,0:T(8,128)S(1)} %get-tuple-element.235), channel_id=1, source_target_pairs={{0,1},{1,0},{2,3},{3,2},{4,5},{5,4},{6,7},{7,6},{8,9},{9,8},{10,11... | collective-permute-start | bytes 1160 | tf_op jit(solution)/shard_map/ppermute | solution.py:30
  200.3 11.9 %collective-permute-start.34 = (f32[2,512]{1,0:T(2,128)S(1)}, f32[2,512]{1,0:T(2,128)S(1)}, u32[]{:S(2)}, u32[]{:S(2)}) collective-permute-start(f32[2,512]{1,0:T(2,128)S(1)} %add_add_fusion.21), channel_id=1, source_target_pairs={{0,24},{1,25},{2,26},{3,27},{4,28},{5,29},{6,30},{7,31},{8,16},{9,... | collective-permute-start | bytes 12296 | tf_op jit(solution)/shard_map/ppermute | solution.py:30
  202.3 9.9 %collective-permute-start.33 = (f32[2,512]{1,0:T(2,128)S(1)}, f32[2,512]{1,0:T(2,128)S(1)}, u32[]{:S(2)}, u32[]{:S(2)}) collective-permute-start(f32[2,512]{1,0:T(2,128)S(1)} %add_add_fusion.21), channel_id=1, source_target_pairs={{0,16},{1,17},{2,18},{3,19},{4,20},{5,21},{6,22},{7,23},{8,24},{9,... | collective-permute-start | bytes 12296 | tf_op jit(solution)/shard_map/ppermute | solution.py:30
  203.4 8.9 %collective-permute-start.32 = (f32[2,512]{1,0:T(2,128)S(1)}, f32[2,512]{1,0:T(2,128)S(1)}, u32[]{:S(2)}, u32[]{:S(2)}) collective-permute-start(f32[2,512]{1,0:T(2,128)S(1)} %add_add_fusion.21), channel_id=1, source_target_pairs={{0,8},{1,9},{2,10},{3,11},{4,12},{5,13},{6,14},{7,15},{8,0},{9,1},... | collective-permute-start | bytes 12296 | tf_op jit(solution)/shard_map/ppermute | solution.py:30
  241.2 41.5 %collective-permute-start.48 = (f32[2,2048]{1,0:T(2,128)S(1)}, f32[2,2048]{1,0:T(2,128)S(1)}, u32[]{:S(2)}, u32[]{:S(2)}) collective-permute-start(f32[2,2048]{1,0:T(2,128)S(1)} %add_add_fusion.9), channel_id=1, source_target_pairs={{0,24},{1,25},{2,26},{3,27},{4,28},{5,29},{6,30},{7,31},{8,16},{9,... | collective-permute-start | bytes 49160 | tf_op jit(solution)/shard_map/ppermute | solution.py:30
  243.0 39.7 %collective-permute-start.47 = (f32[2,2048]{1,0:T(2,128)S(1)}, f32[2,2048]{1,0:T(2,128)S(1)}, u32[]{:S(2)}, u32[]{:S(2)}) collective-permute-start(f32[2,2048]{1,0:T(2,128)S(1)} %add_add_fusion.9), channel_id=1, source_target_pairs={{0,16},{1,17},{2,18},{3,19},{4,20},{5,21},{6,22},{7,23},{8,24},{9,... | collective-permute-start | bytes 49160 | tf_op jit(solution)/shard_map/ppermute | solution.py:30
  244.1 39.2 %collective-permute-start.46 = (f32[2,2048]{1,0:T(2,128)S(1)}, f32[2,2048]{1,0:T(2,128)}, u32[]{:S(2)}, u32[]{:S(2)}) collective-permute-start(f32[2,2048]{1,0:T(2,128)S(1)} %add_add_fusion.9), channel_id=1, source_target_pairs={{0,8},{1,9},{2,10},{3,11},{4,12},{5,13},{6,14},{7,15},{8,0},{9,1},... | collective-permute-start | bytes 49160 | tf_op jit(solution)/shard_map/ppermute | solution.py:30
  296.8 14.6 %collective-permute-start.54 = (f32[4,6,2048]{2,1,0:T(8,128)S(1)}, f32[4,6,2048]{2,1,0:T(8,128)S(1)}, u32[]{:S(2)}, u32[]{:S(2)}) collective-permute-start(f32[4,6,2048]{2,1,0:T(8,128)S(1)} %pad_maximum_fusion.1), channel_id=1, source_target_pairs={{0,6},{1,7},{2,4},{3,5},{4,2},{5,3},{6,0},{7,1},{8,14},{9,15},{10,... | collective-permute-start | bytes 589832 | tf_op jit(solution)/shard_map/ppermute | solution.py:30
  298.4 13.0 %collective-permute-start.53 = (f32[4,6,2048]{2,1,0:T(8,128)S(1)}, f32[4,6,2048]{2,1,0:T(8,128)S(1)}, u32[]{:S(2)}, u32[]{:S(2)}) collective-permute-start(f32[4,6,2048]{2,1,0:T(8,128)S(1)} %pad_maximum_fusion.1), channel_id=1, source_target_pairs={{0,4},{1,5},{2,6},{3,7},{4,0},{5,1},{6,2},{7,3},{8,12},{9,13},{10,... | collective-permute-start | bytes 589832 | tf_op jit(solution)/shard_map/ppermute | solution.py:30
  299.6 11.7 %collective-permute-start.52 = (f32[4,6,2048]{2,1,0:T(8,128)S(1)}, f32[4,6,2048]{2,1,0:T(8,128)S(1)}, u32[]{:S(2)}, u32[]{:S(2)}) collective-permute-start(f32[4,6,2048]{2,1,0:T(8,128)S(1)} %pad_maximum_fusion.1), channel_id=1, source_target_pairs={{0,2},{1,3},{2,0},{3,1},{4,6},{5,7},{6,4},{7,5},{8,10},{9,11},{10,... | collective-permute-start | bytes 589832 | tf_op jit(solution)/shard_map/ppermute | solution.py:30
  350.5 9.2 %collective-permute-start.62 = (f32[2,2048]{1,0:T(2,128)S(1)}, f32[2,2048]{1,0:T(2,128)S(1)}, u32[]{:S(2)}, u32[]{:S(2)}) collective-permute-start(f32[2,2048]{1,0:T(2,128)S(1)} %add_add_fusion.7), channel_id=1, source_target_pairs={{0,24},{1,25},{2,26},{3,27},{4,28},{5,29},{6,30},{7,31},{8,16},{9,... | collective-permute-start | bytes 49160 | tf_op jit(solution)/shard_map/ppermute | solution.py:30
  393.3 8.8 %collective-permute-start.76 = (f32[2,512]{1,0:T(2,128)S(1)}, f32[2,512]{1,0:T(2,128)S(1)}, u32[]{:S(2)}, u32[]{:S(2)}) collective-permute-start(f32[2,512]{1,0:T(2,128)S(1)} %add_add_fusion.15), channel_id=1, source_target_pairs={{0,24},{1,25},{2,26},{3,27},{4,28},{5,29},{6,30},{7,31},{8,16},{9,... | collective-permute-start | bytes 12296 | tf_op jit(solution)/shard_map/ppermute | solution.py:30
  409.7 9.3 %collective-permute-start.77 = (f32[3,2048]{1,0:T(4,128)S(1)}, f32[3,2048]{1,0:T(4,128)S(1)}, u32[]{:S(2)}, u32[]{:S(2)}) collective-permute-start(f32[3,2048]{1,0:T(4,128)S(1)} %pad_maximum_fusion.3), channel_id=1, source_target_pairs={{0,1},{1,0},{2,3},{3,2},{4,5},{5,4},{6,7},{7,6},{8,9},{9,8},{10,11... | collective-permute-start | bytes 73736 | tf_op jit(solution)/shard_map/ppermute | solution.py:30
  425.7 16.4 %collective-permute-start.83 = (f32[3,2048]{1,0:T(4,128)S(1)}, f32[3,2048]{1,0:T(4,128)S(1)}, u32[]{:S(2)}, u32[]{:S(2)}) collective-permute-start(f32[3,2048]{1,0:T(4,128)S(1)} %add_add_fusion.3), channel_id=1, source_target_pairs={{0,24},{1,25},{2,26},{3,27},{4,28},{5,29},{6,30},{7,31},{8,16},{9,... | collective-permute-start | bytes 73736 | tf_op jit(solution)/shard_map/ppermute | solution.py:30
  427.6 14.4 %collective-permute-start.82 = (f32[3,2048]{1,0:T(4,128)S(1)}, f32[3,2048]{1,0:T(4,128)S(1)}, u32[]{:S(2)}, u32[]{:S(2)}) collective-permute-start(f32[3,2048]{1,0:T(4,128)S(1)} %add_add_fusion.3), channel_id=1, source_target_pairs={{0,16},{1,17},{2,18},{3,19},{4,20},{5,21},{6,22},{7,23},{8,24},{9,... | collective-permute-start | bytes 73736 | tf_op jit(solution)/shard_map/ppermute | solution.py:30
  427.7 14.4 %collective-permute-start.81 = (f32[3,2048]{1,0:T(4,128)S(1)}, f32[3,2048]{1,0:T(4,128)S(1)}, u32[]{:S(2)}, u32[]{:S(2)}) collective-permute-start(f32[3,2048]{1,0:T(4,128)S(1)} %add_add_fusion.3), channel_id=1, source_target_pairs={{0,8},{1,9},{2,10},{3,11},{4,12},{5,13},{6,14},{7,15},{8,0},{9,1},... | collective-permute-start | bytes 73736 | tf_op jit(solution)/shard_map/ppermute | solution.py:30
  442.1 43.0 %collective-permute-start.91 = (bf16[16,272,512]{2,1,0:T(8,128)(2,1)}, bf16[16,272,512]{2,1,0:T(8,128)(2,1)}, u32[]{:S(2)}, u32[]{:S(2)}) collective-permute-start(bf16[16,272,512]{2,1,0:T(8,128)(2,1)} %shard_map.152), channel_id=1, source_target_pairs={{0,1},{1,0},{2,3},{3,2},{4,5},{5,4},{6,7},{7,6},{8,9},{9,8},{10,11... | collective-permute-start | bytes 13369352 | tf_op jit(solution)/shard_map/ppermute | solution.py:219
  471.5 13.6 %collective-permute-start.90 = (f32[2,512]{1,0:T(2,128)S(1)}, f32[2,512]{1,0:T(2,128)S(1)}, u32[]{:S(2)}, u32[]{:S(2)}) collective-permute-start(f32[2,512]{1,0:T(2,128)S(1)} %add_add_fusion.13), channel_id=1, source_target_pairs={{0,24},{1,25},{2,26},{3,27},{4,28},{5,29},{6,30},{7,31},{8,16},{9,... | collective-permute-start | bytes 12296 | tf_op jit(solution)/shard_map/ppermute | solution.py:30
  473.5 11.6 %collective-permute-start.89 = (f32[2,512]{1,0:T(2,128)S(1)}, f32[2,512]{1,0:T(2,128)S(1)}, u32[]{:S(2)}, u32[]{:S(2)}) collective-permute-start(f32[2,512]{1,0:T(2,128)S(1)} %add_add_fusion.13), channel_id=1, source_target_pairs={{0,16},{1,17},{2,18},{3,19},{4,20},{5,21},{6,22},{7,23},{8,24},{9,... | collective-permute-start | bytes 12296 | tf_op jit(solution)/shard_map/ppermute | solution.py:30
  473.5 11.6 %collective-permute-start.88 = (f32[2,512]{1,0:T(2,128)S(1)}, f32[2,512]{1,0:T(2,128)S(1)}, u32[]{:S(2)}, u32[]{:S(2)}) collective-permute-start(f32[2,512]{1,0:T(2,128)S(1)} %add_add_fusion.13), channel_id=1, source_target_pairs={{0,8},{1,9},{2,10},{3,11},{4,12},{5,13},{6,14},{7,15},{8,0},{9,1},... | collective-permute-start | bytes 12296 | tf_op jit(solution)/shard_map/ppermute | solution.py:30
  500.9 40.4 %collective-permute-start.99 = (bf16[8,272,512]{2,1,0:T(8,128)(2,1)}, bf16[8,272,512]{2,1,0:T(8,128)(2,1)}, u32[]{:S(2)}, u32[]{:S(2)}) collective-permute-start(bf16[8,272,512]{2,1,0:T(8,128)(2,1)} %get-tuple-element.93), channel_id=1, source_target_pairs={{0,2},{1,5},{2,0},{3,7},{4,6},{5,1},{6,4},{7,3},{8,10},{9,13},{10,... | collective-permute-start | bytes 6684680 | tf_op jit(solution)/shard_map/ppermute | solution.py:219
  501.9 45.7 %collective-permute-start.100 = (bf16[8,368,512]{2,1,0:T(8,128)(2,1)}, bf16[8,368,512]{2,1,0:T(8,128)(2,1)S(1)}, u32[]{:S(2)}, u32[]{:S(2)}) collective-permute-start(bf16[8,368,512]{2,1,0:T(8,128)(2,1)} %shard_map.156), channel_id=1, source_target_pairs={{0,1},{1,0},{2,3},{3,2},{4,5},{5,4},{6,7},{7,6},{8,9},{9,8},{10,11... | collective-permute-start | bytes 9043976 | tf_op jit(solution)/shard_map/ppermute | solution.py:219
  502.1 11.3 %collective-permute-start.94 = (f32[2,512]{1,0:T(2,128)S(1)}, f32[2,512]{1,0:T(2,128)S(1)}, u32[]{:S(2)}, u32[]{:S(2)}) collective-permute-start(f32[2,512]{1,0:T(2,128)S(1)} %fusion.101), channel_id=1, source_target_pairs={{0,4},{1,5},{2,6},{3,7},{4,0},{5,1},{6,2},{7,3},{8,12},{9,13},{10,... | collective-permute-start | bytes 12296 | tf_op jit(solution)/shard_map/ppermute | solution.py:30
  503.3 25.7 %collective-permute-start.95 = (f32[2,512]{1,0:T(2,128)S(1)}, f32[2,512]{1,0:T(2,128)S(1)}, u32[]{:S(2)}, u32[]{:S(2)}) collective-permute-start(f32[2,512]{1,0:T(2,128)S(1)} %fusion.101), channel_id=1, source_target_pairs={{0,6},{1,7},{2,4},{3,5},{4,2},{5,3},{6,0},{7,1},{8,14},{9,15},{10,... | collective-permute-start | bytes 12296 | tf_op jit(solution)/shard_map/ppermute | solution.py:30
  504.9 24.1 %collective-permute-start.93 = (f32[2,512]{1,0:T(2,128)S(1)}, f32[2,512]{1,0:T(2,128)S(1)}, u32[]{:S(2)}, u32[]{:S(2)}) collective-permute-start(f32[2,512]{1,0:T(2,128)S(1)} %fusion.101), channel_id=1, source_target_pairs={{0,2},{1,3},{2,0},{3,1},{4,6},{5,7},{6,4},{7,5},{8,10},{9,11},{10,... | collective-permute-start | bytes 12296 | tf_op jit(solution)/shard_map/ppermute | solution.py:30
  529.1 12.2 %collective-permute-start.98 = (f32[2,512]{1,0:T(2,128)S(1)}, f32[2,512]{1,0:T(2,128)S(1)}, u32[]{:S(2)}, u32[]{:S(2)}) collective-permute-start(f32[2,512]{1,0:T(2,128)S(1)} %add_add_fusion.11), channel_id=1, source_target_pairs={{0,24},{1,25},{2,26},{3,27},{4,28},{5,29},{6,30},{7,31},{8,16},{9,... | collective-permute-start | bytes 12296 | tf_op jit(solution)/shard_map/ppermute | solution.py:30
  531.1 10.1 %collective-permute-start.97 = (f32[2,512]{1,0:T(2,128)S(1)}, f32[2,512]{1,0:T(2,128)S(1)}, u32[]{:S(2)}, u32[]{:S(2)}) collective-permute-start(f32[2,512]{1,0:T(2,128)S(1)} %add_add_fusion.11), channel_id=1, source_target_pairs={{0,16},{1,17},{2,18},{3,19},{4,20},{5,21},{6,22},{7,23},{8,24},{9,... | collective-permute-start | bytes 12296 | tf_op jit(solution)/shard_map/ppermute | solution.py:30
  531.1 10.1 %collective-permute-start.96 = (f32[2,512]{1,0:T(2,128)S(1)}, f32[2,512]{1,0:T(2,128)S(1)}, u32[]{:S(2)}, u32[]{:S(2)}) collective-permute-start(f32[2,512]{1,0:T(2,128)S(1)} %add_add_fusion.11), channel_id=1, source_target_pairs={{0,8},{1,9},{2,10},{3,11},{4,12},{5,13},{6,14},{7,15},{8,0},{9,1},... | collective-permute-start | bytes 12296 | tf_op jit(solution)/shard_map/ppermute | solution.py:30
  552.3 34.6 %collective-permute-start.101 = (bf16[8,368,512]{2,1,0:T(8,128)(2,1)}, bf16[8,368,512]{2,1,0:T(8,128)(2,1)S(1)}, u32[]{:S(2)}, u32[]{:S(2)}) collective-permute-start(bf16[8,368,512]{2,1,0:T(8,128)(2,1)} %shard_map.159), channel_id=1, source_target_pairs={{0,1},{1,0},{2,3},{3,2},{4,5},{5,4},{6,7},{7,6},{8,9},{9,8},{10,11... | collective-permute-start | bytes 9043976 | tf_op jit(solution)/shard_map/ppermute | solution.py:219
  552.3 27.1 %collective-permute-start.103 = (bf16[4,272,512]{2,1,0:T(8,128)(2,1)}, bf16[4,272,512]{2,1,0:T(8,128)(2,1)}, u32[]{:S(2)}, u32[]{:S(2)}) collective-permute-start(bf16[4,272,512]{2,1,0:T(8,128)(2,1)} %get-tuple-element.104), channel_id=1, source_target_pairs={{0,4},{1,3},{2,6},{3,1},{4,0},{5,7},{6,2},{7,5},{8,12},{9,11},{10,... | collective-permute-start | bytes 3342344 | tf_op jit(solution)/shard_map/ppermute | solution.py:219
  553.4 30.3 %collective-permute-start.102 = (bf16[4,368,512]{2,1,0:T(8,128)(2,1)}, bf16[4,368,512]{2,1,0:T(8,128)(2,1)}, u32[]{:S(2)}, u32[]{:S(2)}) collective-permute-start(bf16[4,368,512]{2,1,0:T(8,128)(2,1)} %get-tuple-element.101), channel_id=1, source_target_pairs={{0,2},{1,5},{2,0},{3,7},{4,6},{5,1},{6,4},{7,3},{8,10},{9,13},{10,... | collective-permute-start | bytes 4521992 | tf_op jit(solution)/shard_map/ppermute | solution.py:219
  591.9 28.0 %collective-permute-start.104 = (bf16[4,368,512]{2,1,0:T(8,128)(2,1)}, bf16[4,368,512]{2,1,0:T(8,128)(2,1)S(1)}, u32[]{:S(2)}, u32[]{:S(2)}) collective-permute-start(bf16[4,368,512]{2,1,0:T(8,128)(2,1)} %get-tuple-element.108), channel_id=1, source_target_pairs={{0,2},{1,5},{2,0},{3,7},{4,6},{5,1},{6,4},{7,3},{8,10},{9,13},{10,... | collective-permute-start | bytes 4521992 | tf_op jit(solution)/shard_map/ppermute | solution.py:219
  593.9 17.6 %collective-permute-start.105 = (bf16[2,368,512]{2,1,0:T(8,128)(2,1)}, bf16[2,368,512]{2,1,0:T(8,128)(2,1)}, u32[]{:S(2)}, u32[]{:S(2)}) collective-permute-start(bf16[2,368,512]{2,1,0:T(8,128)(2,1)} %shard_map.160), channel_id=1, source_target_pairs={{0,1},{1,0},{2,3},{3,2},{4,5},{5,4},{6,7},{7,6},{8,9},{9,8},{10,11... | collective-permute-start | bytes 2261000 | tf_op jit(solution)/shard_map/ppermute | solution.py:219
  593.9 20.1 %collective-permute-start.106 = (bf16[2,368,512]{2,1,0:T(8,128)(2,1)}, bf16[2,368,512]{2,1,0:T(8,128)(2,1)}, u32[]{:S(2)}, u32[]{:S(2)}) collective-permute-start(bf16[2,368,512]{2,1,0:T(8,128)(2,1)} %get-tuple-element.114), channel_id=1, source_target_pairs={{0,4},{1,3},{2,6},{3,1},{4,0},{5,7},{6,2},{7,5},{8,12},{9,11},{10,... | collective-permute-start | bytes 2261000 | tf_op jit(solution)/shard_map/ppermute | solution.py:219
  594.2 15.0 %collective-permute-start.107 = (bf16[2,272,512]{2,1,0:T(8,128)(2,1)}, bf16[2,272,512]{2,1,0:T(8,128)(2,1)}, u32[]{:S(2)}, u32[]{:S(2)}) collective-permute-start(bf16[2,272,512]{2,1,0:T(8,128)(2,1)} %get-tuple-element.117), channel_id=1, source_target_pairs={{0,8},{1,9},{2,10},{3,11},{4,12},{5,13},{6,14},{7,15},{8,0},{9,1},... | collective-permute-start | bytes 1671176 | tf_op jit(solution)/shard_map/ppermute | solution.py:219
  620.3 15.9 %collective-permute-start.108 = (bf16[2,368,512]{2,1,0:T(8,128)(2,1)S(1)}, bf16[2,368,512]{2,1,0:T(8,128)(2,1)S(1)}, u32[]{:S(2)}, u32[]{:S(2)}) collective-permute-start(bf16[2,368,512]{2,1,0:T(8,128)(2,1)S(1)} %get-tuple-element.119), channel_id=1, source_target_pairs={{0,4},{1,3},{2,6},{3,1},{4,0},{5,7},{6,2},{7,5},{8,12},{9,11},{10,... | collective-permute-start | bytes 2261000 | tf_op jit(solution)/shard_map/ppermute | solution.py:219
  624.2 11.8 %collective-permute-start.109 = (bf16[1,368,512]{2,1,0:T(8,128)(2,1)S(1)}, bf16[1,368,512]{2,1,0:T(8,128)(2,1)S(1)}, u32[]{:S(2)}, u32[]{:S(2)}) collective-permute-start(bf16[1,368,512]{2,1,0:T(8,128)(2,1)S(1)} %get-tuple-element.122), channel_id=1, source_target_pairs={{0,2},{1,3},{2,0},{3,1},{4,6},{5,7},{6,4},{7,5},{8,10},{9,11},{10,... | collective-permute-start | bytes 1130504 | tf_op jit(solution)/shard_map/ppermute | solution.py:219
  626.1 10.0 %collective-permute-start.110 = (bf16[1,368,512]{2,1,0:T(8,128)(2,1)S(1)}, bf16[1,368,512]{2,1,0:T(8,128)(2,1)S(1)}, u32[]{:S(2)}, u32[]{:S(2)}) collective-permute-start(bf16[1,368,512]{2,1,0:T(8,128)(2,1)S(1)} %get-tuple-element.125), channel_id=1, source_target_pairs={{0,8},{1,9},{2,10},{3,11},{4,12},{5,13},{6,14},{7,15},{8,0},{9,1},... | collective-permute-start | bytes 1130504 | tf_op jit(solution)/shard_map/ppermute | solution.py:219
  636.4 12.4 %collective-permute-start.111 = (bf16[1,368,512]{2,1,0:T(8,128)(2,1)S(1)}, bf16[1,368,512]{2,1,0:T(8,128)(2,1)S(1)}, u32[]{:S(2)}, u32[]{:S(2)}) collective-permute-start(bf16[1,368,512]{2,1,0:T(8,128)(2,1)S(1)} %get-tuple-element.126), channel_id=1, source_target_pairs={{0,8},{1,9},{2,10},{3,11},{4,12},{5,13},{6,14},{7,15},{8,0},{9,1},... | collective-permute-start | bytes 1130504 | tf_op jit(solution)/shard_map/ppermute | solution.py:219
  636.5 12.2 %collective-permute-start.112 = (bf16[1,368,512]{2,1,0:T(8,128)(2,1)S(1)}, bf16[1,368,512]{2,1,0:T(8,128)(2,1)S(1)}, u32[]{:S(2)}, u32[]{:S(2)}) collective-permute-start(bf16[1,368,512]{2,1,0:T(8,128)(2,1)S(1)} %shard_map.170.refs_0_), channel_id=1, source_target_pairs={{4,0},{5,1},{6,2},{7,3},{12,8},{13,9},{14,10},{15,11},{20,16},{21,... | collective-permute-start | bytes 1130504 | tf_op jit(solution)/shard_map/ppermute | solution.py:219
  648.9 22.3 %collective-permute-start.114 = (bf16[1,368,512]{2,1,0:T(8,128)(2,1)S(1)}, bf16[1,368,512]{2,1,0:T(8,128)(2,1)S(1)}, u32[]{:S(2)}, u32[]{:S(2)}) collective-permute-start(bf16[1,368,512]{2,1,0:T(8,128)(2,1)S(1)} %shard_map.173.refs_0_), channel_id=1, source_target_pairs={{8,0},{9,1},{10,2},{11,3},{24,16},{25,17},{26,18},{27,19}} | collective-permute-start | bytes 1130504 | tf_op jit(solution)/shard_map/ppermute | solution.py:219
  650.2 27.2 %collective-permute-start.117 = (bf16[1,272,512]{2,1,0:T(8,128)(2,1)S(1)}, bf16[1,272,512]{2,1,0:T(8,128)(2,1)S(1)}, u32[]{:S(2)}, u32[]{:S(2)}) collective-permute-start(bf16[1,272,512]{2,1,0:T(8,128)(2,1)S(1)} %get-tuple-element.132), channel_id=1, source_target_pairs={{0,16},{1,17},{2,18},{3,19},{4,20},{5,21},{6,22},{7,23},{8,24},{9,... | collective-permute-start | bytes 835592 | tf_op jit(solution)/shard_map/ppermute | solution.py:219
  653.3 25.2 %collective-permute-start.116 = (bf16[1,368,512]{2,1,0:T(8,128)(2,1)S(1)}, bf16[1,368,512]{2,1,0:T(8,128)(2,1)S(1)}, u32[]{:S(2)}, u32[]{:S(2)}) collective-permute-start(bf16[1,368,512]{2,1,0:T(8,128)(2,1)S(1)} %shard_map.171), channel_id=1, source_target_pairs={{0,16},{1,17},{2,18},{3,19},{4,20},{5,21},{6,22},{7,23},{8,24},{9,... | collective-permute-start | bytes 1130504 | tf_op jit(solution)/shard_map/ppermute | solution.py:219
  655.4 28.5 %collective-permute-start.113 = (bf16[1,368,512]{2,1,0:T(8,128)(2,1)S(1)}, bf16[1,368,512]{2,1,0:T(8,128)(2,1)S(1)}, u32[]{:S(2)}, u32[]{:S(2)}) collective-permute-start(bf16[1,368,512]{2,1,0:T(8,128)(2,1)S(1)} %shard_map.172), channel_id=1, source_target_pairs={{16,0},{17,1},{18,2},{19,3},{20,4},{21,5},{22,6},{23,7},{24,8},{25... | collective-permute-start | bytes 1130504 | tf_op jit(solution)/shard_map/ppermute | solution.py:219
  671.3 20.5 %collective-permute-start.115 = (bf16[1,368,512]{2,1,0:T(8,128)(2,1)S(1)}, bf16[1,368,512]{2,1,0:T(8,128)(2,1)S(1)}, u32[]{:S(2)}, u32[]{:S(2)}) collective-permute-start(bf16[1,368,512]{2,1,0:T(8,128)(2,1)S(1)} %shard_map.174), channel_id=1, source_target_pairs={{16,0},{17,1},{18,2},{19,3}} | collective-permute-start | bytes 1130504 | tf_op jit(solution)/shard_map/ppermute | solution.py:219
  (229 other events, 2199.5 us)
Sparse Core Ops, SparseCore 0:
  11.4 96.3 all-gather.3
  111.2 78.2 all-gather.5
  192.4 78.8 all-gather.7

commit v2 on v1

--- a/solution.py
+++ b/solution.py
@@ -46,50 +46,289 @@
     return bit_groups_of(device_count())
 
 
-def all_sum(values):
-    for masks in bit_groups():
+def all_sum(values, groups=(), held=None):
+    stages = bit_groups()
+    for stage, masks in enumerate(stages):
+        if stage == len(stages) - 1 and held is not None:
+            values, held = step(groups, (values, held))
         others = [swap(values, mask) for mask in masks]
         values = values + others[0]
         if len(others) == 3:
             values = values + (others[1] + others[2])
-    return values
-
-
-def reorder_kernel(device, source, target):
-    groups = bit_groups_of(source.shape[0])
-    for i in range(source.shape[0]):
-        offset = jnp.bitwise_xor(device[0], i)
-        place = jnp.int32(0)
-        width = 0
-        for masks in reversed(groups):
-            bits = len(masks).bit_length()
-            low = masks[0].bit_length() - 1
-            place += ((offset >> low) & (2**bits - 1)) << width
-            width += bits
-        target[i] = source[place]
-
-
-def all_blocks(values):
+    return values if held is None else (values, held)
+
+
+def gather_blocks(values):
     gathered = values[None]
     for masks in reversed(bit_groups()):
         gathered = jnp.concatenate([gathered] + [swap(gathered, mask) for mask in masks], axis=0)
+    return gathered
+
+
+def place_of(device, i, count):
+    offset = jnp.bitwise_xor(device, i)
+    place = jnp.int32(0)
+    width = 0
+    for masks in reversed(bit_groups_of(count)):
+        bits = len(masks).bit_length()
+        low = masks[0].bit_length() - 1
+        place += ((offset >> low) & (2**bits - 1)) << width
+        width += bits
+    return place
+
+
+def head_kernel(
+    device,
+    gathered,
+    order,
+    affine,
+    flat,
+    pooled_out,
+    hidden_out,
+    raw_cot_out,
+    embed_cot,
+    grads,
+    losses,
+    pooled_cot,
+    rows_in,
+    weights,
+    embed_rows,
+    w_embed,
+    pooled,
+    hidden,
+    raw_cot,
+    partners,
+    terms,
+    normed,
+    slope,
+    inv_std,
+    embed,
+    units,
+    own_terms,
+    own_wide,
+    sems,
+    out_sems,
+):
+    count, views_dev = gathered.shape[:2]
+    total = count * views_dev
+    tile = 256
+    tiles = HEAD // tile
+
+    def fetch(n):
+        return pltpu.make_async_copy(
+            flat.at[pl.ds(n * 4 * tile, 4 * tile), :], rows_in.at[n], sems.at[n]
+        )
+
+    def fetch_embed():
+        return pltpu.make_async_copy(
+            flat.at[pl.ds(4 * C_OUT, C_MID), :], embed_rows, sems.at[tiles]
+        )
+
+    def flush(source, target, n):
+        return pltpu.make_async_copy(source, target, out_sems.at[n])
+
+    for n in range(tiles):
+        fetch(n).start()
+    fetch_embed().start()
+
+    for i in range(count):
+        block = gathered[place_of(device[0], i, count)]
+        pooled[i * views_dev : (i + 1) * views_dev, :] = block[:, :C_OUT]
+        partners[i * views_dev : (i + 1) * views_dev, :] = block[:, C_OUT:]
+    flush(pooled, pooled_out, 0).start()
+
+    def halves(values):
+        high = values.astype(BF16)
+        return high, (values - high.astype(F32)).astype(BF16)
+
+    def cut(n, carry):
+        cols = pl.ds(pl.multiple_of(n * tile, tile), tile)
+        terms[:total, cols], terms[total:, cols] = halves(pooled[:, cols])
+        return carry
+
+    lax.fori_loop(0, tiles, cut, 0)
+
+    def unflatten_rows(n, carry):
+        fetch(n).wait()
+        for at in range(0, tile, 64):
+            sorted_rows = jnp.dot(
+                order[...], rows_in[n, 4 * at : 4 * at + 256, :], preferred_element_type=F32
+            )
+            for part in range(4):
+                weights[
+                    pl.ds(pl.multiple_of(n * tile + at, 64), 64), part * C_MID : (part + 1) * C_MID
+                ] = sorted_rows[64 * part : 64 * part + 64, :].astype(BF16)
+        return carry
+
+    lax.fori_loop(0, tiles, unflatten_rows, 0)
+    fetch_embed().wait()
+    for part in range(4):
+        embed_rows_wide = embed_rows[:, part * EMBED : (part + 1) * EMBED].astype(F32)
+        own_wide[pl.ds(part, C_MID, stride=4), :] = embed_rows_wide
+    w_embed[...] = own_wide[...].astype(BF16)
+    embed[...] = jnp.zeros_like(embed)
+
+    def forward(n, carry):
+        cols = pl.ds(pl.multiple_of(n * tile, tile), tile)
+        product = jnp.dot(terms[...], weights[:, cols], preferred_element_type=F32)
+        raw = product[:total] + product[total:]
+        center = jnp.sum(raw, axis=0, keepdims=True) / total
+        spread = jnp.sum(raw * raw, axis=0, keepdims=True) / total - center * center
+        scale = lax.rsqrt(spread + EPSILON)
+        unit = (raw - center) * scale
+        shifted = unit * affine[0:1, cols] + affine[1:2, cols]
+        logistic = jax.nn.sigmoid(shifted)
+        value = shifted * logistic
+        inv_std[:, cols] = scale
+        normed[:, cols] = unit
+        slope[:, cols] = logistic * (1.0 + shifted * (1.0 - logistic))
+        hidden[:, cols] = value
+        high, low = halves(value)
+        embed[...] += jnp.dot(high, w_embed[cols, :], preferred_element_type=F32) + jnp.dot(
+            low, w_embed[cols, :], preferred_element_type=F32
+        )
+        return carry
+
+    lax.fori_loop(0, tiles, forward, 0)
+    flush(hidden, hidden_out, 1).start()
+
+    values = embed[...]
+    length = lax.rsqrt(jnp.sum(values * values, axis=1, keepdims=True) + NORM_EPS)
+    units[...] = jnp.zeros_like(units)
+    units[:total, :] = (values * length).astype(BF16)
+    every = units[...]
+    size = every.shape[0]
+    across = lax.broadcasted_iota(jnp.int32, (size, size), 0)
+    along = lax.broadcasted_iota(jnp.int32, (size, size), 1)
+    valid = (across != along) & (across < total) & (along < total)
+    scores = (
+        lax.dot_general(every, every, (((1,), (1,)), ((), ())), preferred_element_type=F32) / TAU
+    )
+    scores = jnp.where(valid, scores, -1e30)
+    highest = jnp.max(scores, axis=1, keepdims=True)
+    log_total = highest + jnp.log(jnp.sum(jnp.exp(scores - highest), axis=1, keepdims=True))
+    chances = jnp.where(valid, jnp.exp(scores - log_total), 0.0)
+    match = (along == partners[:, 0:1].astype(jnp.int32)) & valid
+    loss = log_total - jnp.sum(jnp.where(match, scores, 0.0), axis=1, keepdims=True)
+    losses[...] = jnp.broadcast_to(loss, losses.shape)
+    near = chances - 2.0 * match.astype(F32)
+    unit_cot = jnp.zeros((size, EMBED), F32)
+    for part in halves(near):
+        unit_cot += jnp.dot(part, every, preferred_element_type=F32)
+    for part in halves(chances):
+        unit_cot += lax.dot_general(
+            part, every, (((0,), (0,)), ((), ())), preferred_element_type=F32
+        )
+    unit_cot = unit_cot[:total] * (1.0 / (total * TAU))
+    along_cot = jnp.sum(values * unit_cot, axis=1, keepdims=True)
+    cot = length * unit_cot - values * (length * length * length * along_cot)
+    embed_cot[...] = cot
+    cot_high, cot_low = halves(cot)
+    rows = own_terms.shape[0] // 2
+    chosen = lax.broadcasted_iota(jnp.int32, (rows, total), 1) == (
+        device[0] * views_dev + lax.broadcasted_iota(jnp.int32, (rows, total), 0)
+    )
+    chosen = jnp.where(chosen, 1.0, 0.0).astype(BF16)
+
+    def backward(n, carry):
+        cols = pl.ds(pl.multiple_of(n * tile, tile), tile)
+        pull = (((1,), (1,)), ((), ()))
+        grad = lax.dot_general(
+            cot_high, w_embed[cols, :], pull, preferred_element_type=F32
+        ) + lax.dot_general(cot_low, w_embed[cols, :], pull, preferred_element_type=F32)
+        grad = grad * slope[:, cols]
+        unit = normed[:, cols]
+        gain = jnp.sum(grad * unit, axis=0, keepdims=True)
+        shift = jnp.sum(grad, axis=0, keepdims=True)
+        grads[0:1, cols] = gain
+        grads[1:2, cols] = shift
+        raw = affine[0:1, cols] * inv_std[:, cols] * (grad - shift / total - unit * (gain / total))
+        raw_cot[:, cols] = raw
+        own = [
+            jnp.dot(chosen, part, preferred_element_type=F32).astype(BF16) for part in halves(raw)
+        ]
+        own_terms[:, cols] = jnp.concatenate(own, axis=0)
+        return carry
+
+    lax.fori_loop(0, tiles, backward, 0)
+    flush(raw_cot, raw_cot_out, 2).start()
+
+    def pull_pooled(n, carry):
+        at = pl.ds(pl.multiple_of(n * tile, tile), tile)
+        product = lax.dot_general(
+            own_terms[...],
+            weights[at, :],
+            (((1,), (1,)), ((), ())),
+            preferred_element_type=F32,
+        )
+        pooled_cot[:, at] = product[:rows] + product[rows:]
+        return carry
+
+    lax.fori_loop(0, tiles, pull_pooled, 0)
+    flush(pooled, pooled_out, 0).wait()
+    flush(hidden, hidden_out, 1).wait()
+    flush(raw_cot, raw_cot_out, 2).wait()
+
+
+def head_pass(gathered, flat, affine):
+    count, views_dev, width = gathered.shape
+    total = count * views_dev
+    size = -(-total // 256) * 256
+    rows = 16
+    tiles = HEAD // 256
+    whole = pl.BlockSpec(memory_space=pltpu.VMEM)
+    apart = pl.BlockSpec(memory_space=pl.ANY)
+    shape = jax.ShapeDtypeStruct
     return pl.pallas_call(
-        reorder_kernel,
-        out_shape=jax.ShapeDtypeStruct(gathered.shape, gathered.dtype),
-        in_specs=[
-            pl.BlockSpec(memory_space=pltpu.SMEM),
-            pl.BlockSpec(memory_space=pltpu.VMEM),
+        head_kernel,
+        out_shape=[
+            shape((total, C_OUT), F32),
+            shape((total, HEAD), F32),
+            shape((total, HEAD), F32),
+            shape((total, EMBED), F32),
+            shape((2, HEAD), F32),
+            shape((size, EMBED), F32),
+            shape((rows, C_OUT), F32),
         ],
-        out_specs=pl.BlockSpec(memory_space=pltpu.VMEM),
-        compiler_params=pltpu.CompilerParams(vmem_limit_bytes=48 << 20),
+        in_specs=[pl.BlockSpec(memory_space=pltpu.SMEM), whole, whole, whole, apart],
+        out_specs=[apart] * 3 + [whole] * 4,
+        scratch_shapes=[
+            pltpu.VMEM((tiles, 1024, C_MID), BF16),
+            pltpu.VMEM((C_OUT, HEAD), BF16),
+            pltpu.VMEM((C_MID, C_MID), BF16),
+            pltpu.VMEM((HEAD, EMBED), BF16),
+            pltpu.VMEM((total, C_OUT), F32),
+            pltpu.VMEM((total, HEAD), F32),
+            pltpu.VMEM((total, HEAD), F32),
+            pltpu.VMEM((size, width - C_OUT), F32),
+            pltpu.VMEM((2 * total, C_OUT), BF16),
+            pltpu.VMEM((total, HEAD), F32),
+            pltpu.VMEM((total, HEAD), F32),
+            pltpu.VMEM((1, HEAD), F32),
+            pltpu.VMEM((total, EMBED), F32),
+            pltpu.VMEM((size, EMBED), BF16),
+            pltpu.VMEM((2 * rows, HEAD), BF16),
+            pltpu.VMEM((HEAD, EMBED), F32),
+            pltpu.SemaphoreType.DMA((tiles + 1,)),
+            pltpu.SemaphoreType.DMA((3,)),
+        ],
+        compiler_params=pltpu.CompilerParams(vmem_limit_bytes=52 << 20),
         cost_estimate=pl.CostEstimate(
-            flops=0, bytes_accessed=8 * np.prod(gathered.shape).item(), transcendentals=0
+            flops=4 * total * C_OUT * HEAD, bytes_accessed=20 << 20, transcendentals=3 * total * HEAD
         ),
-    )(lax.axis_index(BOTH).reshape(1), gathered)
-
-
-def copy_kernel(device, source, target):
-    target[...] = source[...]
+    )(
+        lax.axis_index(BOTH).reshape(1),
+        gathered,
+        jnp.asarray(row_order(), BF16),
+        affine,
+        flat,
+    )
+
+
+def copy_kernel(device, *refs):
+    sources, target = refs[:-1], refs[-1]
+    for way, source in enumerate(sources):
+        target[way] = source[0]
 
 
 def add_kernel(device, *refs):
@@ -102,19 +341,25 @@
 def copy_blocks(source, count, place):
     block = (1, *source.shape[1:])
     shape = (count, *source.shape[1:])
+    ways = min(count, 4)
+
+    def read(way):
+        return pl.BlockSpec(block, lambda i, device: (place(ways * i + way, device[0]), 0, 0))
+
     return pl.pallas_call(
         copy_kernel,
         out_shape=jax.ShapeDtypeStruct(shape, source.dtype),
         grid_spec=pltpu.PrefetchScalarGridSpec(
             num_scalar_prefetch=1,
-            grid=(count,),
-            in_specs=[pl.BlockSpec(block, lambda i, device: (place(i, device[0]), 0, 0))],
-            out_specs=pl.BlockSpec(block, lambda i, device: (i, 0, 0)),
+            grid=(count // ways,),
+            in_specs=[read(way) for way in range(ways)],
+            out_specs=pl.BlockSpec((ways, *source.shape[1:]), lambda i, device: (i, 0, 0)),
         ),
+        compiler_params=pltpu.CompilerParams(vmem_limit_bytes=24 << 20),
         cost_estimate=pl.CostEstimate(
             flops=0, bytes_accessed=4 * np.prod(shape).item(), transcendentals=0
         ),
-    )(lax.axis_index(BOTH).reshape(1), source)
+    )(lax.axis_index(BOTH).reshape(1), *[source] * ways)
 
 
 def add_blocks(source, incoming, count, places):
@@ -143,10 +388,10 @@
 
 
 class ScatterSum:
-    def __init__(self, data, base):
+    def __init__(self, data, base, size):
         self.count = device_count()
         self.base = base
-        self.size = data.shape[0]
+        self.size = size
         self.width = self.size
         self.source = data
         self.incoming = None
@@ -154,24 +399,27 @@
         self.live = [True] * self.count
         self.stage = 0
         self.stages = self.count.bit_length() - 1
-        self.crossed = self.size > 4
+        order = list(range(self.stages))
+        if self.size > 8:
+            other = [0, 2, 1] + order[3:]
+        elif self.size == 8:
+            other = [0, 2, 1] + order[4:] + [3]
+        else:
+            other = [0, 1] + order[3:] + [2]
+        self.orders = [order, other]
 
     def bit(self, device):
-        if self.crossed and self.stage in (1, 2) and device & 1:
-            return 3 - self.stage
-        return self.stage
+        return self.orders[device & 1][self.stage]
 
     def halves(self, other):
-        stage, crossed = self.stage, self.crossed
+        bits = [order[self.stage] for order in self.orders]
+        ranks = [sorted(order[self.stage :]).index(order[self.stage]) for order in self.orders]
 
         def place(i, device):
             core = device & 1
-            if crossed and stage in (1, 2):
-                bit = stage + core * (3 - 2 * stage)
-            else:
-                bit = stage
+            bit = bits[0] + core * (bits[1] - bits[0])
+            at = ranks[0] + core * (ranks[1] - ranks[0])
             value = ((device >> bit) & 1) ^ int(other)
-            at = core if crossed and stage == 1 else 0
             return ((i >> at) << (at + 1)) | (value << at) | (i & ((1 << at) - 1))
 
         return place
@@ -179,16 +427,18 @@
     def within(self, place):
         if not self.folded:
             return place
-        return lambda i, device: 2 * place(i, device) + (device & 1)
+        return lambda i, device: self.base + 2 * place(i, device) + (device & 1)
 
     def prepare(self):
-        self.split = self.size > 1 << self.stage
+        self.split = self.width > 1
         if self.split:
             self.width //= 2
             keep, send = self.halves(False), self.halves(True)
             if self.incoming is None:
                 self.folded = True
-                return copy_blocks(self.source, self.width, send)
+                return copy_blocks(
+                    self.source, self.width, lambda i, device: self.base + send(i, device)
+                )
             self.source, outgoing = add_blocks(
                 self.source,
                 self.incoming,
@@ -198,13 +448,7 @@
             self.folded = False
             return outgoing
 
-        def same(i, device):
-            return i
-
-        (self.source,) = add_blocks(
-            self.source, self.incoming, self.width, [(self.within(same), same)]
-        )
-        self.folded = False
+        self.source = (self.source.astype(F32) + self.incoming.astype(F32)).astype(BF16)
         return self.source
 
     def send(self, outgoing):
@@ -235,6 +479,13 @@
     return held
 
 
+def row_order():
+    order = np.zeros((256, 256), np.float32)
+    for row in range(256):
+        order[row, 4 * (row % 64) + row // 64] = 1.0
+    return order
+
+
 def unflatten_kernel(order, source, target):
     for at in range(0, target.shape[0], 64):
         sorted_rows = jnp.dot(
@@ -250,9 +501,6 @@
     tile = 256
     while first % (4 * tile):
         tile //= 2
-    order = np.zeros((256, 256), np.float32)
-    for row in range(256):
-        order[row, 4 * (row % 64) + row // 64] = 1.0
     return pl.pallas_call(
         unflatten_kernel,
         out_shape=jax.ShapeDtypeStruct((rows, 4 * C_MID), BF16),
@@ -266,10 +514,11 @@
         cost_estimate=pl.CostEstimate(
             flops=2048 * rows * C_MID, bytes_accessed=16 * rows * C_MID, transcendentals=0
         ),
-    )(jnp.asarray(order, BF16), flat)
-
-
-def flat_grad_kernel(inputs, cotan, target, scratch):
+    )(jnp.asarray(row_order(), BF16), flat)
+
+
+def flat_grad_kernel(inputs, cotan, *refs):
+    target, scratch = refs[-2:]
     rows = inputs.shape[1]
     grad = lax.dot_general(
         inputs[...], cotan[...], (((0,), (0,)), ((), ())), preferred_element_type=F32
@@ -281,28 +530,43 @@
         target[:, lane * 128 : (lane + 1) * 128] = scratch[lane].astype(BF16)
 
 
-def flat_grad(inputs, cotan):
-    inputs = inputs.reshape(-1, inputs.shape[-1])
-    cotan = cotan.reshape(-1, cotan.shape[-1])
+def row_grad_kernel(inputs, cotan, *refs):
+    refs[-1][...] = lax.dot_general(
+        inputs[...], cotan[...], (((0,), (0,)), ((), ())), preferred_element_type=F32
+    ).astype(BF16)
+
+
+def grad_into(total, first, inputs, cotan, into=None):
     count, depth = inputs.shape
-    tile = 128
+    width = cotan.shape[1]
+    parts = width // C_MID
+    if parts == 4:
+        kernel, tile = flat_grad_kernel, 128
+        scratch = [pltpu.VMEM((4, 4 * tile, 128), F32)]
+    else:
+        kernel, tile = row_grad_kernel, 256
+        scratch = []
+    at = first // (parts * tile)
+    given = [] if into is None else [into]
     return pl.pallas_call(
-        flat_grad_kernel,
-        out_shape=jax.ShapeDtypeStruct((4 * depth, C_MID), BF16),
+        kernel,
+        out_shape=jax.ShapeDtypeStruct((total, C_MID), BF16),
         grid=(depth // tile,),
         in_specs=[
             pl.BlockSpec((count, tile), lambda i: (0, i)),
-            pl.BlockSpec((count, 4 * C_MID), lambda i: (0, 0)),
-        ],
-        out_specs=pl.BlockSpec((4 * tile, C_MID), lambda i: (i, 0)),
-        scratch_shapes=[pltpu.VMEM((4, 4 * tile, 128), F32)],
+            pl.BlockSpec((count, width), lambda i: (0, 0)),
+        ]
+        + [pl.BlockSpec(memory_space=pl.ANY) for _ in given],
+        out_specs=pl.BlockSpec((parts * tile, C_MID), lambda i: (at + i, 0)),
+        scratch_shapes=scratch,
+        input_output_aliases={2: 0} if given else {},
         compiler_params=pltpu.CompilerParams(vmem_limit_bytes=24 << 20),
         cost_estimate=pl.CostEstimate(
-            flops=2 * count * depth * 4 * C_MID,
-            bytes_accessed=2 * count * (depth + 4 * C_MID) + 8 * depth * C_MID,
+            flops=2 * count * depth * width,
+            bytes_accessed=2 * count * (depth + width) + 2 * depth * width,
             transcendentals=0,
         ),
-    )(inputs, cotan)
+    )(inputs, cotan, *given)
 
 
 def split_norms(norm_params):
@@ -433,6 +697,36 @@
         jnp.zeros((), values.dtype),
         ((0, 0, 0), (0, 0, 0), (0, size - values.shape[2], 0), (0, 0, 0)),
     )
+
+
+def even_cells_kernel(source, target, scratch):
+    side = source.shape[1]
+    scratch[...] = jnp.zeros_like(scratch)
+    for lane in range(C_IN // 128):
+        for row in range(0, side, 2):
+            scratch[lane, 8 * row : 8 * row + side, :] = source[
+                0, row, :, lane * 128 : (lane + 1) * 128
+            ].astype(F32)
+            target[0, row // 2, :, lane * 128 : (lane + 1) * 128] = scratch[
+                lane, pl.ds(8 * row, 8, stride=2), :
+            ].astype(BF16)
+
+
+def even_cells(views):
+    count, side = views.shape[:2]
+    padded = pl.pallas_call(
+        even_cells_kernel,
+        out_shape=jax.ShapeDtypeStruct((count, side // 2, 8, C_IN), BF16),
+        grid=(count,),
+        in_specs=[pl.BlockSpec((1, side, side, C_IN), lambda i: (i, 0, 0, 0))],
+        out_specs=pl.BlockSpec((1, side // 2, 8, C_IN), lambda i: (i, 0, 0, 0)),
+        scratch_shapes=[pltpu.VMEM((C_IN // 128, side * 8, 128), F32)],
+        compiler_params=pltpu.CompilerParams(vmem_limit_bytes=24 << 20),
+        cost_estimate=pl.CostEstimate(
+            flops=0, bytes_accessed=3 * count * side * side * C_IN, transcendentals=0
+        ),
+    )(views)
+    return padded
 
 
 def input_grad_kernel(cotan, kernel, strided, target, spread):
@@ -521,11 +815,12 @@
     return jnp.where(place < split, hidden_part, embed_part)
 
 
-def placed(rows, *pieces):
-    flat = jnp.zeros((rows, C_MID), BF16)
-    for at, piece in pieces:
-        flat = lax.dynamic_update_slice(flat, piece.astype(BF16), (at, 0))
-    return flat
+def placed(flat, at, piece):
+    return lax.dynamic_update_slice(flat, piece.astype(BF16), (at, 0))
+
+
+def cell_rows(values, size):
+    return pad_side(values, size).reshape(-1, values.shape[-1])
 
 
 def tied(*values):
@@ -543,11 +838,11 @@
         return lax.all_gather(flat.reshape(-1, C_MID), BOTH, axis=0, tiled=True)
 
     first = gather(block1_params)
+    head = gather(head_params)
     second = gather(block2_params)
-    head = gather(head_params)
-    strided = views[:, ::2, ::2, :]
-    partners = all_blocks(partner[:, None]).reshape(-1)
-    first, strided, partners = tied(first, strided, partners)
+    strided = even_cells(views)
+    full_views = pad_side(views, 16).reshape(-1, C_IN)
+    first, strided, full_views = tied(first, strided, full_views)
     w_reduce = first[:1024]
     w_spatial = first[1024:5632]
 
@@ -557,14 +852,13 @@
     rows = total_views * half * half
 
     raw_one = times(views, w_reduce)
-    w_short = unflatten(first, 7680, C_IN)
-    raw_short = times(strided, w_short)
-    sums, raw_short = tied(all_sum(moments(raw_one)), raw_short)
-    norm_one = Norm(raw_one, sums, norms[0], wide_rows)
+    norm_one = Norm(raw_one, all_sum(moments(raw_one)), norms[0], wide_rows)
     act_one = jax.nn.silu(norm_one.shifted()).astype(BF16)
     raw_two = conv(act_one, w_spatial, 2)
     w_expand = unflatten(first, 5632, C_MID)
-    sums, w_expand = tied(all_sum(moments(raw_two)), w_expand)
+    w_short = unflatten(first, 7680, C_IN)
+    raw_short = times(strided, w_short)[:, :, :half]
+    sums, w_expand, raw_short = tied(all_sum(moments(raw_two)), w_expand, raw_short)
     norm_two = Norm(raw_two, sums, norms[1], rows)
     act_two = jax.nn.silu(norm_two.shifted()).astype(BF16)
     raw_three = times(act_two, w_expand)
@@ -585,27 +879,41 @@
     norm_six = Norm(raw_six, all_sum(moments(raw_six)), norms[5], rows)
     act_four = jax.nn.silu(norm_six.shifted()).astype(BF16)
     raw_seven = times(act_four, w_widen)
-    w_hidden = unflatten(head, 0, C_OUT)
-    w_embed = head[4 * C_OUT :].reshape(HEAD, EMBED)
-    sums, w_hidden, w_embed = tied(all_sum(moments(raw_seven)), w_hidden, w_embed)
-    norm_seven = Norm(raw_seven, sums, norms[6], rows)
+    norm_seven = Norm(raw_seven, all_sum(moments(raw_seven)), norms[6], rows)
     joined_two = norm_seven.shifted() + result_one.astype(F32)
     pooled_own = jnp.mean(jax.nn.silu(joined_two), axis=(1, 2))
 
-    pooled = all_blocks(pooled_own).reshape(total_views, C_OUT)
-    raw_hidden = exact_times(pooled, w_hidden, 0)
-    norm_head = Norm(raw_hidden, moments(raw_hidden), norms[7], total_views)
-    shifted_head = norm_head.shifted()
-    hidden = jax.nn.silu(shifted_head)
-    embed = exact_times(hidden, w_embed, 0)
-    losses, unit_cot = contrast(unit_norm(embed).astype(BF16), partners, total_views)
-    _, norm_pull = jax.vjp(unit_norm, embed)
-    embed_cot = norm_pull(unit_cot)[0]
-    hidden_cot = exact_times(embed_cot, w_embed, 1) * silu_slope(shifted_head)
-    grads_head = norm_head.partial_grads(hidden_cot)
-    raw_hidden_cot = norm_head.pull(hidden_cot, grads_head)
-    own_cot = lax.dynamic_slice_in_dim(raw_hidden_cot, device * views_dev, views_dev, axis=0)
-    pooled_cot = exact_times(own_cot, w_hidden, 1)
+    gathered = gather_blocks(
+        jnp.concatenate(
+            [pooled_own, jnp.broadcast_to(partner.astype(F32)[:, None], (views_dev, EMBED))], axis=1
+        )
+    )
+    if total_views <= 256:
+        pooled, hidden, raw_hidden_cot, embed_cot, grads_head, losses, pooled_cot = head_pass(
+            gathered, head, norms[7]
+        )
+        losses = losses[:, 0]
+        pooled_cot = pooled_cot[:views_dev]
+    else:
+        w_hidden = unflatten(head, 0, C_OUT)
+        w_embed = head[4 * C_OUT :].reshape(HEAD, EMBED)
+        order = jnp.stack([place_of(device, i, count) for i in range(count)])
+        pooled = jnp.take(gathered, order, axis=0).reshape(total_views, -1)
+        partners = pooled[:, C_OUT].astype(jnp.int32)
+        pooled = pooled[:, :C_OUT]
+        raw_hidden = exact_times(pooled, w_hidden, 0)
+        norm_head = Norm(raw_hidden, moments(raw_hidden), norms[7], total_views)
+        shifted_head = norm_head.shifted()
+        hidden = jax.nn.silu(shifted_head)
+        embed = exact_times(hidden, w_embed, 0)
+        losses, unit_cot = contrast(unit_norm(embed).astype(BF16), partners, total_views)
+        _, norm_pull = jax.vjp(unit_norm, embed)
+        embed_cot = norm_pull(unit_cot)[0]
+        hidden_cot = exact_times(embed_cot, w_embed, 1) * silu_slope(shifted_head)
+        grads_head = norm_head.partial_grads(hidden_cot)
+        raw_hidden_cot = norm_head.pull(hidden_cot, grads_head)
+        own_cot = lax.dynamic_slice_in_dim(raw_hidden_cot, device * views_dev, views_dev, axis=0)
+        pooled_cot = exact_times(own_cot, w_hidden, 1)
 
     joined_cot = (pooled_cot / (half * half))[:, None, None, :] * silu_slope(joined_two)
     head_out = head_kernel_grads(pooled, raw_hidden_cot, hidden, embed_cot, head_params.shape[0])
@@ -613,82 +921,80 @@
     grads_seven, head_out, loss = tied(all_sum(norm_seven.partial_grads(joined_cot)), head_out, loss)
     low_seven = norm_seven.pull(joined_cot, grads_seven).astype(BF16)
     act_four_cot = times_back(low_seven, w_widen) * silu_slope(norm_six.shifted())
-    grad_widen = flat_grad(act_four, low_seven)
-    grads_six, grad_widen = tied(all_sum(norm_six.partial_grads(act_four_cot)), grad_widen)
+    second_grad = grad_into(second.shape[0], 6656, cell_rows(act_four, 8), cell_rows(low_seven, 8))
+    grads_six, second_grad = tied(all_sum(norm_six.partial_grads(act_four_cot)), second_grad)
     low_six = norm_six.pull(act_four_cot, grads_six).astype(BF16)
     act_three_cot = conv_back(low_six, w_middle, 1) * silu_slope(norm_five.shifted())
-    grad_middle = conv_kernel_grad(act_three, low_six, 1).astype(BF16)
-    grads_five, grad_middle = tied(all_sum(norm_five.partial_grads(act_three_cot)), grad_middle)
+    second_grad = placed(second_grad, 2048, conv_kernel_grad(act_three, low_six, 1))
+    grads_five, second_grad = tied(all_sum(norm_five.partial_grads(act_three_cot)), second_grad)
     low_five = norm_five.pull(act_three_cot, grads_five).astype(BF16)
     result_one_cot = joined_cot + times_back(low_five, w_narrow)
-    grad_narrow = kernel_grad(result_one, low_five)
 
     joined_one_cot = result_one_cot * silu_slope(joined_one)
-    grads_join = all_sum(
-        jnp.concatenate(
-            [
-                norm_three.partial_grads(joined_one_cot),
-                norm_short.partial_grads(joined_one_cot)[:1],
-            ],
-            axis=0,
-        )
-    )
-    second_rows = second.shape[0] // count
-    first_rows = first.shape[0] // count
+    grads_join = jnp.concatenate(
+        [norm_three.partial_grads(joined_one_cot), norm_short.partial_grads(joined_one_cot)[:1]],
+        axis=0,
+    )
+    second_grad = grad_into(
+        second.shape[0], 0, cell_rows(result_one, 8), cell_rows(low_five, 8), second_grad
+    )
     sum_second = ScatterSum(
-        placed(second.shape[0], (0, grad_narrow), (2048, grad_middle), (6656, grad_widen)).reshape(
-            count, second_rows, C_MID
-        ),
-        0,
-    )
-    grads_join = step([sum_second], grads_join)
+        second_grad.reshape(count, second.shape[0] // count, C_MID), 0, count
+    )
+    grads_join, second_grad = all_sum(grads_join, [sum_second], second_grad)
     grads_three = grads_join[:2]
     grads_short = jnp.stack([grads_join[2], grads_join[1]])
     low_three = norm_three.pull(joined_one_cot, grads_three).astype(BF16)
     low_short = norm_short.pull(joined_one_cot, grads_short).astype(BF16)
     act_two_cot = times_back(low_three, w_expand) * silu_slope(norm_two.shifted())
-    grad_expand = flat_grad(act_two, low_three)
-    grad_short = flat_grad(strided, low_short)
-    strided_cot = times_back(pad_side(low_short, 8), w_short)
-    grads_two = all_sum(norm_two.partial_grads(act_two_cot))
-    middle = count // 2 * first_rows
-    sum_late = ScatterSum(
-        placed(
-            middle, (0, grad_expand[middle - 5632 :]), (7680 - middle, grad_short)
-        ).reshape(count // 2, first_rows, C_MID),
-        count // 2,
-    )
-    grads_two = step([sum_second, sum_late], grads_two)
+    low_short = pad_side(low_short, 8)
+    first_grad = grad_into(first.shape[0], 5632, cell_rows(act_two, 8), cell_rows(low_three, 8))
+    first_grad = grad_into(
+        first.shape[0],
+        7680,
+        strided.reshape(-1, C_IN),
+        low_short.reshape(-1, C_OUT),
+        first_grad,
+    )
+    strided_cot = times_back(low_short, w_short)
+    grads_two = step([sum_second], norm_two.partial_grads(act_two_cot))
+    grads_two = all_sum(grads_two)
+    first_shape = (count, first.shape[0] // count, C_MID)
+    first_blocks = first_grad.reshape(first_shape)
+    part = count // 4
+    late = ScatterSum(first_blocks, 2 * part, 2 * part)
+    grads_two, first_grad = step([sum_second, late], (grads_two, first_grad))
     low_two = norm_two.pull(act_two_cot, grads_two).astype(BF16)
-    act_one_cot = conv_back(low_two, w_spatial, 2) * silu_slope(norm_one.shifted())
-    grad_spatial = conv_kernel_grad(act_one, low_two, 2)
-    grads_one = all_sum(norm_one.partial_grads(act_one_cot))
-    sum_early = ScatterSum(
-        placed(
-            middle, (1024, grad_spatial), (5632, grad_expand[: middle - 5632])
-        ).reshape(count // 2, first_rows, C_MID),
-        0,
-    )
-    grads_one = step([sum_second, sum_late, sum_early], grads_one)
-    low_one = norm_one.pull(act_one_cot, grads_one).astype(BF16)
-    grad_reduce = kernel_grad(views, low_one)
-    reduce_blocks = count // 8
-    sum_reduce = ScatterSum(
-        placed(reduce_blocks * first_rows, (0, grad_reduce)).reshape(
-            reduce_blocks, first_rows, C_MID
-        ),
-        0,
-    )
-    sums = [sum_reduce, sum_early, sum_late, sum_second]
-    low_one = step(sums, low_one)
-    views_cot = input_grad(pad_side(low_one, 16), w_reduce, strided_cot)
-    while not all(group.done() for group in sums):
-        step(sums, ())
+    act_one_cot = conv_back(low_two, w_spatial, 2)
+    act_one_cot, first_grad = step([late], (act_one_cot, first_grad))
+    act_one_cot = act_one_cot * silu_slope(norm_one.shifted())
+    grads_one, first_grad = step(
+        [sum_second], (norm_one.partial_grads(act_one_cot), first_grad)
+    )
+    grads_one = all_sum(grads_one)
+    first_grad = placed(first_grad, 1024, conv_kernel_grad(act_one, low_two, 2))
+    first_blocks = first_grad.reshape(first_shape)
+    early = ScatterSum(first_blocks, part, part)
+    grads_one, first_grad = step([early, late, sum_second], (grads_one, first_grad))
+    low_one = pad_side(norm_one.pull(act_one_cot, grads_one).astype(BF16), 16)
+    first_grad = grad_into(
+        first.shape[0], 0, full_views, low_one.reshape(-1, C_MID), first_grad
+    )
+    last = ScatterSum(first_grad.reshape(first_shape), 0, part)
+    early.source = last.source
+    low_one = step([early, last], low_one)
+    views_cot = input_grad(low_one, w_reduce, strided_cot)
+    groups = [early, last, late, sum_second]
+    while any(not group.done() for group in groups):
+        for group in groups:
+            if not group.done():
+                group.send(group.prepare())
 
     second_out = sum_second.result().reshape(-1)
-    early = sum_early.result()
-    early = early + jnp.where(device < reduce_blocks, sum_reduce.result(), 0.0)
-    first_out = jnp.where(device < count // 2, early, sum_late.result()).reshape(-1)
+    first_out = last.result()
+    for group in [early, late]:
+        first_out = jnp.where(device < group.base, first_out, group.result())
+    first_out = first_out.reshape(-1)
     norm_grad = jnp.concatenate(
         [
             grads_one,

time: 712 us -> 595 us (0.84)
  local copies, waits for them, and re-layouts: 96 us -> 47.2 us
  Pallas kernels: 74.9 us -> 55.6 us
  other arithmetic: 38.3 us -> 23.7 us
  matrix products: 77.3 us -> 64.1 us
  starting transfers between devices: 135 us -> 125 us
  waiting for transfers between devices: 262 us -> 253 us
    ppermute x20, waiting for transfers between devices: 81.6 us -> 52.8 us  [send(): self.incoming = lax.ppermute(outgoing, BOTH, pairs)]
    pallas_call x5 -> x7, Pallas kernels: 9.46 us -> 38.2 us  [the longest x1 22.6 us: head_pass(): pl.pallas_call(head_kernel, out_shape=[shape((total, C_OUT), F32), shape(...]
    pallas_call x16 -> x11, Pallas kernels: 27.1 us -> 4.89 us  [add_blocks(): pl.pallas_call(add_kernel, out_shape=[shape] * ways, grid_spec=pltpu.Pref...]
    pallas_call x4, Pallas kernels: 24.5 us -> 2.47 us  [copy_blocks(): pl.pallas_call(copy_kernel, out_shape=jax.ShapeDtypeStruct(shape, source....]
    unnamed x330 -> x215, local copies, waits for them, and re-layouts: 41.5 us -> 22.5 us
    slice x4 -> x1, local copies, waits for them, and re-layouts: 18.5 us -> 0.01 us  [split_norms(): pieces.append(norm_params[:, offset:offset + span_width])]
    ppermute x98 -> x91, waiting for transfers between devices: 75.9 us -> 91.5 us  [swap(): lax.ppermute(values, BOTH, [(i, i ^ mask) for i in range(device_count())])]
    dot_general x8 -> x0, matrix products: 14.9 us -> none  [the longest x4 9.38 us: exact_times(): lax.dot_general(terms, kernel, (((1,), (contract,)), ((), ())), preferred...]
  transfers between devices with their start and end apart: 121 -> 114, of which waited for: 59 -> 54; matrix products, arithmetic and copies ran while one was open for 17% -> 15% of each run, Pallas kernels for 9% -> 5%
where the time goes in v2:
time: 595 us; the launch traced here: 585 us
  waiting for transfers between devices  253 us (43%)
  starting transfers between devices  125 us (21%)
  matrix products  64.1 us (11%)
  Pallas kernels  55.6 us (9%)
  local copies, waits for them, and re-layouts  47.2 us (8%)
  other arithmetic  23.7 us (4%)
  between operations  16.2 us (3%)
    all_gather x3, waiting for transfers between devices, gather(): return lax.all_gather(flat.reshape(-1, C_MID), BOTH, axis=0, tiled=True)  109 us
    ppermute x91, starting transfers between devices, swap(): lax.ppermute(values, BOTH, [(i, i ^ mask) for i in range(device_count())])  105 us
    ppermute x91, waiting for transfers between devices, swap(): lax.ppermute(values, BOTH, [(i, i ^ mask) for i in range(device_count())])  91.5 us
    ppermute x20, waiting for transfers between devices, send(): self.incoming = lax.ppermute(outgoing, BOTH, pairs)  52.8 us
    pallas_call x1, Pallas kernels, head_pass(): pl.pallas_call(head_kernel, out_shape=[shape((total, C_OUT), F32), shape(...  22.6 us
    unnamed x215, local copies, waits for them, and re-layouts  22.5 us
    ppermute x20, starting transfers between devices, send(): self.incoming = lax.ppermute(outgoing, BOTH, pairs)  19.7 us
    dot_general x4, matrix products, times_back(): lax.dot_general(cotan, kernel, (((cotan.ndim - 1,), (1,)), ((), ())), pre...  18.2 us
  transfers between devices with their start and end apart: 114, of which 54 were waited for; matrix products, arithmetic and copies ran while one was open for 15% of the time, Pallas kernels for 5%

profile of v2, /device:TPU:0, one launch (start us, length us, event | category | flops | bytes accessed | tf_op | source)
XLA Modules:
  0.0 585.0 jit_solution(2887065185712952950)
XLA Ops:
  16.8 91.1 %all-gather.4.cloned.1.call-done.source = bf16[11776,512]{1,0:T(8,128)(2,1)} async-done(((bf16[368,512]{1,0:T(8,128)(2,1)}), bf16[11776,512]{1,0:T(8,128)(2,1)}) %all-gather.4.cloned.1.call-update) | async-done | bytes 12058640 | tf_op jit(solution)/shard_map/all_gather | solution.py:838
  108.0 4.6 fusion.67
  125.3 2.8 slice.200
  130.0 4.5 fusion.69
  144.9 2.7 collective-permute-start.11
  160.5 2.6 collective-permute-start.20
  167.3 2.9 collective-permute-done.19
  172.7 17.5 %all-gather.6.cloned.1.call-done.source = bf16[8704,512]{1,0:T(8,128)(2,1)} async-done(((bf16[272,512]{1,0:T(8,128)(2,1)}), bf16[8704,512]{1,0:T(8,128)(2,1)}) %all-gather.6.cloned.1.call-update) | async-done | bytes 8912912 | tf_op jit(solution)/shard_map/all_gather | solution.py:838
  190.2 3.5 fusion.70
  205.8 3.6 copy-done.2
  214.7 3.3 fusion.68
  223.0 2.6 collective-permute-done.31
  227.2 2.9 collective-permute-start.32
  253.5 2.8 collective-permute-start.42
  256.3 3.9 collective-permute-done.44
  260.2 6.3 %collective-permute-done.43 = f32[1,6,2176]{2,1,0:T(8,128)S(1)} collective-permute-done((f32[1,6,2176]{2,1,0:T(8,128)S(1)}, f32[1,6,2176]{2,1,0:T(8,128)S(1)}, u32[]{:S(2)}, u32[]{:S(2)}) %collective-permute-start.43) | collective-permute-done | bytes 52256 | tf_op jit(solution)/shard_map/ppermute | solution.py:30
  270.2 9.6 %collective-permute-done.45 = f32[4,6,2176]{2,1,0:T(8,128)S(1)} collective-permute-done((f32[4,6,2176]{2,1,0:T(8,128)S(1)}, f32[4,6,2176]{2,1,0:T(8,128)S(1)}, u32[]{:S(2)}, u32[]{:S(2)}) %collective-permute-start.45) | collective-permute-done | bytes 208928 | tf_op jit(solution)/shard_map/ppermute | solution.py:30
  286.2 22.6 %shard_map.149 = (f32[192,2048]{1,0:T(8,128)}, f32[192,2048]{1,0:T(8,128)}, f32[192,2048]{1,0:T(8,128)}, f32[192,128]{1,0:T(8,128)S(1)}, f32[2,2048]{1,0:T(2,128...) custom-call(s32[1]{0:T(128)} %bitcast.device, f32[32,6,2176]{2,1,0:T(8,128)} %copy_dynamic-update-slice_fusion.gathered, ...), custom_call_target="tpu_custom_call" | custom-call | flops 3221225472 | bytes 20971520 | tf_op jit(solution)/shard_map/pallas_call | solution.py:282
  308.9 3.4 multiply_reduce_fusion.2
  317.1 3.5 fusion.39
  322.6 2.7 collective-permute-start.55
  327.0 4.2 fusion
  332.0 2.6 multiply_convert_fusion.2
  334.6 2.6 multiply_reduce_fusion.10
  344.5 2.7 collective-permute-start.62
  352.0 3.4 multiply_reduce_fusion.9
  360.2 4.0 convolution_convert_fusion.1
  372.1 6.6 %multiply_reduce_fusion.1 = (f32[2048]{0:T(1024)S(1)}, f32[2048]{0:T(1024)S(1)}, f32[2048]{0:T(1024)S(1)}, f32[6,7,7,2048]{3,2,1,0:T(8,128)}) fusion(f32[6,7,7,2048]{3,2,1,0:T(8,128)S(1)} %copy-done.31, f32[2048]{0:T(1024)S(1)} %get-tuple-element.250, f32[2048]{0:T(1024)S(1)} %bitcast.246, f32[2048]{0:T(1024)S(1)} %get-tuple-element.207, ...), kind=kOutput, calls=%fused_computation.23 | convolution fusion | flops 630405120 | bytes 12122112 | tf_op jit(solution)/shard_map/dot_general | solution.py:629
  383.6 2.8 shard_map.151
  387.4 2.5 collective-permute-start.76
  395.5 3.0 multiply_convert_fusion
  398.5 4.5 multiply_reduce_fusion.8
  412.8 19.5 %collective-permute-done.81 = f32[2,512]{1,0:T(2,128)S(1)} collective-permute-done((f32[2,512]{1,0:T(2,128)S(1)}, f32[2,512]{1,0:T(2,128)S(1)}, u32[]{:S(2)}, u32[]{:S(2)}) %collective-permute-start.81) | collective-permute-done | bytes 4128 | tf_op jit(solution)/shard_map/ppermute | solution.py:30
  436.8 4.6 shard_map.155
  444.3 3.5 fusion.75
  447.8 10.3 %collective-permute-done.87.refs_1_.refs_3_ = bf16[4,272,512]{2,1,0:T(8,128)(2,1)S(1)} collective-permute-done((bf16[4,272,512]{2,1,0:T(8,128)(2,1)S(1)}, bf16[4,272,512]{2,1,0:T(8,128)(2,1)S(1)}, u32[]{:S(2)}, u32[]{:S(2)}) %collective-permute-start.87) | collective-permute-done | bytes 1114144 | tf_op jit(solution)/shard_map/ppermute | solution.py:463
  467.3 6.3 %convolution_convert_fusion = bf16[3,3,512,512]{3,2,1,0:T(8,128)(2,1)} fusion(bf16[6,7,7,512]{3,0,2,1:T(8,128)(2,1)S(1)} %multiply_convert_fusion.5, bf16[6,14,14,512]{3,2,1,0:T(8,128)(2,1)S(1)} %copy-done.42), kind=kOutput, calls=%fused_computation.9 | convolution fusion | flops 1260650496 | bytes 6223872 | tf_op jit(solution)/shard_map/conv_general_dilated | solution.py:671
  473.8 9.0 %collective-permute-done.91 = f32[2,512]{1,0:T(2,128)S(1)} collective-permute-done((f32[2,512]{1,0:T(2,128)S(1)}, f32[2,512]{1,0:T(2,128)S(1)}, u32[]{:S(2)}, u32[]{:S(2)}) %collective-permute-start.91) | collective-permute-done | bytes 4128 | tf_op jit(solution)/shard_map/ppermute | solution.py:30
  487.3 2.9 constant_dynamic-update-slice_fusion.22.refs_0_
  495.4 2.8 shard_map.163
  499.5 3.5 copy-done
  507.2 4.5 fusion.1.strided
  516.7 12.9 %collective-permute-done.103.refs_1_.refs_3_ = bf16[2,368,512]{2,1,0:T(8,128)(2,1)S(1)} collective-permute-done((bf16[2,368,512]{2,1,0:T(8,128)(2,1)S(1)}, bf16[2,368,512]{2,1,0:T(8,128)(2,1)S(1)}, u32[]{:S(2)}, u32[]{:S(2)}) %collective-permute-start.103) | collective-permute-done | bytes 753696 | tf_op jit(solution)/shard_map/ppermute | solution.py:463
  530.9 12.8 %collective-permute-done.99.refs_1_.refs_3_ = bf16[2,368,512]{2,1,0:T(8,128)(2,1)S(1)} collective-permute-done((bf16[2,368,512]{2,1,0:T(8,128)(2,1)S(1)}, bf16[2,368,512]{2,1,0:T(8,128)(2,1)S(1)}, u32[]{:S(2)}, u32[]{:S(2)}) %collective-permute-start.99) | collective-permute-done | bytes 753696 | tf_op jit(solution)/shard_map/ppermute | solution.py:463
  545.8 3.5 collective-permute-start.105
  552.9 8.9 %collective-permute-done.108 = bf16[1,368,512]{2,1,0:T(8,128)(2,1)S(1)} collective-permute-done((bf16[1,368,512]{2,1,0:T(8,128)(2,1)S(1)}, bf16[1,368,512]{2,1,0:T(8,128)(2,1)S(1)}, u32[]{:S(2)}, u32[]{:S(2)}) %collective-permute-start.108) | collective-permute-done | bytes 376864 | tf_op jit(solution)/shard_map/ppermute | solution.py:463
  568.8 4.8 shard_map.166
  573.6 3.4 collective-permute-done.102
  (568 shorter events, 217.4 us)
Async XLA Ops:
  7.2 100.8 %all-gather.4.cloned.1.call-start = ((), (), s32[]{:S(2)}) async-start(), calls=%async_computation | async-start | bytes 12435456 | tf_op jit(solution)/shard_map/all_gather | solution.py:838
  9.2 181.0 %all-gather.6.cloned.1.call-start = ((), (), s32[]{:S(2)}) async-start(), calls=%async_computation.1 | async-start | bytes 9191424 | tf_op jit(solution)/shard_map/all_gather | solution.py:838
  11.1 275.1 %all-gather.8.cloned.1.call-start = ((), (), s32[]{:S(2)}) async-start(), calls=%async_computation.2 | async-start | bytes 9191424 | tf_op jit(solution)/shard_map/all_gather | solution.py:838
  120.2 7.9 %collective-permute-start.6 = (f32[2,512]{1,0:T(2,128)S(1)}, f32[2,512]{1,0:T(2,128)S(1)}, u32[]{:S(2)}, u32[]{:S(2)}) collective-permute-start(f32[2,512]{1,0:T(2,128)S(1)} %add_add_fusion.24), channel_id=1, source_target_pairs={{0,24},{1,25},{2,26},{3,27},{4,28},{5,29},{6,30},{7,31},{8,16},{9,... | collective-permute-start | bytes 12296 | tf_op jit(solution)/shard_map/ppermute | solution.py:30
  163.1 7.2 %collective-permute-start.19 = (f32[4,2048]{1,0:T(4,128)S(1)}, f32[4,2048]{1,0:T(4,128)S(1)}, u32[]{:S(2)}, u32[]{:S(2)}) collective-permute-start(f32[4,2048]{1,0:T(4,128)S(1)} %add_add_fusion.4), channel_id=1, source_target_pairs={{0,16},{1,17},{2,18},{3,19},{4,20},{5,21},{6,22},{7,23},{8,24},{9,... | collective-permute-start | bytes 98312 | tf_op jit(solution)/shard_map/ppermute | solution.py:30
  201.4 11.9 %collective-permute-start.27 = (f32[2,512]{1,0:T(2,128)S(1)}, f32[2,512]{1,0:T(2,128)S(1)}, u32[]{:S(2)}, u32[]{:S(2)}) collective-permute-start(f32[2,512]{1,0:T(2,128)S(1)} %add_add_fusion.20), channel_id=1, source_target_pairs={{0,24},{1,25},{2,26},{3,27},{4,28},{5,29},{6,30},{7,31},{8,16},{9,... | collective-permute-start | bytes 12296 | tf_op jit(solution)/shard_map/ppermute | solution.py:30
  203.1 10.2 %collective-permute-start.26 = (f32[2,512]{1,0:T(2,128)S(1)}, f32[2,512]{1,0:T(2,128)S(1)}, u32[]{:S(2)}, u32[]{:S(2)}) collective-permute-start(f32[2,512]{1,0:T(2,128)S(1)} %add_add_fusion.20), channel_id=1, source_target_pairs={{0,16},{1,17},{2,18},{3,19},{4,20},{5,21},{6,22},{7,23},{8,24},{9,... | collective-permute-start | bytes 12296 | tf_op jit(solution)/shard_map/ppermute | solution.py:30
  203.9 9.4 %collective-permute-start.25 = (f32[2,512]{1,0:T(2,128)S(1)}, f32[2,512]{1,0:T(2,128)S(1)}, u32[]{:S(2)}, u32[]{:S(2)}) collective-permute-start(f32[2,512]{1,0:T(2,128)S(1)} %add_add_fusion.20), channel_id=1, source_target_pairs={{0,8},{1,9},{2,10},{3,11},{4,12},{5,13},{6,14},{7,15},{8,0},{9,1},... | collective-permute-start | bytes 12296 | tf_op jit(solution)/shard_map/ppermute | solution.py:30
  251.8 8.4 %collective-permute-start.44 = (f32[1,6,2176]{2,1,0:T(8,128)S(1)}, f32[1,6,2176]{2,1,0:T(8,128)S(1)}, u32[]{:S(2)}, u32[]{:S(2)}) collective-permute-start(f32[1,6,2176]{2,1,0:T(8,128)S(1)} %maximum_bitcast_fusion), channel_id=1, source_target_pairs={{0,24},{1,25},{2,26},{3,27},{4,28},{5,29},{6,30},{7,31},{8,16},{9,... | collective-permute-start | bytes 156680 | tf_op jit(solution)/shard_map/ppermute | solution.py:30
  253.4 13.1 %collective-permute-start.43 = (f32[1,6,2176]{2,1,0:T(8,128)S(1)}, f32[1,6,2176]{2,1,0:T(8,128)S(1)}, u32[]{:S(2)}, u32[]{:S(2)}) collective-permute-start(f32[1,6,2176]{2,1,0:T(8,128)S(1)} %maximum_bitcast_fusion), channel_id=1, source_target_pairs={{0,16},{1,17},{2,18},{3,19},{4,20},{5,21},{6,22},{7,23},{8,24},{9,... | collective-permute-start | bytes 156680 | tf_op jit(solution)/shard_map/ppermute | solution.py:30
  253.5 13.0 %collective-permute-start.42 = (f32[1,6,2176]{2,1,0:T(8,128)S(1)}, f32[1,6,2176]{2,1,0:T(8,128)S(1)}, u32[]{:S(2)}, u32[]{:S(2)}) collective-permute-start(f32[1,6,2176]{2,1,0:T(8,128)S(1)} %maximum_bitcast_fusion), channel_id=1, source_target_pairs={{0,8},{1,9},{2,10},{3,11},{4,12},{5,13},{6,14},{7,15},{8,0},{9,1},... | collective-permute-start | bytes 156680 | tf_op jit(solution)/shard_map/ppermute | solution.py:30
  266.6 13.3 %collective-permute-start.47 = (f32[4,6,2176]{2,1,0:T(8,128)S(1)}, f32[4,6,2176]{2,1,0:T(8,128)S(1)}, u32[]{:S(2)}, u32[]{:S(2)}) collective-permute-start(f32[4,6,2176]{2,1,0:T(8,128)S(1)} %pad_maximum_fusion), channel_id=1, source_target_pairs={{0,6},{1,7},{2,4},{3,5},{4,2},{5,3},{6,0},{7,1},{8,14},{9,15},{10,... | collective-permute-start | bytes 626696 | tf_op jit(solution)/shard_map/ppermute | solution.py:30
  268.5 11.3 %collective-permute-start.46 = (f32[4,6,2176]{2,1,0:T(8,128)S(1)}, f32[4,6,2176]{2,1,0:T(8,128)S(1)}, u32[]{:S(2)}, u32[]{:S(2)}) collective-permute-start(f32[4,6,2176]{2,1,0:T(8,128)S(1)} %pad_maximum_fusion), channel_id=1, source_target_pairs={{0,4},{1,5},{2,6},{3,7},{4,0},{5,1},{6,2},{7,3},{8,12},{9,13},{10,... | collective-permute-start | bytes 626696 | tf_op jit(solution)/shard_map/ppermute | solution.py:30
  269.3 10.4 %collective-permute-start.45 = (f32[4,6,2176]{2,1,0:T(8,128)S(1)}, f32[4,6,2176]{2,1,0:T(8,128)S(1)}, u32[]{:S(2)}, u32[]{:S(2)}) collective-permute-start(f32[4,6,2176]{2,1,0:T(8,128)S(1)} %pad_maximum_fusion), channel_id=1, source_target_pairs={{0,2},{1,3},{2,0},{3,1},{4,6},{5,7},{6,4},{7,5},{8,10},{9,11},{10,... | collective-permute-start | bytes 626696 | tf_op jit(solution)/shard_map/ppermute | solution.py:30
  313.6 9.0 %collective-permute-start.51 = (f32[2,2048]{1,0:T(2,128)S(1)}, f32[2,2048]{1,0:T(2,128)S(1)}, u32[]{:S(2)}, u32[]{:S(2)}) collective-permute-start(f32[2,2048]{1,0:T(2,128)S(1)} %fusion.57), channel_id=1, source_target_pairs={{0,4},{1,5},{2,6},{3,7},{4,0},{5,1},{6,2},{7,3},{8,12},{9,13},{10,... | collective-permute-start | bytes 49160 | tf_op jit(solution)/shard_map/ppermute | solution.py:30
  314.7 7.9 %collective-permute-start.52 = (f32[2,2048]{1,0:T(2,128)S(1)}, f32[2,2048]{1,0:T(2,128)S(1)}, u32[]{:S(2)}, u32[]{:S(2)}) collective-permute-start(f32[2,2048]{1,0:T(2,128)S(1)} %fusion.57), channel_id=1, source_target_pairs={{0,6},{1,7},{2,4},{3,5},{4,2},{5,3},{6,0},{7,1},{8,14},{9,15},{10,... | collective-permute-start | bytes 49160 | tf_op jit(solution)/shard_map/ppermute | solution.py:30
  322.6 9.3 %collective-permute-start.55 = (f32[2,2048]{1,0:T(2,128)S(1)}, f32[2,2048]{1,0:T(2,128)S(1)}, u32[]{:S(2)}, u32[]{:S(2)}) collective-permute-start(f32[2,2048]{1,0:T(2,128)S(1)} %add_add_fusion.6), channel_id=1, source_target_pairs={{0,24},{1,25},{2,26},{3,27},{4,28},{5,29},{6,30},{7,31},{8,16},{9,... | collective-permute-start | bytes 49160 | tf_op jit(solution)/shard_map/ppermute | solution.py:30
  344.5 7.0 %collective-permute-start.62 = (f32[2,512]{1,0:T(2,128)S(1)}, f32[2,512]{1,0:T(2,128)S(1)}, u32[]{:S(2)}, u32[]{:S(2)}) collective-permute-start(f32[2,512]{1,0:T(2,128)S(1)} %add_add_fusion.16), channel_id=1, source_target_pairs={{0,24},{1,25},{2,26},{3,27},{4,28},{5,29},{6,30},{7,31},{8,16},{9,... | collective-permute-start | bytes 12296 | tf_op jit(solution)/shard_map/ppermute | solution.py:30
  356.6 7.5 %collective-permute-start.65 = (f32[2,512]{1,0:T(2,128)S(1)}, f32[2,512]{1,0:T(2,128)S(1)}, u32[]{:S(2)}, u32[]{:S(2)}) collective-permute-start(f32[2,512]{1,0:T(2,128)S(1)} %fusion.51), channel_id=1, source_target_pairs={{0,4},{1,5},{2,6},{3,7},{4,0},{5,1},{6,2},{7,3},{8,12},{9,13},{10,... | collective-permute-start | bytes 12296 | tf_op jit(solution)/shard_map/ppermute | solution.py:30
  380.1 7.2 %collective-permute-start.72 = (f32[3,2048]{1,0:T(4,128)S(1)}, f32[3,2048]{1,0:T(4,128)S(1)}, u32[]{:S(2)}, u32[]{:S(2)}) collective-permute-start(f32[3,2048]{1,0:T(4,128)S(1)} %fusion.59), channel_id=1, source_target_pairs={{0,4},{1,5},{2,6},{3,7},{4,0},{5,1},{6,2},{7,3},{8,12},{9,13},{10,... | collective-permute-start | bytes 73736 | tf_op jit(solution)/shard_map/ppermute | solution.py:30
  387.3 15.7 %collective-permute-start.77 = (bf16[16,272,512]{2,1,0:T(8,128)(2,1)S(1)}, bf16[16,272,512]{2,1,0:T(8,128)(2,1)S(1)}, u32[]{:S(2)}, u32[]{:S(2)}) collective-permute-start(bf16[16,272,512]{2,1,0:T(8,128)(2,1)S(1)} %shard_map.152), channel_id=1, source_target_pairs={{0,1},{1,0},{2,3},{3,2},{4,5},{5,4},{6,7},{7,6},{8,9},{9,8},{10,11... | collective-permute-start | bytes 13369352 | tf_op jit(solution)/shard_map/ppermute | solution.py:463
  404.3 37.5 %collective-permute-start.85 = (bf16[8,272,512]{2,1,0:T(8,128)(2,1)S(1)}, bf16[8,272,512]{2,1,0:T(8,128)(2,1)S(1)}, u32[]{:S(2)}, u32[]{:S(2)}) collective-permute-start(bf16[8,272,512]{2,1,0:T(8,128)(2,1)S(1)} %get-tuple-element.96), channel_id=1, source_target_pairs={{0,2},{1,5},{2,0},{3,7},{4,6},{5,1},{6,4},{7,3},{8,10},{9,13},{10,... | collective-permute-start | bytes 6684680 | tf_op jit(solution)/shard_map/ppermute | solution.py:463
  406.7 25.6 %collective-permute-start.81 = (f32[2,512]{1,0:T(2,128)S(1)}, f32[2,512]{1,0:T(2,128)S(1)}, u32[]{:S(2)}, u32[]{:S(2)}) collective-permute-start(f32[2,512]{1,0:T(2,128)S(1)} %add.678), channel_id=1, source_target_pairs={{0,6},{1,7},{2,4},{3,5},{4,2},{5,3},{6,0},{7,1},{8,14},{9,15},{10,... | collective-permute-start | bytes 12296 | tf_op jit(solution)/shard_map/ppermute | solution.py:30
  408.0 24.4 %collective-permute-start.80 = (f32[2,512]{1,0:T(2,128)S(1)}, f32[2,512]{1,0:T(2,128)S(1)}, u32[]{:S(2)}, u32[]{:S(2)}) collective-permute-start(f32[2,512]{1,0:T(2,128)S(1)} %add.678), channel_id=1, source_target_pairs={{0,4},{1,5},{2,6},{3,7},{4,0},{5,1},{6,2},{7,3},{8,12},{9,13},{10,... | collective-permute-start | bytes 12296 | tf_op jit(solution)/shard_map/ppermute | solution.py:30
  409.0 23.4 %collective-permute-start.79 = (f32[2,512]{1,0:T(2,128)S(1)}, f32[2,512]{1,0:T(2,128)S(1)}, u32[]{:S(2)}, u32[]{:S(2)}) collective-permute-start(f32[2,512]{1,0:T(2,128)S(1)} %add.678), channel_id=1, source_target_pairs={{0,2},{1,3},{2,0},{3,1},{4,6},{5,7},{6,4},{7,5},{8,10},{9,11},{10,... | collective-permute-start | bytes 12296 | tf_op jit(solution)/shard_map/ppermute | solution.py:30
  432.4 9.3 %collective-permute-start.84 = (f32[2,512]{1,0:T(2,128)S(1)}, f32[2,512]{1,0:T(2,128)S(1)}, u32[]{:S(2)}, u32[]{:S(2)}) collective-permute-start(f32[2,512]{1,0:T(2,128)S(1)} %add_add_fusion.12), channel_id=1, source_target_pairs={{0,24},{1,25},{2,26},{3,27},{4,28},{5,29},{6,30},{7,31},{8,16},{9,... | collective-permute-start | bytes 12296 | tf_op jit(solution)/shard_map/ppermute | solution.py:30
  434.5 7.2 %collective-permute-start.83 = (f32[2,512]{1,0:T(2,128)S(1)}, f32[2,512]{1,0:T(2,128)S(1)}, u32[]{:S(2)}, u32[]{:S(2)}) collective-permute-start(f32[2,512]{1,0:T(2,128)S(1)} %add_add_fusion.12), channel_id=1, source_target_pairs={{0,16},{1,17},{2,18},{3,19},{4,20},{5,21},{6,22},{7,23},{8,24},{9,... | collective-permute-start | bytes 12296 | tf_op jit(solution)/shard_map/ppermute | solution.py:30
  442.4 16.0 %collective-permute-start.86 = (bf16[8,368,512]{2,1,0:T(8,128)(2,1)S(1)}, bf16[8,368,512]{2,1,0:T(8,128)(2,1)S(1)}, u32[]{:S(2)}, u32[]{:S(2)}) collective-permute-start(bf16[8,368,512]{2,1,0:T(8,128)(2,1)S(1)} %shard_map.157), channel_id=1, source_target_pairs={{0,1},{1,0},{2,3},{3,2},{4,5},{5,4},{6,7},{7,6},{8,9},{9,8},{10,11... | collective-permute-start | bytes 9043976 | tf_op jit(solution)/shard_map/ppermute | solution.py:463
  442.5 15.6 %collective-permute-start.87 = (bf16[4,272,512]{2,1,0:T(8,128)(2,1)S(1)}, bf16[4,272,512]{2,1,0:T(8,128)(2,1)S(1)}, u32[]{:S(2)}, u32[]{:S(2)}) collective-permute-start(bf16[4,272,512]{2,1,0:T(8,128)(2,1)S(1)} %get-tuple-element.105), channel_id=1, source_target_pairs={{0,4},{1,3},{2,6},{3,1},{4,0},{5,7},{6,2},{7,5},{8,12},{9,11},{10,... | collective-permute-start | bytes 3342344 | tf_op jit(solution)/shard_map/ppermute | solution.py:463
  462.5 28.1 %collective-permute-start.95 = (bf16[4,368,512]{2,1,0:T(8,128)(2,1)S(1)}, bf16[4,368,512]{2,1,0:T(8,128)(2,1)S(1)}, u32[]{:S(2)}, u32[]{:S(2)}) collective-permute-start(bf16[4,368,512]{2,1,0:T(8,128)(2,1)S(1)} %get-tuple-element.110), channel_id=1, source_target_pairs={{0,2},{1,5},{2,0},{3,7},{4,6},{5,1},{6,4},{7,3},{8,10},{9,13},{10,... | collective-permute-start | bytes 4521992 | tf_op jit(solution)/shard_map/ppermute | solution.py:463
  463.8 19.0 %collective-permute-start.91 = (f32[2,512]{1,0:T(2,128)S(1)}, f32[2,512]{1,0:T(2,128)S(1)}, u32[]{:S(2)}, u32[]{:S(2)}) collective-permute-start(f32[2,512]{1,0:T(2,128)S(1)} %add.686), channel_id=1, source_target_pairs={{0,6},{1,7},{2,4},{3,5},{4,2},{5,3},{6,0},{7,1},{8,14},{9,15},{10,... | collective-permute-start | bytes 12296 | tf_op jit(solution)/shard_map/ppermute | solution.py:30
  465.3 17.5 %collective-permute-start.90 = (f32[2,512]{1,0:T(2,128)S(1)}, f32[2,512]{1,0:T(2,128)S(1)}, u32[]{:S(2)}, u32[]{:S(2)}) collective-permute-start(f32[2,512]{1,0:T(2,128)S(1)} %add.686), channel_id=1, source_target_pairs={{0,4},{1,5},{2,6},{3,7},{4,0},{5,1},{6,2},{7,3},{8,12},{9,13},{10,... | collective-permute-start | bytes 12296 | tf_op jit(solution)/shard_map/ppermute | solution.py:30
  466.3 16.5 %collective-permute-start.89 = (f32[2,512]{1,0:T(2,128)S(1)}, f32[2,512]{1,0:T(2,128)S(1)}, u32[]{:S(2)}, u32[]{:S(2)}) collective-permute-start(f32[2,512]{1,0:T(2,128)S(1)} %add.686), channel_id=1, source_target_pairs={{0,2},{1,3},{2,0},{3,1},{4,6},{5,7},{6,4},{7,5},{8,10},{9,11},{10,... | collective-permute-start | bytes 12296 | tf_op jit(solution)/shard_map/ppermute | solution.py:30
  473.7 16.7 %collective-permute-start.96 = (bf16[2,272,512]{2,1,0:T(8,128)(2,1)S(1)}, bf16[2,272,512]{2,1,0:T(8,128)(2,1)S(1)}, u32[]{:S(2)}, u32[]{:S(2)}) collective-permute-start(bf16[2,272,512]{2,1,0:T(8,128)(2,1)S(1)} %get-tuple-element.113), channel_id=1, source_target_pairs={{0,8},{1,9},{2,10},{3,11},{4,12},{5,13},{6,14},{7,15},{8,0},{9,1},... | collective-permute-start | bytes 1671176 | tf_op jit(solution)/shard_map/ppermute | solution.py:463
  482.8 7.5 %collective-permute-start.94 = (f32[2,512]{1,0:T(2,128)S(1)}, f32[2,512]{1,0:T(2,128)S(1)}, u32[]{:S(2)}, u32[]{:S(2)}) collective-permute-start(f32[2,512]{1,0:T(2,128)S(1)} %add_add_fusion.10), channel_id=1, source_target_pairs={{0,24},{1,25},{2,26},{3,27},{4,28},{5,29},{6,30},{7,31},{8,16},{9,... | collective-permute-start | bytes 12296 | tf_op jit(solution)/shard_map/ppermute | solution.py:30
  505.2 7.9 %collective-permute-start.98 = (bf16[4,368,512]{2,1,0:T(8,128)(2,1)}, bf16[4,368,512]{2,1,0:T(8,128)(2,1)S(1)}, u32[]{:S(2)}, u32[]{:S(2)}) collective-permute-start(bf16[4,368,512]{2,1,0:T(8,128)(2,1)} %shard_map.165), channel_id=1, source_target_pairs={{0,1},{1,0},{2,3},{3,2},{4,5},{5,4},{6,7},{7,6},{8,9},{9,8},{10,11... | collective-permute-start | bytes 4521992 | tf_op jit(solution)/shard_map/ppermute | solution.py:463
  511.8 17.8 %collective-permute-start.103 = (bf16[2,368,512]{2,1,0:T(8,128)(2,1)S(1)}, bf16[2,368,512]{2,1,0:T(8,128)(2,1)S(1)}, u32[]{:S(2)}, u32[]{:S(2)}) collective-permute-start(bf16[2,368,512]{2,1,0:T(8,128)(2,1)S(1)} %copy-done.18), channel_id=1, source_target_pairs={{0,2},{1,5},{2,0},{3,7},{4,6},{5,1},{6,4},{7,3},{8,10},{9,13},{10,... | collective-permute-start | bytes 2261000 | tf_op jit(solution)/shard_map/ppermute | solution.py:463
  513.5 30.2 %collective-permute-start.99 = (bf16[2,368,512]{2,1,0:T(8,128)(2,1)S(1)}, bf16[2,368,512]{2,1,0:T(8,128)(2,1)S(1)}, u32[]{:S(2)}, u32[]{:S(2)}) collective-permute-start(bf16[2,368,512]{2,1,0:T(8,128)(2,1)S(1)} %get-tuple-element.123), channel_id=1, source_target_pairs={{0,2},{1,5},{2,0},{3,7},{4,6},{5,1},{6,4},{7,3},{8,10},{9,13},{10,... | collective-permute-start | bytes 2261000 | tf_op jit(solution)/shard_map/ppermute | solution.py:463
  514.3 53.4 %collective-permute-start.110 = (bf16[1,272,512]{2,1,0:T(8,128)(2,1)S(1)}, bf16[1,272,512]{2,1,0:T(8,128)(2,1)S(1)}, u32[]{:S(2)}, u32[]{:S(2)}) collective-permute-start(bf16[1,272,512]{2,1,0:T(8,128)(2,1)S(1)} %get-tuple-element.135), channel_id=1, source_target_pairs={{0,16},{1,17},{2,18},{3,19},{4,20},{5,21},{6,22},{7,23},{8,24},{9,... | collective-permute-start | bytes 835592 | tf_op jit(solution)/shard_map/ppermute | solution.py:463
  515.6 29.4 %collective-permute-start.107 = (bf16[2,368,512]{2,1,0:T(8,128)(2,1)S(1)}, bf16[2,368,512]{2,1,0:T(8,128)(2,1)S(1)}, u32[]{:S(2)}, u32[]{:S(2)}) collective-permute-start(bf16[2,368,512]{2,1,0:T(8,128)(2,1)S(1)} %copy-done.16), channel_id=1, source_target_pairs={{0,4},{1,3},{2,6},{3,1},{4,0},{5,7},{6,2},{7,5},{8,12},{9,11},{10,... | collective-permute-start | bytes 2261000 | tf_op jit(solution)/shard_map/ppermute | solution.py:463
  529.7 16.0 %collective-permute-start.104 = (bf16[1,368,512]{2,1,0:T(8,128)(2,1)S(1)}, bf16[1,368,512]{2,1,0:T(8,128)(2,1)S(1)}, u32[]{:S(2)}, u32[]{:S(2)}) collective-permute-start(bf16[1,368,512]{2,1,0:T(8,128)(2,1)S(1)} %get-tuple-element.129), channel_id=1, source_target_pairs={{0,4},{1,3},{2,6},{3,1},{4,0},{5,7},{6,2},{7,5},{8,12},{9,11},{10,... | collective-permute-start | bytes 1130504 | tf_op jit(solution)/shard_map/ppermute | solution.py:463
  543.8 7.7 %collective-permute-start.100 = (bf16[1,368,512]{2,1,0:T(8,128)(2,1)S(1)}, bf16[1,368,512]{2,1,0:T(8,128)(2,1)S(1)}, u32[]{:S(2)}, u32[]{:S(2)}) collective-permute-start(bf16[1,368,512]{2,1,0:T(8,128)(2,1)S(1)} %get-tuple-element.125), channel_id=1, source_target_pairs={{0,4},{1,3},{2,6},{3,1},{4,0},{5,7},{6,2},{7,5},{8,12},{9,11},{10,... | collective-permute-start | bytes 1130504 | tf_op jit(solution)/shard_map/ppermute | solution.py:463
  545.2 16.6 %collective-permute-start.108 = (bf16[1,368,512]{2,1,0:T(8,128)(2,1)S(1)}, bf16[1,368,512]{2,1,0:T(8,128)(2,1)S(1)}, u32[]{:S(2)}, u32[]{:S(2)}) collective-permute-start(bf16[1,368,512]{2,1,0:T(8,128)(2,1)S(1)} %get-tuple-element.133), channel_id=1, source_target_pairs={{0,8},{1,9},{2,10},{3,11},{4,12},{5,13},{6,14},{7,15},{8,0},{9,1},... | collective-permute-start | bytes 1130504 | tf_op jit(solution)/shard_map/ppermute | solution.py:463
  545.8 17.4 %collective-permute-start.105 = (bf16[1,368,512]{2,1,0:T(8,128)(2,1)S(1)}, bf16[1,368,512]{2,1,0:T(8,128)(2,1)S(1)}, u32[]{:S(2)}, u32[]{:S(2)}) collective-permute-start(bf16[1,368,512]{2,1,0:T(8,128)(2,1)S(1)} %add_convert_fusion.2), channel_id=1, source_target_pairs={{0,8},{2,10},{4,12},{6,14},{16,24},{17,1},{18,26},{19,3},{20,28},{... | collective-permute-start | bytes 1130504 | tf_op jit(solution)/shard_map/ppermute | solution.py:463
  551.6 14.8 %collective-permute-start.101 = (bf16[1,368,512]{2,1,0:T(8,128)(2,1)S(1)}, bf16[1,368,512]{2,1,0:T(8,128)(2,1)S(1)}, u32[]{:S(2)}, u32[]{:S(2)}) collective-permute-start(bf16[1,368,512]{2,1,0:T(8,128)(2,1)S(1)} %add_convert_fusion.4), channel_id=1, source_target_pairs={{8,0},{10,2},{12,4},{14,6},{17,1},{19,3},{21,5},{23,7},{24,16},{25... | collective-permute-start | bytes 1130504 | tf_op jit(solution)/shard_map/ppermute | solution.py:463
  561.9 11.7 %collective-permute-start.109 = (bf16[1,368,512]{2,1,0:T(8,128)(2,1)S(1)}, bf16[1,368,512]{2,1,0:T(8,128)(2,1)S(1)}, u32[]{:S(2)}, u32[]{:S(2)}) collective-permute-start(bf16[1,368,512]{2,1,0:T(8,128)(2,1)S(1)} %add_convert_fusion), channel_id=1, source_target_pairs={{0,16},{1,17},{2,18},{3,19},{4,20},{5,21},{6,22},{7,23},{8,24},{9,... | collective-permute-start | bytes 1130504 | tf_op jit(solution)/shard_map/ppermute | solution.py:463
  563.3 10.3 %collective-permute-start.106 = (bf16[1,368,512]{2,1,0:T(8,128)(2,1)S(1)}, bf16[1,368,512]{2,1,0:T(8,128)(2,1)S(1)}, u32[]{:S(2)}, u32[]{:S(2)}) collective-permute-start(bf16[1,368,512]{2,1,0:T(8,128)(2,1)S(1)} %add_convert_fusion.1), channel_id=1, source_target_pairs={{1,9},{3,11},{5,13},{7,15},{24,8},{26,10},{28,12},{30,14}} | collective-permute-start | bytes 1130504 | tf_op jit(solution)/shard_map/ppermute | solution.py:463
  566.5 10.5 %collective-permute-start.102 = (bf16[1,368,512]{2,1,0:T(8,128)(2,1)S(1)}, bf16[1,368,512]{2,1,0:T(8,128)(2,1)S(1)}, u32[]{:S(2)}, u32[]{:S(2)}) collective-permute-start(bf16[1,368,512]{2,1,0:T(8,128)(2,1)S(1)} %add_convert_fusion.3), channel_id=1, source_target_pairs={{9,1},{11,3},{13,5},{15,7},{16,0},{18,2},{20,4},{22,6}} | collective-permute-start | bytes 1130504 | tf_op jit(solution)/shard_map/ppermute | solution.py:463
  (167 other events, 977.8 us)
Sparse Core Ops, SparseCore 0:
  11.4 96.4 all-gather.3
  111.4 78.8 all-gather.5
  193.6 83.9 all-gather.7

commit v3 on v2

--- a/solution.py
+++ b/solution.py
@@ -46,16 +46,27 @@
     return bit_groups_of(device_count())
 
 
-def all_sum(values, groups=(), held=None):
+def arrive(groups, values):
+    values, arrivals = tied(values, [group.incoming for group in groups])
+    for group, incoming in zip(groups, arrivals):
+        group.incoming = incoming
+    return values
+
+
+def all_sum(values, groups=(), held=None, gate=None):
     stages = bit_groups()
     for stage, masks in enumerate(stages):
+        if stage == 1 and gate is not None:
+            _, gate = tied(values, gate)
         if stage == len(stages) - 1 and held is not None:
             values, held = step(groups, (values, held))
         others = [swap(values, mask) for mask in masks]
         values = values + others[0]
         if len(others) == 3:
             values = values + (others[1] + others[2])
-    return values if held is None else (values, held)
+    if held is None and gate is None:
+        return values
+    return (values, gate) if held is None else (values, held)
 
 
 def gather_blocks(values):
@@ -132,7 +143,7 @@
     fetch_embed().start()
 
     for i in range(count):
-        block = gathered[place_of(device[0], i, count)]
+        block = gathered[place_of(device[0], i, count)].astype(F32)
         pooled[i * views_dev : (i + 1) * views_dev, :] = block[:, :C_OUT]
         partners[i * views_dev : (i + 1) * views_dev, :] = block[:, C_OUT:]
     flush(pooled, pooled_out, 0).start()
@@ -143,7 +154,7 @@
 
     def cut(n, carry):
         cols = pl.ds(pl.multiple_of(n * tile, tile), tile)
-        terms[:total, cols], terms[total:, cols] = halves(pooled[:, cols])
+        terms[:, cols] = pooled[:, cols].astype(BF16)
         return carry
 
     lax.fori_loop(0, tiles, cut, 0)
@@ -170,8 +181,7 @@
 
     def forward(n, carry):
         cols = pl.ds(pl.multiple_of(n * tile, tile), tile)
-        product = jnp.dot(terms[...], weights[:, cols], preferred_element_type=F32)
-        raw = product[:total] + product[total:]
+        raw = jnp.dot(terms[...], weights[:, cols], preferred_element_type=F32)
         center = jnp.sum(raw, axis=0, keepdims=True) / total
         spread = jnp.sum(raw * raw, axis=0, keepdims=True) / total - center * center
         scale = lax.rsqrt(spread + EPSILON)
@@ -208,7 +218,8 @@
     highest = jnp.max(scores, axis=1, keepdims=True)
     log_total = highest + jnp.log(jnp.sum(jnp.exp(scores - highest), axis=1, keepdims=True))
     chances = jnp.where(valid, jnp.exp(scores - log_total), 0.0)
-    match = (along == partners[:, 0:1].astype(jnp.int32)) & valid
+    partner = (partners[:, 0:1] * 64.0 + partners[:, 1:2]).astype(jnp.int32)
+    match = (along == partner) & valid
     loss = log_total - jnp.sum(jnp.where(match, scores, 0.0), axis=1, keepdims=True)
     losses[...] = jnp.broadcast_to(loss, losses.shape)
     near = chances - 2.0 * match.astype(F32)
@@ -301,7 +312,7 @@
             pltpu.VMEM((total, HEAD), F32),
             pltpu.VMEM((total, HEAD), F32),
             pltpu.VMEM((size, width - C_OUT), F32),
-            pltpu.VMEM((2 * total, C_OUT), BF16),
+            pltpu.VMEM((total, C_OUT), BF16),
             pltpu.VMEM((total, HEAD), F32),
             pltpu.VMEM((total, HEAD), F32),
             pltpu.VMEM((1, HEAD), F32),
@@ -486,30 +497,51 @@
     return order
 
 
-def unflatten_kernel(order, source, target):
-    for at in range(0, target.shape[0], 64):
-        sorted_rows = jnp.dot(
-            order[...], source[4 * at : 4 * at + 256, :], preferred_element_type=F32
+def unflatten_kernel(order, flat, target, rows_in, sems, *, first):
+    tiles, rows = rows_in.shape[:2]
+
+    def fetch(n):
+        return pltpu.make_async_copy(
+            flat.at[pl.ds(pl.multiple_of(first + n * rows, 256), rows), :], rows_in.at[n], sems.at[n]
         )
-        for part in range(4):
-            target[at : at + 64, part * C_MID : (part + 1) * C_MID] = sorted_rows[
-                64 * part : 64 * part + 64, :
-            ].astype(BF16)
+
+    for n in range(tiles):
+        fetch(n).start()
+
+    def sort_rows(n, carry):
+        fetch(n).wait()
+        for at in range(0, rows // 4, 64):
+            sorted_rows = jnp.dot(
+                order[...], rows_in[n, 4 * at : 4 * at + 256, :], preferred_element_type=F32
+            )
+            for part in range(4):
+                target[
+                    pl.ds(pl.multiple_of(n * (rows // 4) + at, 64), 64),
+                    part * C_MID : (part + 1) * C_MID,
+                ] = sorted_rows[64 * part : 64 * part + 64, :].astype(BF16)
+        return carry
+
+    lax.fori_loop(0, tiles, sort_rows, 0)
 
 
 def unflatten(flat, first, rows):
-    tile = 256
-    while first % (4 * tile):
-        tile //= 2
+    tile = 128
+
+    def kernel(*refs):
+        unflatten_kernel(*refs, first=first)
+
     return pl.pallas_call(
-        unflatten_kernel,
+        kernel,
         out_shape=jax.ShapeDtypeStruct((rows, 4 * C_MID), BF16),
-        grid=(rows // tile,),
         in_specs=[
-            pl.BlockSpec((256, 256), lambda i: (0, 0)),
-            pl.BlockSpec((4 * tile, C_MID), lambda i: (first // (4 * tile) + i, 0)),
+            pl.BlockSpec(memory_space=pltpu.VMEM),
+            pl.BlockSpec(memory_space=pltpu.HBM),
         ],
-        out_specs=pl.BlockSpec((tile, 4 * C_MID), lambda i: (i, 0)),
+        out_specs=pl.BlockSpec(memory_space=pltpu.VMEM),
+        scratch_shapes=[
+            pltpu.VMEM((rows // tile, 4 * tile, C_MID), BF16),
+            pltpu.SemaphoreType.DMA((rows // tile,)),
+        ],
         compiler_params=pltpu.CompilerParams(vmem_limit_bytes=24 << 20),
         cost_estimate=pl.CostEstimate(
             flops=2048 * rows * C_MID, bytes_accessed=16 * rows * C_MID, transcendentals=0
@@ -767,6 +799,20 @@
     )(cotan, kernel, strided)
 
 
+def silu_moments(mean, spread):
+    nodes, weights = np.polynomial.hermite_e.hermegauss(5)
+    weights = weights / weights.sum()
+    values = [jax.nn.silu(mean + float(node) * jnp.sqrt(spread)) for node in nodes]
+    first = sum(float(weight) * value for weight, value in zip(weights, values))
+    second = sum(float(weight) * value * value for weight, value in zip(weights, values))
+    return first, jnp.maximum(second - first * first, 0.0)
+
+
+def pooled_center(main, short, last):
+    joined, spread = silu_moments(main[1] + short[1], main[0] * main[0] + short[0] * short[0])
+    return silu_moments(last[1] + joined, last[0] * last[0] + spread)[0]
+
+
 def unit_norm(embed):
     return embed * lax.rsqrt(jnp.sum(embed * embed, axis=1, keepdims=True) + NORM_EPS)
 
@@ -871,22 +917,24 @@
     w_narrow = second[:2048]
     w_middle = second[2048:6656]
     raw_five = times(result_one, w_narrow)
-    w_widen = unflatten(second, 6656, C_MID)
-    sums, w_widen = tied(all_sum(moments(raw_five)), w_widen)
-    norm_five = Norm(raw_five, sums, norms[4], rows)
+    norm_five = Norm(raw_five, all_sum(moments(raw_five)), norms[4], rows)
     act_three = jax.nn.silu(norm_five.shifted()).astype(BF16)
     raw_six = conv(act_three, w_middle, 1)
-    norm_six = Norm(raw_six, all_sum(moments(raw_six)), norms[5], rows)
+    w_widen = unflatten(second, 6656, C_MID)
+    sums, w_widen = tied(all_sum(moments(raw_six)), w_widen)
+    norm_six = Norm(raw_six, sums, norms[5], rows)
     act_four = jax.nn.silu(norm_six.shifted()).astype(BF16)
     raw_seven = times(act_four, w_widen)
     norm_seven = Norm(raw_seven, all_sum(moments(raw_seven)), norms[6], rows)
     joined_two = norm_seven.shifted() + result_one.astype(F32)
     pooled_own = jnp.mean(jax.nn.silu(joined_two), axis=(1, 2))
 
+    center = pooled_center(norms[2], norms[3], norms[6])
+    digits = jnp.stack([partner // 64, partner % 64], axis=1).astype(F32)
     gathered = gather_blocks(
         jnp.concatenate(
-            [pooled_own, jnp.broadcast_to(partner.astype(F32)[:, None], (views_dev, EMBED))], axis=1
-        )
+            [pooled_own - center, jnp.pad(digits, ((0, 0), (0, EMBED - 2)))], axis=1
+        ).astype(BF16)
     )
     if total_views <= 256:
         pooled, hidden, raw_hidden_cot, embed_cot, grads_head, losses, pooled_cot = head_pass(
@@ -898,8 +946,8 @@
         w_hidden = unflatten(head, 0, C_OUT)
         w_embed = head[4 * C_OUT :].reshape(HEAD, EMBED)
         order = jnp.stack([place_of(device, i, count) for i in range(count)])
-        pooled = jnp.take(gathered, order, axis=0).reshape(total_views, -1)
-        partners = pooled[:, C_OUT].astype(jnp.int32)
+        pooled = jnp.take(gathered, order, axis=0).reshape(total_views, -1).astype(F32)
+        partners = (pooled[:, C_OUT] * 64.0 + pooled[:, C_OUT + 1]).astype(jnp.int32)
         pooled = pooled[:, :C_OUT]
         raw_hidden = exact_times(pooled, w_hidden, 0)
         norm_head = Norm(raw_hidden, moments(raw_hidden), norms[7], total_views)
@@ -916,9 +964,8 @@
         pooled_cot = exact_times(own_cot, w_hidden, 1)
 
     joined_cot = (pooled_cot / (half * half))[:, None, None, :] * silu_slope(joined_two)
-    head_out = head_kernel_grads(pooled, raw_hidden_cot, hidden, embed_cot, head_params.shape[0])
     loss = lax.dynamic_slice_in_dim(losses, device * views_dev, views_dev)
-    grads_seven, head_out, loss = tied(all_sum(norm_seven.partial_grads(joined_cot)), head_out, loss)
+    grads_seven, loss = tied(all_sum(norm_seven.partial_grads(joined_cot)), loss)
     low_seven = norm_seven.pull(joined_cot, grads_seven).astype(BF16)
     act_four_cot = times_back(low_seven, w_widen) * silu_slope(norm_six.shifted())
     second_grad = grad_into(second.shape[0], 6656, cell_rows(act_four, 8), cell_rows(low_seven, 8))
@@ -956,14 +1003,19 @@
         low_short.reshape(-1, C_OUT),
         first_grad,
     )
+    grads_two = step([sum_second], norm_two.partial_grads(act_two_cot))
+    grads_two, (head_rows, low_short) = all_sum(
+        grads_two, gate=((pooled, raw_hidden_cot, hidden, embed_cot), low_short)
+    )
+    head_out = head_kernel_grads(*head_rows, head_params.shape[0])
     strided_cot = times_back(low_short, w_short)
-    grads_two = step([sum_second], norm_two.partial_grads(act_two_cot))
-    grads_two = all_sum(grads_two)
     first_shape = (count, first.shape[0] // count, C_MID)
     first_blocks = first_grad.reshape(first_shape)
     part = count // 4
     late = ScatterSum(first_blocks, 2 * part, 2 * part)
-    grads_two, first_grad = step([sum_second, late], (grads_two, first_grad))
+    grads_two, first_grad, head_out, strided_cot = step(
+        [sum_second, late], (grads_two, first_grad, head_out, strided_cot)
+    )
     low_two = norm_two.pull(act_two_cot, grads_two).astype(BF16)
     act_one_cot = conv_back(low_two, w_spatial, 2)
     act_one_cot, first_grad = step([late], (act_one_cot, first_grad))
@@ -972,17 +1024,20 @@
         [sum_second], (norm_one.partial_grads(act_one_cot), first_grad)
     )
     grads_one = all_sum(grads_one)
-    first_grad = placed(first_grad, 1024, conv_kernel_grad(act_one, low_two, 2))
-    first_blocks = first_grad.reshape(first_shape)
-    early = ScatterSum(first_blocks, part, part)
-    grads_one, first_grad = step([early, late, sum_second], (grads_one, first_grad))
+    grad_spatial = conv_kernel_grad(act_one, low_two, 2).astype(BF16)
+    early_rows = part * first_shape[1]
+    first_grad = placed(first_grad, early_rows, grad_spatial[early_rows - 1024 :])
+    last_grad = jnp.pad(grad_spatial[: early_rows - 1024], ((1024, 0), (0, 0)))
+    early = ScatterSum(first_grad.reshape(first_shape), part, part)
+    grads_one, first_grad, last_grad = step(
+        [early, late, sum_second], (grads_one, first_grad, last_grad)
+    )
     low_one = pad_side(norm_one.pull(act_one_cot, grads_one).astype(BF16), 16)
-    first_grad = grad_into(
-        first.shape[0], 0, full_views, low_one.reshape(-1, C_MID), first_grad
-    )
-    last = ScatterSum(first_grad.reshape(first_shape), 0, part)
-    early.source = last.source
-    low_one = step([early, last], low_one)
+    low_one = step([early], low_one)
+    last_grad = grad_into(early_rows, 0, full_views, low_one.reshape(-1, C_MID), last_grad)
+    last_grad = arrive([late], last_grad)
+    last = ScatterSum(last_grad.reshape(part, *first_shape[1:]), 0, part)
+    low_one = step([last], low_one)
     views_cot = input_grad(low_one, w_reduce, strided_cot)
     groups = [early, last, late, sum_second]
     while any(not group.done() for group in groups):

time: 595 us -> 568 us (0.955)
  waiting for transfers between devices: 253 us -> 216 us
    ppermute x91, waiting for transfers between devices: 91.5 us -> 60.7 us  [swap(): lax.ppermute(values, BOTH, [(i, i ^ mask) for i in range(device_count())])]
    pallas_call x11, Pallas kernels: 4.89 us -> 11.2 us  [add_blocks(): pl.pallas_call(add_kernel, out_shape=[shape] * ways, grid_spec=pltpu.Pref...]
    unnamed x215 -> x237, local copies, waits for them, and re-layouts: 22.5 us -> 17.1 us
  transfers between devices with their start and end apart: 114 -> 114, of which waited for: 54 -> 64; matrix products, arithmetic and copies ran while one was open for 15% -> 18% of each run, Pallas kernels for 5% -> 5%
where the time goes in v3:
time: 568 us; the launch traced here: 558 us
  waiting for transfers between devices  216 us (38%)
  starting transfers between devices  127 us (22%)
  matrix products  62.5 us (11%)
  Pallas kernels  60.5 us (11%)
  local copies, waits for them, and re-layouts  46.6 us (8%)
  other arithmetic  28.7 us (5%)
  between operations  16.5 us (3%)
    all_gather x3, waiting for transfers between devices, gather(): return lax.all_gather(flat.reshape(-1, C_MID), BOTH, axis=0, tiled=True)  107 us
    ppermute x91, starting transfers between devices, swap(): lax.ppermute(values, BOTH, [(i, i ^ mask) for i in range(device_count())])  106 us
    ppermute x91, waiting for transfers between devices, swap(): lax.ppermute(values, BOTH, [(i, i ^ mask) for i in range(device_count())])  60.7 us
    ppermute x20, waiting for transfers between devices, send(): self.incoming = lax.ppermute(outgoing, BOTH, pairs)  48.2 us
    ppermute x20, starting transfers between devices, send(): self.incoming = lax.ppermute(outgoing, BOTH, pairs)  21.4 us
    pallas_call x1, Pallas kernels, head_pass(): pl.pallas_call(head_kernel, out_shape=[shape((total, C_OUT), F32), shape(...  21.1 us
    unnamed x237, local copies, waits for them, and re-layouts  17.1 us
    dot_general x4, matrix products, times_back(): lax.dot_general(cotan, kernel, (((cotan.ndim - 1,), (1,)), ((), ())), pre...  15.6 us
  transfers between devices with their start and end apart: 114, of which 64 were waited for; matrix products, arithmetic and copies ran while one was open for 18% of the time, Pallas kernels for 5%

profile of v3, /device:TPU:0, one launch (start us, length us, event | category | flops | bytes accessed | tf_op | source)
XLA Modules:
  0.0 557.8 jit_solution(1474082654725165520)
XLA Ops:
  16.8 91.1 %all-gather.4.cloned.1.call-done.refs_1_ = bf16[11776,512]{1,0:T(8,128)(2,1)} async-done(((bf16[368,512]{1,0:T(8,128)(2,1)}), bf16[11776,512]{1,0:T(8,128)(2,1)}) %all-gather.4.cloned.1.call-update) | async-done | bytes 12058640 | tf_op jit(solution)/shard_map/all_gather | solution.py:884
  108.0 4.5 fusion.73
  126.1 2.8 slice.215
  130.8 4.5 fusion.75
  135.4 2.8 shard_map.147
  146.0 2.8 collective-permute-start.11
  158.8 2.5 collective-permute-done.17
  168.9 3.2 collective-permute-done.19
  172.2 2.4 multiply_convert_fusion.3
  174.6 15.7 %all-gather.6.cloned.1.call-done.refs_1_ = bf16[8704,512]{1,0:T(8,128)(2,1)} async-done(((bf16[272,512]{1,0:T(8,128)(2,1)}), bf16[8704,512]{1,0:T(8,128)(2,1)}) %all-gather.6.cloned.1.call-update) | async-done | bytes 8912912 | tf_op jit(solution)/shard_map/all_gather | solution.py:884
  190.3 3.5 fusion.76
  198.8 2.6 collective-permute-done.24
  206.0 2.7 slice.272
  209.5 3.2 fusion.74
  227.9 3.0 fusion.70
  236.0 2.4 collective-permute-done.38
  246.0 3.5 multiply_reduce_fusion.3
  257.0 2.9 collective-permute-done.44
  273.3 21.1 %shard_map.149 = (f32[192,2048]{1,0:T(8,128)}, f32[192,2048]{1,0:T(8,128)}, f32[192,2048]{1,0:T(8,128)}, f32[192,128]{1,0:T(8,128)S(1)}, f32[2,2048]{1,0:T(2,128...) custom-call(s32[1]{0:T(128)} %bitcast.device, bf16[32,6,2176]{2,1,0:T(8,128)(2,1)} %copy_dynamic-update-slice_fusion.gathered, ...), custom_call_target="tpu_custom_call" | custom-call | flops 3221225472 | bytes 20971520 | tf_op jit(solution)/shard_map/pallas_call | solution.py:293
  294.4 3.4 multiply_reduce_fusion.2
  312.9 3.4 multiply_convert_fusion.2
  316.4 2.7 multiply_reduce_fusion.10
  333.1 3.4 multiply_reduce_fusion.9
  341.3 4.1 convolution_convert_fusion.1
  353.4 6.6 %multiply_reduce_fusion.1 = (f32[2048]{0:T(1024)S(1)}, f32[2048]{0:T(1024)S(1)}, f32[2048]{0:T(1024)S(1)}, f32[6,7,7,2048]{3,2,1,0:T(8,128)}) fusion(f32[6,7,7,2048]{3,2,1,0:T(8,128)S(1)} %copy-done.32, f32[2048]{0:T(1024)S(1)} %get-tuple-element.272, f32[2048]{0:T(1024)S(1)} %bitcast.250, f32[2048]{0:T(1024)S(1)} %get-tuple-element.227, ...), kind=kOutput, calls=%fused_computation.24 | convolution fusion | flops 630405120 | bytes 12122112 | tf_op jit(solution)/shard_map/dot_general | solution.py:661
  364.9 2.8 shard_map.151
  376.2 4.1 multiply_convert_fusion
  380.3 3.6 multiply_reduce_fusion.8
  383.9 3.5 shard_map.153
  394.4 4.6 shard_map.155
  399.3 5.2 copy-done
  408.1 2.7 fusion.1.strided
  412.9 2.8 collective-permute-done.81
  420.1 4.3 fusion
  424.5 3.4 shard_map.156
  429.4 5.3 fusion.79
  434.8 8.8 %collective-permute-done.87.refs_1_.refs_3_ = bf16[4,272,512]{2,1,0:T(8,128)(2,1)S(1)} collective-permute-done((bf16[4,272,512]{2,1,0:T(8,128)(2,1)S(1)}, bf16[4,272,512]{2,1,0:T(8,128)(2,1)S(1)}, u32[]{:S(2)}, u32[]{:S(2)}) %collective-permute-start.87) | collective-permute-done | bytes 1114144 | tf_op jit(solution)/shard_map/ppermute | solution.py:474
  452.6 6.2 %convolution_convert_fusion = bf16[3,3,512,512]{3,2,1,0:T(8,128)(2,1)} fusion(bf16[6,7,7,512]{3,0,2,1:T(8,128)(2,1)S(1)} %multiply_convert_fusion.5, bf16[6,14,14,512]{3,2,1,0:T(8,128)(2,1)S(1)} %copy-done.45), kind=kOutput, calls=%fused_computation.9 | convolution fusion | flops 1260650496 | bytes 6223872 | tf_op jit(solution)/shard_map/conv_general_dilated | solution.py:703
  461.2 7.2 %collective-permute-done.91 = f32[2,512]{1,0:T(2,128)S(1)} collective-permute-done((f32[2,512]{1,0:T(2,128)S(1)}, f32[2,512]{1,0:T(2,128)S(1)}, u32[]{:S(2)}, u32[]{:S(2)}) %collective-permute-start.91) | collective-permute-done | bytes 4128 | tf_op jit(solution)/shard_map/ppermute | solution.py:30
  470.4 2.5 collective-permute-start.92
  480.9 2.9 shard_map.164
  483.9 4.3 collective-permute-done.98.refs_1_.refs_3_
  498.4 4.5 collective-permute-done.104.refs_1_.refs_3_
  504.2 10.8 %collective-permute-done.100.refs_1_.refs_3_ = bf16[2,368,512]{2,1,0:T(8,128)(2,1)S(1)} collective-permute-done((bf16[2,368,512]{2,1,0:T(8,128)(2,1)S(1)}, bf16[2,368,512]{2,1,0:T(8,128)(2,1)S(1)}, u32[]{:S(2)}, u32[]{:S(2)}) %collective-permute-start.100) | collective-permute-done | bytes 753696 | tf_op jit(solution)/shard_map/ppermute | solution.py:474
  517.9 2.7 collective-permute-start.106
  524.2 10.2 %collective-permute-done.108 = bf16[1,368,512]{2,1,0:T(8,128)(2,1)S(1)} collective-permute-done((bf16[1,368,512]{2,1,0:T(8,128)(2,1)S(1)}, bf16[1,368,512]{2,1,0:T(8,128)(2,1)S(1)}, u32[]{:S(2)}, u32[]{:S(2)}) %collective-permute-start.108) | collective-permute-done | bytes 376864 | tf_op jit(solution)/shard_map/ppermute | solution.py:474
  541.3 4.8 shard_map.166
  546.1 3.4 collective-permute-done.103
  (595 shorter events, 229.8 us)
Async XLA Ops:
  7.2 100.8 %all-gather.4.cloned.1.call-start = ((), (), s32[]{:S(2)}) async-start(), calls=%async_computation | async-start | bytes 12435456 | tf_op jit(solution)/shard_map/all_gather | solution.py:884
  9.2 181.1 %all-gather.6.cloned.1.call-start = ((), (), s32[]{:S(2)}) async-start(), calls=%async_computation.1 | async-start | bytes 9191424 | tf_op jit(solution)/shard_map/all_gather | solution.py:884
  11.1 262.2 %all-gather.8.cloned.1.call-start = ((), (), s32[]{:S(2)}) async-start(), calls=%async_computation.2 | async-start | bytes 9191424 | tf_op jit(solution)/shard_map/all_gather | solution.py:884
  120.1 8.8 %collective-permute-start.6 = (f32[2,512]{1,0:T(2,128)S(1)}, f32[2,512]{1,0:T(2,128)S(1)}, u32[]{:S(2)}, u32[]{:S(2)}) collective-permute-start(f32[2,512]{1,0:T(2,128)S(1)} %add_add_fusion.24), channel_id=1, source_target_pairs={{0,24},{1,25},{2,26},{3,27},{4,28},{5,29},{6,30},{7,31},{8,16},{9,... | collective-permute-start | bytes 12296 | tf_op jit(solution)/shard_map/ppermute | solution.py:30
  121.8 7.1 %collective-permute-start.5 = (f32[2,512]{1,0:T(2,128)S(1)}, f32[2,512]{1,0:T(2,128)S(1)}, u32[]{:S(2)}, u32[]{:S(2)}) collective-permute-start(f32[2,512]{1,0:T(2,128)S(1)} %add_add_fusion.24), channel_id=1, source_target_pairs={{0,16},{1,17},{2,18},{3,19},{4,20},{5,21},{6,22},{7,23},{8,24},{9,... | collective-permute-start | bytes 12296 | tf_op jit(solution)/shard_map/ppermute | solution.py:30
  122.7 6.2 %collective-permute-start.4 = (f32[2,512]{1,0:T(2,128)S(1)}, f32[2,512]{1,0:T(2,128)S(1)}, u32[]{:S(2)}, u32[]{:S(2)}) collective-permute-start(f32[2,512]{1,0:T(2,128)S(1)} %add_add_fusion.24), channel_id=1, source_target_pairs={{0,8},{1,9},{2,10},{3,11},{4,12},{5,13},{6,14},{7,15},{8,0},{9,1},... | collective-permute-start | bytes 12296 | tf_op jit(solution)/shard_map/ppermute | solution.py:30
  144.3 6.0 %collective-permute-start.13 = (f32[2,512]{1,0:T(2,128)S(1)}, f32[2,512]{1,0:T(2,128)S(1)}, u32[]{:S(2)}, u32[]{:S(2)}) collective-permute-start(f32[2,512]{1,0:T(2,128)S(1)} %add_add_fusion.22), channel_id=1, source_target_pairs={{0,24},{1,25},{2,26},{3,27},{4,28},{5,29},{6,30},{7,31},{8,16},{9,... | collective-permute-start | bytes 12296 | tf_op jit(solution)/shard_map/ppermute | solution.py:30
  162.1 6.8 %collective-permute-start.20 = (f32[4,2048]{1,0:T(4,128)S(1)}, f32[4,2048]{1,0:T(4,128)S(1)}, u32[]{:S(2)}, u32[]{:S(2)}) collective-permute-start(f32[4,2048]{1,0:T(4,128)S(1)} %add_add_fusion.4), channel_id=1, source_target_pairs={{0,24},{1,25},{2,26},{3,27},{4,28},{5,29},{6,30},{7,31},{8,16},{9,... | collective-permute-start | bytes 98312 | tf_op jit(solution)/shard_map/ppermute | solution.py:30
  164.4 7.7 %collective-permute-start.19 = (f32[4,2048]{1,0:T(4,128)S(1)}, f32[4,2048]{1,0:T(4,128)S(1)}, u32[]{:S(2)}, u32[]{:S(2)}) collective-permute-start(f32[4,2048]{1,0:T(4,128)S(1)} %add_add_fusion.4), channel_id=1, source_target_pairs={{0,16},{1,17},{2,18},{3,19},{4,20},{5,21},{6,22},{7,23},{8,24},{9,... | collective-permute-start | bytes 98312 | tf_op jit(solution)/shard_map/ppermute | solution.py:30
  165.4 6.7 %collective-permute-start.18 = (f32[4,2048]{1,0:T(4,128)S(1)}, f32[4,2048]{1,0:T(4,128)S(1)}, u32[]{:S(2)}, u32[]{:S(2)}) collective-permute-start(f32[4,2048]{1,0:T(4,128)S(1)} %add_add_fusion.4), channel_id=1, source_target_pairs={{0,8},{1,9},{2,10},{3,11},{4,12},{5,13},{6,14},{7,15},{8,0},{9,1},... | collective-permute-start | bytes 98312 | tf_op jit(solution)/shard_map/ppermute | solution.py:30
  201.6 7.1 %collective-permute-start.27 = (f32[2,512]{1,0:T(2,128)S(1)}, f32[2,512]{1,0:T(2,128)S(1)}, u32[]{:S(2)}, u32[]{:S(2)}) collective-permute-start(f32[2,512]{1,0:T(2,128)S(1)} %add_add_fusion.20), channel_id=1, source_target_pairs={{0,24},{1,25},{2,26},{3,27},{4,28},{5,29},{6,30},{7,31},{8,16},{9,... | collective-permute-start | bytes 12296 | tf_op jit(solution)/shard_map/ppermute | solution.py:30
  220.1 6.1 %collective-permute-start.34 = (f32[2,512]{1,0:T(2,128)S(1)}, f32[2,512]{1,0:T(2,128)S(1)}, u32[]{:S(2)}, u32[]{:S(2)}) collective-permute-start(f32[2,512]{1,0:T(2,128)S(1)} %add_add_fusion.18), channel_id=1, source_target_pairs={{0,24},{1,25},{2,26},{3,27},{4,28},{5,29},{6,30},{7,31},{8,16},{9,... | collective-permute-start | bytes 12296 | tf_op jit(solution)/shard_map/ppermute | solution.py:30
  250.2 6.4 %collective-permute-start.43 = (bf16[1,6,2176]{2,1,0:T(8,128)(2,1)S(1)}, bf16[1,6,2176]{2,1,0:T(8,128)(2,1)S(1)}, u32[]{:S(2)}, u32[]{:S(2)}) collective-permute-start(bf16[1,6,2176]{2,1,0:T(8,128)(2,1)S(1)} %get-tuple-element.216), channel_id=1, source_target_pairs={{0,16},{1,17},{2,18},{3,19},{4,20},{5,21},{6,22},{7,23},{8,24},{9,... | collective-permute-start | bytes 78344 | tf_op jit(solution)/shard_map/ppermute | solution.py:30
  253.4 6.5 %collective-permute-start.44 = (bf16[1,6,2176]{2,1,0:T(8,128)(2,1)S(1)}, bf16[1,6,2176]{2,1,0:T(8,128)(2,1)S(1)}, u32[]{:S(2)}, u32[]{:S(2)}) collective-permute-start(bf16[1,6,2176]{2,1,0:T(8,128)(2,1)S(1)} %get-tuple-element.216), channel_id=1, source_target_pairs={{0,24},{1,25},{2,26},{3,27},{4,28},{5,29},{6,30},{7,31},{8,16},{9,... | collective-permute-start | bytes 78344 | tf_op jit(solution)/shard_map/ppermute | solution.py:30
  259.9 8.9 %collective-permute-start.47 = (bf16[4,6,2176]{2,1,0:T(8,128)(2,1)S(1)}, bf16[4,6,2176]{2,1,0:T(8,128)(2,1)S(1)}, u32[]{:S(2)}, u32[]{:S(2)}) collective-permute-start(bf16[4,6,2176]{2,1,0:T(8,128)(2,1)S(1)} %pad_maximum_fusion), channel_id=1, source_target_pairs={{0,6},{1,7},{2,4},{3,5},{4,2},{5,3},{6,0},{7,1},{8,14},{9,15},{10,... | collective-permute-start | bytes 313352 | tf_op jit(solution)/shard_map/ppermute | solution.py:30
  260.6 7.6 %collective-permute-start.46 = (bf16[4,6,2176]{2,1,0:T(8,128)(2,1)S(1)}, bf16[4,6,2176]{2,1,0:T(8,128)(2,1)S(1)}, u32[]{:S(2)}, u32[]{:S(2)}) collective-permute-start(bf16[4,6,2176]{2,1,0:T(8,128)(2,1)S(1)} %pad_maximum_fusion), channel_id=1, source_target_pairs={{0,4},{1,5},{2,6},{3,7},{4,0},{5,1},{6,2},{7,3},{8,12},{9,13},{10,... | collective-permute-start | bytes 313352 | tf_op jit(solution)/shard_map/ppermute | solution.py:30
  325.9 6.8 %collective-permute-start.62 = (f32[2,512]{1,0:T(2,128)S(1)}, f32[2,512]{1,0:T(2,128)S(1)}, u32[]{:S(2)}, u32[]{:S(2)}) collective-permute-start(f32[2,512]{1,0:T(2,128)S(1)} %add_add_fusion.16), channel_id=1, source_target_pairs={{0,24},{1,25},{2,26},{3,27},{4,28},{5,29},{6,30},{7,31},{8,16},{9,... | collective-permute-start | bytes 12296 | tf_op jit(solution)/shard_map/ppermute | solution.py:30
  337.7 7.7 %collective-permute-start.65 = (f32[2,512]{1,0:T(2,128)S(1)}, f32[2,512]{1,0:T(2,128)S(1)}, u32[]{:S(2)}, u32[]{:S(2)}) collective-permute-start(f32[2,512]{1,0:T(2,128)S(1)} %fusion.58), channel_id=1, source_target_pairs={{0,4},{1,5},{2,6},{3,7},{4,0},{5,1},{6,2},{7,3},{8,12},{9,13},{10,... | collective-permute-start | bytes 12296 | tf_op jit(solution)/shard_map/ppermute | solution.py:30
  338.9 6.5 %collective-permute-start.66 = (f32[2,512]{1,0:T(2,128)S(1)}, f32[2,512]{1,0:T(2,128)S(1)}, u32[]{:S(2)}, u32[]{:S(2)}) collective-permute-start(f32[2,512]{1,0:T(2,128)S(1)} %fusion.58), channel_id=1, source_target_pairs={{0,6},{1,7},{2,4},{3,5},{4,2},{5,3},{6,0},{7,1},{8,14},{9,15},{10,... | collective-permute-start | bytes 12296 | tf_op jit(solution)/shard_map/ppermute | solution.py:30
  361.3 6.8 %collective-permute-start.72 = (f32[3,2048]{1,0:T(4,128)S(1)}, f32[3,2048]{1,0:T(4,128)S(1)}, u32[]{:S(2)}, u32[]{:S(2)}) collective-permute-start(f32[3,2048]{1,0:T(4,128)S(1)} %fusion.66), channel_id=1, source_target_pairs={{0,4},{1,5},{2,6},{3,7},{4,0},{5,1},{6,2},{7,3},{8,12},{9,13},{10,... | collective-permute-start | bytes 73736 | tf_op jit(solution)/shard_map/ppermute | solution.py:30
  368.4 15.6 %collective-permute-start.77 = (bf16[16,272,512]{2,1,0:T(8,128)(2,1)S(1)}, bf16[16,272,512]{2,1,0:T(8,128)(2,1)S(1)}, u32[]{:S(2)}, u32[]{:S(2)}) collective-permute-start(bf16[16,272,512]{2,1,0:T(8,128)(2,1)S(1)} %shard_map.152), channel_id=1, source_target_pairs={{0,1},{1,0},{2,3},{3,2},{4,5},{5,4},{6,7},{7,6},{8,9},{9,8},{10,11... | collective-permute-start | bytes 13369352 | tf_op jit(solution)/shard_map/ppermute | solution.py:474
  387.4 37.1 %collective-permute-start.85 = (bf16[8,272,512]{2,1,0:T(8,128)(2,1)}, bf16[8,272,512]{2,1,0:T(8,128)(2,1)}, u32[]{:S(2)}, u32[]{:S(2)}) collective-permute-start(bf16[8,272,512]{2,1,0:T(8,128)(2,1)} %get-tuple-element.110), channel_id=1, source_target_pairs={{0,2},{1,5},{2,0},{3,7},{4,6},{5,1},{6,4},{7,3},{8,10},{9,13},{10,... | collective-permute-start | bytes 6684680 | tf_op jit(solution)/shard_map/ppermute | solution.py:474
  394.3 10.2 %collective-permute-start.78 = (f32[2,512]{1,0:T(2,128)S(1)}, f32[2,512]{1,0:T(2,128)S(1)}, u32[]{:S(2)}, u32[]{:S(2)}) collective-permute-start(f32[2,512]{1,0:T(2,128)S(1)} %pad_maximum_fusion.12), channel_id=1, source_target_pairs={{0,1},{1,0},{2,3},{3,2},{4,5},{5,4},{6,7},{7,6},{8,9},{9,8},{10,11... | collective-permute-start | bytes 12296 | tf_op jit(solution)/shard_map/ppermute | solution.py:30
  404.6 11.1 %collective-permute-start.81 = (f32[2,512]{1,0:T(2,128)S(1)}, f32[2,512]{1,0:T(2,128)S(1)}, u32[]{:S(2)}, u32[]{:S(2)}) collective-permute-start(f32[2,512]{1,0:T(2,128)S(1)} %add.870), channel_id=1, source_target_pairs={{0,6},{1,7},{2,4},{3,5},{4,2},{5,3},{6,0},{7,1},{8,14},{9,15},{10,... | collective-permute-start | bytes 12296 | tf_op jit(solution)/shard_map/ppermute | solution.py:30
  405.7 9.9 %collective-permute-start.80 = (f32[2,512]{1,0:T(2,128)S(1)}, f32[2,512]{1,0:T(2,128)S(1)}, u32[]{:S(2)}, u32[]{:S(2)}) collective-permute-start(f32[2,512]{1,0:T(2,128)S(1)} %add.870), channel_id=1, source_target_pairs={{0,4},{1,5},{2,6},{3,7},{4,0},{5,1},{6,2},{7,3},{8,12},{9,13},{10,... | collective-permute-start | bytes 12296 | tf_op jit(solution)/shard_map/ppermute | solution.py:30
  406.7 8.9 %collective-permute-start.79 = (f32[2,512]{1,0:T(2,128)S(1)}, f32[2,512]{1,0:T(2,128)S(1)}, u32[]{:S(2)}, u32[]{:S(2)}) collective-permute-start(f32[2,512]{1,0:T(2,128)S(1)} %add.870), channel_id=1, source_target_pairs={{0,2},{1,3},{2,0},{3,1},{4,6},{5,7},{6,4},{7,5},{8,10},{9,11},{10,... | collective-permute-start | bytes 12296 | tf_op jit(solution)/shard_map/ppermute | solution.py:30
  415.7 8.8 %collective-permute-start.84 = (f32[2,512]{1,0:T(2,128)S(1)}, f32[2,512]{1,0:T(2,128)S(1)}, u32[]{:S(2)}, u32[]{:S(2)}) collective-permute-start(f32[2,512]{1,0:T(2,128)S(1)} %add_add_fusion.12), channel_id=1, source_target_pairs={{0,24},{1,25},{2,26},{3,27},{4,28},{5,29},{6,30},{7,31},{8,16},{9,... | collective-permute-start | bytes 12296 | tf_op jit(solution)/shard_map/ppermute | solution.py:30
  417.7 6.8 %collective-permute-start.83 = (f32[2,512]{1,0:T(2,128)S(1)}, f32[2,512]{1,0:T(2,128)S(1)}, u32[]{:S(2)}, u32[]{:S(2)}) collective-permute-start(f32[2,512]{1,0:T(2,128)S(1)} %add_add_fusion.12), channel_id=1, source_target_pairs={{0,16},{1,17},{2,18},{3,19},{4,20},{5,21},{6,22},{7,23},{8,24},{9,... | collective-permute-start | bytes 12296 | tf_op jit(solution)/shard_map/ppermute | solution.py:30
  428.0 16.0 %collective-permute-start.86 = (bf16[8,368,512]{2,1,0:T(8,128)(2,1)S(1)}, bf16[8,368,512]{2,1,0:T(8,128)(2,1)S(1)}, u32[]{:S(2)}, u32[]{:S(2)}) collective-permute-start(bf16[8,368,512]{2,1,0:T(8,128)(2,1)S(1)} %copy-done.15), channel_id=1, source_target_pairs={{0,1},{1,0},{2,3},{3,2},{4,5},{5,4},{6,7},{7,6},{8,9},{9,8},{10,11... | collective-permute-start | bytes 9043976 | tf_op jit(solution)/shard_map/ppermute | solution.py:474
  428.1 15.6 %collective-permute-start.87 = (bf16[4,272,512]{2,1,0:T(8,128)(2,1)S(1)}, bf16[4,272,512]{2,1,0:T(8,128)(2,1)S(1)}, u32[]{:S(2)}, u32[]{:S(2)}) collective-permute-start(bf16[4,272,512]{2,1,0:T(8,128)(2,1)S(1)} %get-tuple-element.119), channel_id=1, source_target_pairs={{0,4},{1,3},{2,6},{3,1},{4,0},{5,7},{6,2},{7,5},{8,12},{9,11},{10,... | collective-permute-start | bytes 3342344 | tf_op jit(solution)/shard_map/ppermute | solution.py:474
  448.0 28.0 %collective-permute-start.95 = (bf16[4,368,512]{2,1,0:T(8,128)(2,1)S(1)}, bf16[4,368,512]{2,1,0:T(8,128)(2,1)S(1)}, u32[]{:S(2)}, u32[]{:S(2)}) collective-permute-start(bf16[4,368,512]{2,1,0:T(8,128)(2,1)S(1)} %get-tuple-element.124), channel_id=1, source_target_pairs={{0,2},{1,5},{2,0},{3,7},{4,6},{5,1},{6,4},{7,3},{8,10},{9,13},{10,... | collective-permute-start | bytes 4521992 | tf_op jit(solution)/shard_map/ppermute | solution.py:474
  449.1 19.3 %collective-permute-start.91 = (f32[2,512]{1,0:T(2,128)S(1)}, f32[2,512]{1,0:T(2,128)S(1)}, u32[]{:S(2)}, u32[]{:S(2)}) collective-permute-start(f32[2,512]{1,0:T(2,128)S(1)} %add.882), channel_id=1, source_target_pairs={{0,6},{1,7},{2,4},{3,5},{4,2},{5,3},{6,0},{7,1},{8,14},{9,15},{10,... | collective-permute-start | bytes 12296 | tf_op jit(solution)/shard_map/ppermute | solution.py:30
  451.0 17.4 %collective-permute-start.90 = (f32[2,512]{1,0:T(2,128)S(1)}, f32[2,512]{1,0:T(2,128)S(1)}, u32[]{:S(2)}, u32[]{:S(2)}) collective-permute-start(f32[2,512]{1,0:T(2,128)S(1)} %add.882), channel_id=1, source_target_pairs={{0,4},{1,5},{2,6},{3,7},{4,0},{5,1},{6,2},{7,3},{8,12},{9,13},{10,... | collective-permute-start | bytes 12296 | tf_op jit(solution)/shard_map/ppermute | solution.py:30
  451.6 16.8 %collective-permute-start.89 = (f32[2,512]{1,0:T(2,128)S(1)}, f32[2,512]{1,0:T(2,128)S(1)}, u32[]{:S(2)}, u32[]{:S(2)}) collective-permute-start(f32[2,512]{1,0:T(2,128)S(1)} %add.882), channel_id=1, source_target_pairs={{0,2},{1,3},{2,0},{3,1},{4,6},{5,7},{6,4},{7,5},{8,10},{9,11},{10,... | collective-permute-start | bytes 12296 | tf_op jit(solution)/shard_map/ppermute | solution.py:30
  460.7 14.4 %collective-permute-start.96 = (bf16[2,272,512]{2,1,0:T(8,128)(2,1)S(1)}, bf16[2,272,512]{2,1,0:T(8,128)(2,1)S(1)}, u32[]{:S(2)}, u32[]{:S(2)}) collective-permute-start(bf16[2,272,512]{2,1,0:T(8,128)(2,1)S(1)} %get-tuple-element.127), channel_id=1, source_target_pairs={{0,8},{1,9},{2,10},{3,11},{4,12},{5,13},{6,14},{7,15},{8,0},{9,1},... | collective-permute-start | bytes 1671176 | tf_op jit(solution)/shard_map/ppermute | solution.py:474
  468.4 6.7 %collective-permute-start.94 = (f32[2,512]{1,0:T(2,128)S(1)}, f32[2,512]{1,0:T(2,128)S(1)}, u32[]{:S(2)}, u32[]{:S(2)}) collective-permute-start(f32[2,512]{1,0:T(2,128)S(1)} %add_add_fusion.10), channel_id=1, source_target_pairs={{0,24},{1,25},{2,26},{3,27},{4,28},{5,29},{6,30},{7,31},{8,16},{9,... | collective-permute-start | bytes 12296 | tf_op jit(solution)/shard_map/ppermute | solution.py:30
  476.5 11.7 %collective-permute-start.98 = (bf16[2,368,512]{2,1,0:T(8,128)(2,1)S(1)}, bf16[2,368,512]{2,1,0:T(8,128)(2,1)S(1)}, u32[]{:S(2)}, u32[]{:S(2)}) collective-permute-start(bf16[2,368,512]{2,1,0:T(8,128)(2,1)S(1)} %get-tuple-element.135), channel_id=1, source_target_pairs={{0,4},{1,3},{2,6},{3,1},{4,0},{5,7},{6,2},{7,5},{8,12},{9,11},{10,... | collective-permute-start | bytes 2261000 | tf_op jit(solution)/shard_map/ppermute | solution.py:474
  491.0 11.9 %collective-permute-start.104 = (bf16[2,368,512]{2,1,0:T(8,128)(2,1)}, bf16[2,368,512]{2,1,0:T(8,128)(2,1)S(1)}, u32[]{:S(2)}, u32[]{:S(2)}) collective-permute-start(bf16[2,368,512]{2,1,0:T(8,128)(2,1)} %copy-done.20), channel_id=1, source_target_pairs={{0,2},{1,5},{2,0},{3,7},{4,6},{5,1},{6,4},{7,3},{8,10},{9,13},{10,... | collective-permute-start | bytes 2261000 | tf_op jit(solution)/shard_map/ppermute | solution.py:474
  494.8 20.2 %collective-permute-start.100 = (bf16[2,368,512]{2,1,0:T(8,128)(2,1)S(1)}, bf16[2,368,512]{2,1,0:T(8,128)(2,1)S(1)}, u32[]{:S(2)}, u32[]{:S(2)}) collective-permute-start(bf16[2,368,512]{2,1,0:T(8,128)(2,1)S(1)} %get-tuple-element.141), channel_id=1, source_target_pairs={{0,2},{1,5},{2,0},{3,7},{4,6},{5,1},{6,4},{7,3},{8,10},{9,13},{10,... | collective-permute-start | bytes 2261000 | tf_op jit(solution)/shard_map/ppermute | solution.py:474
  496.4 43.9 %collective-permute-start.110 = (bf16[1,272,512]{2,1,0:T(8,128)(2,1)S(1)}, bf16[1,272,512]{2,1,0:T(8,128)(2,1)S(1)}, u32[]{:S(2)}, u32[]{:S(2)}) collective-permute-start(bf16[1,272,512]{2,1,0:T(8,128)(2,1)S(1)} %copy-done.22), channel_id=1, source_target_pairs={{0,16},{1,17},{2,18},{3,19},{4,20},{5,21},{6,22},{7,23},{8,24},{9,... | collective-permute-start | bytes 835592 | tf_op jit(solution)/shard_map/ppermute | solution.py:474
  503.1 14.7 %collective-permute-start.105 = (bf16[1,368,512]{2,1,0:T(8,128)(2,1)S(1)}, bf16[1,368,512]{2,1,0:T(8,128)(2,1)S(1)}, u32[]{:S(2)}, u32[]{:S(2)}) collective-permute-start(bf16[1,368,512]{2,1,0:T(8,128)(2,1)S(1)} %get-tuple-element.147), channel_id=1, source_target_pairs={{0,4},{1,3},{2,6},{3,1},{4,0},{5,7},{6,2},{7,5},{8,12},{9,11},{10,... | collective-permute-start | bytes 1130504 | tf_op jit(solution)/shard_map/ppermute | solution.py:474
  515.2 7.7 %collective-permute-start.101 = (bf16[1,368,512]{2,1,0:T(8,128)(2,1)S(1)}, bf16[1,368,512]{2,1,0:T(8,128)(2,1)S(1)}, u32[]{:S(2)}, u32[]{:S(2)}) collective-permute-start(bf16[1,368,512]{2,1,0:T(8,128)(2,1)S(1)} %get-tuple-element.143), channel_id=1, source_target_pairs={{0,4},{1,3},{2,6},{3,1},{4,0},{5,7},{6,2},{7,5},{8,12},{9,11},{10,... | collective-permute-start | bytes 1130504 | tf_op jit(solution)/shard_map/ppermute | solution.py:474
  516.5 17.9 %collective-permute-start.108 = (bf16[1,368,512]{2,1,0:T(8,128)(2,1)S(1)}, bf16[1,368,512]{2,1,0:T(8,128)(2,1)S(1)}, u32[]{:S(2)}, u32[]{:S(2)}) collective-permute-start(bf16[1,368,512]{2,1,0:T(8,128)(2,1)S(1)} %get-tuple-element.151), channel_id=1, source_target_pairs={{0,8},{1,9},{2,10},{3,11},{4,12},{5,13},{6,14},{7,15},{8,0},{9,1},... | collective-permute-start | bytes 1130504 | tf_op jit(solution)/shard_map/ppermute | solution.py:474
  517.9 18.1 %collective-permute-start.106 = (bf16[1,368,512]{2,1,0:T(8,128)(2,1)S(1)}, bf16[1,368,512]{2,1,0:T(8,128)(2,1)S(1)}, u32[]{:S(2)}, u32[]{:S(2)}) collective-permute-start(bf16[1,368,512]{2,1,0:T(8,128)(2,1)S(1)} %add_convert_fusion.2), channel_id=1, source_target_pairs={{0,8},{2,10},{4,12},{6,14},{16,24},{17,1},{18,26},{19,3},{20,28},{... | collective-permute-start | bytes 1130504 | tf_op jit(solution)/shard_map/ppermute | solution.py:474
  523.0 15.9 %collective-permute-start.102 = (bf16[1,368,512]{2,1,0:T(8,128)(2,1)S(1)}, bf16[1,368,512]{2,1,0:T(8,128)(2,1)S(1)}, u32[]{:S(2)}, u32[]{:S(2)}) collective-permute-start(bf16[1,368,512]{2,1,0:T(8,128)(2,1)S(1)} %add_convert_fusion.4), channel_id=1, source_target_pairs={{8,0},{10,2},{12,4},{14,6},{17,1},{19,3},{21,5},{23,7},{24,16},{25... | collective-permute-start | bytes 1130504 | tf_op jit(solution)/shard_map/ppermute | solution.py:474
  534.5 11.5 %collective-permute-start.109 = (bf16[1,368,512]{2,1,0:T(8,128)(2,1)S(1)}, bf16[1,368,512]{2,1,0:T(8,128)(2,1)S(1)}, u32[]{:S(2)}, u32[]{:S(2)}) collective-permute-start(bf16[1,368,512]{2,1,0:T(8,128)(2,1)S(1)} %add_convert_fusion), channel_id=1, source_target_pairs={{0,16},{1,17},{2,18},{3,19},{4,20},{5,21},{6,22},{7,23},{8,24},{9,... | collective-permute-start | bytes 1130504 | tf_op jit(solution)/shard_map/ppermute | solution.py:474
  536.1 10.0 %collective-permute-start.107 = (bf16[1,368,512]{2,1,0:T(8,128)(2,1)S(1)}, bf16[1,368,512]{2,1,0:T(8,128)(2,1)S(1)}, u32[]{:S(2)}, u32[]{:S(2)}) collective-permute-start(bf16[1,368,512]{2,1,0:T(8,128)(2,1)S(1)} %add_convert_fusion.1), channel_id=1, source_target_pairs={{1,9},{3,11},{5,13},{7,15},{24,8},{26,10},{28,12},{30,14}} | collective-permute-start | bytes 1130504 | tf_op jit(solution)/shard_map/ppermute | solution.py:474
  538.9 10.5 %collective-permute-start.103 = (bf16[1,368,512]{2,1,0:T(8,128)(2,1)S(1)}, bf16[1,368,512]{2,1,0:T(8,128)(2,1)S(1)}, u32[]{:S(2)}, u32[]{:S(2)}) collective-permute-start(bf16[1,368,512]{2,1,0:T(8,128)(2,1)S(1)} %add_convert_fusion.3), channel_id=1, source_target_pairs={{9,1},{11,3},{13,5},{15,7},{16,0},{18,2},{20,4},{22,6}} | collective-permute-start | bytes 1130504 | tf_op jit(solution)/shard_map/ppermute | solution.py:474
  (178 other events, 1125.6 us)
Sparse Core Ops, SparseCore 0:
  11.4 96.4 all-gather.3
  111.4 78.9 all-gather.5
  193.2 80.1 all-gather.7

commit v4 on v3

--- a/solution.py
+++ b/solution.py
@@ -1020,24 +1020,21 @@
     act_one_cot = conv_back(low_two, w_spatial, 2)
     act_one_cot, first_grad = step([late], (act_one_cot, first_grad))
     act_one_cot = act_one_cot * silu_slope(norm_one.shifted())
-    grads_one, first_grad = step(
-        [sum_second], (norm_one.partial_grads(act_one_cot), first_grad)
-    )
-    grads_one = all_sum(grads_one)
+    grads_one = norm_one.partial_grads(act_one_cot)
     grad_spatial = conv_kernel_grad(act_one, low_two, 2).astype(BF16)
     early_rows = part * first_shape[1]
     first_grad = placed(first_grad, early_rows, grad_spatial[early_rows - 1024 :])
     last_grad = jnp.pad(grad_spatial[: early_rows - 1024], ((1024, 0), (0, 0)))
     early = ScatterSum(first_grad.reshape(first_shape), part, part)
+    grads_one, (first_grad, last_grad) = all_sum(grads_one, [early], (first_grad, last_grad))
     grads_one, first_grad, last_grad = step(
-        [early, late, sum_second], (grads_one, first_grad, last_grad)
+        [early, late], (grads_one, first_grad, last_grad)
     )
     low_one = pad_side(norm_one.pull(act_one_cot, grads_one).astype(BF16), 16)
-    low_one = step([early], low_one)
     last_grad = grad_into(early_rows, 0, full_views, low_one.reshape(-1, C_MID), last_grad)
     last_grad = arrive([late], last_grad)
     last = ScatterSum(last_grad.reshape(part, *first_shape[1:]), 0, part)
-    low_one = step([last], low_one)
+    low_one = step([last, sum_second], low_one)
     views_cot = input_grad(low_one, w_reduce, strided_cot)
     groups = [early, last, late, sum_second]
     while any(not group.done() for group in groups):

time: 568 us -> 602 us (1.060)
  waiting for transfers between devices: 216 us -> 250 us
    ppermute x20, waiting for transfers between devices: 48.2 us -> 74.3 us  [send(): self.incoming = lax.ppermute(outgoing, BOTH, pairs)]
    ppermute x91, waiting for transfers between devices: 60.7 us -> 69 us  [swap(): lax.ppermute(values, BOTH, [(i, i ^ mask) for i in range(device_count())])]
  transfers between devices with their start and end apart: 114 -> 114, of which waited for: 64 -> 64; matrix products, arithmetic and copies ran while one was open for 18% -> 17% of each run, Pallas kernels for 5% -> 5%
where the time goes in v4:
time: 602 us; the launch traced here: 593 us
  waiting for transfers between devices  250 us (42%)
  starting transfers between devices  123 us (20%)
  matrix products  62.7 us (10%)
  Pallas kernels  59.8 us (10%)
  local copies, waits for them, and re-layouts  50.4 us (8%)
  other arithmetic  30.1 us (5%)
  between operations  16.4 us (3%)
    all_gather x3, waiting for transfers between devices, gather(): return lax.all_gather(flat.reshape(-1, C_MID), BOTH, axis=0, tiled=True)  107 us
    ppermute x91, starting transfers between devices, swap(): lax.ppermute(values, BOTH, [(i, i ^ mask) for i in range(device_count())])  104 us
    ppermute x20, waiting for transfers between devices, send(): self.incoming = lax.ppermute(outgoing, BOTH, pairs)  74.3 us
    ppermute x91, waiting for transfers between devices, swap(): lax.ppermute(values, BOTH, [(i, i ^ mask) for i in range(device_count())])  69 us
    pallas_call x1, Pallas kernels, head_pass(): pl.pallas_call(head_kernel, out_shape=[shape((total, C_OUT), F32), shape(...  21.1 us
    unnamed x237, local copies, waits for them, and re-layouts  21 us
    ppermute x20, starting transfers between devices, send(): self.incoming = lax.ppermute(outgoing, BOTH, pairs)  18.9 us
    dot_general x4, matrix products, times_back(): lax.dot_general(cotan, kernel, (((cotan.ndim - 1,), (1,)), ((), ())), pre...  15.6 us
  transfers between devices with their start and end apart: 114, of which 64 were waited for; matrix products, arithmetic and copies ran while one was open for 17% of the time, Pallas kernels for 5%

profile of v4, /device:TPU:0, one launch (start us, length us, event | category | flops | bytes accessed | tf_op | source)
XLA Modules:
  0.0 592.8 jit_solution(1147588117998059383)
XLA Ops:
  16.8 91.1 %all-gather.4.cloned.1.call-done.refs_1_ = bf16[11776,512]{1,0:T(8,128)(2,1)} async-done(((bf16[368,512]{1,0:T(8,128)(2,1)}), bf16[11776,512]{1,0:T(8,128)(2,1)}) %all-gather.4.cloned.1.call-update) | async-done | bytes 12058640 | tf_op jit(solution)/shard_map/all_gather | solution.py:884
  108.0 4.5 fusion.74
  126.1 2.8 slice.215
  130.8 4.5 fusion.76
  135.4 2.8 shard_map.147
  146.0 2.8 collective-permute-start.11
  158.8 2.5 collective-permute-done.17
  168.9 3.2 collective-permute-done.19
  172.2 2.4 multiply_convert_fusion.3
  174.6 15.7 %all-gather.6.cloned.1.call-done.refs_1_ = bf16[8704,512]{1,0:T(8,128)(2,1)} async-done(((bf16[272,512]{1,0:T(8,128)(2,1)}), bf16[8704,512]{1,0:T(8,128)(2,1)}) %all-gather.6.cloned.1.call-update) | async-done | bytes 8912912 | tf_op jit(solution)/shard_map/all_gather | solution.py:884
  190.3 3.5 fusion.77
  198.8 2.6 collective-permute-done.24
  206.0 2.7 slice.272
  209.5 3.2 fusion.75
  227.9 3.0 fusion.71
  246.0 3.5 multiply_reduce_fusion.3
  257.0 2.9 collective-permute-done.44
  273.3 21.1 %shard_map.149 = (f32[192,2048]{1,0:T(8,128)}, f32[192,2048]{1,0:T(8,128)}, f32[192,2048]{1,0:T(8,128)}, f32[192,128]{1,0:T(8,128)S(1)}, f32[2,2048]{1,0:T(2,128...) custom-call(s32[1]{0:T(128)} %bitcast.device, bf16[32,6,2176]{2,1,0:T(8,128)(2,1)} %copy_dynamic-update-slice_fusion.gathered, ...), custom_call_target="tpu_custom_call" | custom-call | flops 3221225472 | bytes 20971520 | tf_op jit(solution)/shard_map/pallas_call | solution.py:293
  294.4 3.4 multiply_reduce_fusion.2
  312.9 3.4 multiply_convert_fusion.2
  316.4 2.7 multiply_reduce_fusion.10
  333.1 3.4 multiply_reduce_fusion.9
  341.3 4.1 convolution_convert_fusion.1
  353.4 6.6 %multiply_reduce_fusion.1 = (f32[2048]{0:T(1024)S(1)}, f32[2048]{0:T(1024)S(1)}, f32[2048]{0:T(1024)S(1)}, f32[6,7,7,2048]{3,2,1,0:T(8,128)}) fusion(f32[6,7,7,2048]{3,2,1,0:T(8,128)S(1)} %copy-done.34, f32[2048]{0:T(1024)S(1)} %get-tuple-element.268, f32[2048]{0:T(1024)S(1)} %bitcast.250, f32[2048]{0:T(1024)S(1)} %get-tuple-element.223, ...), kind=kOutput, calls=%fused_computation.24 | convolution fusion | flops 630405120 | bytes 12122112 | tf_op jit(solution)/shard_map/dot_general | solution.py:661
  364.9 2.8 shard_map.151
  376.2 4.1 multiply_convert_fusion
  380.3 3.6 multiply_reduce_fusion.8
  383.9 3.5 shard_map.153
  394.4 4.6 shard_map.155
  399.3 5.2 copy-done
  408.1 2.7 fusion.1.strided
  412.9 2.8 collective-permute-done.81
  420.1 4.3 fusion
  424.5 2.8 shard_map.156
  429.1 5.3 fusion.80
  439.0 6.4 %convolution_convert_fusion = bf16[3,3,512,512]{3,2,1,0:T(8,128)(2,1)} fusion(bf16[6,7,7,512]{3,0,2,1:T(8,128)(2,1)S(1)} %multiply_convert_fusion.5, bf16[6,14,14,512]{3,2,1,0:T(8,128)(2,1)S(1)} %copy-done.46), kind=kOutput, calls=%fused_computation.9 | convolution fusion | flops 1260650496 | bytes 6223872 | tf_op jit(solution)/shard_map/conv_general_dilated | solution.py:703
  454.0 13.7 %collective-permute-done.90 = f32[2,512]{1,0:T(2,128)S(1)} collective-permute-done((f32[2,512]{1,0:T(2,128)S(1)}, f32[2,512]{1,0:T(2,128)S(1)}, u32[]{:S(2)}, u32[]{:S(2)}) %collective-permute-start.90) | collective-permute-done | bytes 4128 | tf_op jit(solution)/shard_map/ppermute | solution.py:30
  470.7 12.6 %collective-permute-done.97.refs_1_.refs_3_ = bf16[4,272,512]{2,1,0:T(8,128)(2,1)S(1)} collective-permute-done((bf16[4,272,512]{2,1,0:T(8,128)(2,1)S(1)}, bf16[4,272,512]{2,1,0:T(8,128)(2,1)S(1)}, u32[]{:S(2)}, u32[]{:S(2)}) %collective-permute-start.97) | collective-permute-done | bytes 1114144 | tf_op jit(solution)/shard_map/ppermute | solution.py:474
  494.0 2.9 shard_map.162
  497.0 4.6 collective-permute-done.96.refs_1_.refs_3_
  509.8 6.4 %collective-permute-done.103.refs_1_.refs_3_ = bf16[2,368,512]{2,1,0:T(8,128)(2,1)S(1)} collective-permute-done((bf16[2,368,512]{2,1,0:T(8,128)(2,1)}, bf16[2,368,512]{2,1,0:T(8,128)(2,1)S(1)}, u32[]{:S(2)}, u32[]{:S(2)}) %collective-permute-start.103) | collective-permute-done | bytes 753696 | tf_op jit(solution)/shard_map/ppermute | solution.py:474
  517.5 10.9 %collective-permute-done.99.refs_1_.refs_3_ = bf16[2,368,512]{2,1,0:T(8,128)(2,1)S(1)} collective-permute-done((bf16[2,368,512]{2,1,0:T(8,128)(2,1)S(1)}, bf16[2,368,512]{2,1,0:T(8,128)(2,1)S(1)}, u32[]{:S(2)}, u32[]{:S(2)}) %collective-permute-start.99) | collective-permute-done | bytes 753696 | tf_op jit(solution)/shard_map/ppermute | solution.py:474
  537.6 12.0 %collective-permute-done.107 = bf16[1,368,512]{2,1,0:T(8,128)(2,1)S(1)} collective-permute-done((bf16[1,368,512]{2,1,0:T(8,128)(2,1)S(1)}, bf16[1,368,512]{2,1,0:T(8,128)(2,1)S(1)}, u32[]{:S(2)}, u32[]{:S(2)}) %collective-permute-start.107) | collective-permute-done | bytes 376864 | tf_op jit(solution)/shard_map/ppermute | solution.py:474
  551.2 8.8 %collective-permute-done.109.refs_1_.refs_3_ = bf16[2,272,512]{2,1,0:T(8,128)(2,1)S(1)} collective-permute-done((bf16[2,272,512]{2,1,0:T(8,128)(2,1)S(1)}, bf16[2,272,512]{2,1,0:T(8,128)(2,1)S(1)}, u32[]{:S(2)}, u32[]{:S(2)}) %collective-permute-start.109) | collective-permute-done | bytes 557088 | tf_op jit(solution)/shard_map/ppermute | solution.py:474
  561.1 3.1 collective-permute-done.101
  565.6 4.8 shard_map.165
  570.4 10.0 %collective-permute-done.110 = bf16[1,272,512]{2,1,0:T(8,128)(2,1)S(1)} collective-permute-done((bf16[1,272,512]{2,1,0:T(8,128)(2,1)S(1)}, bf16[1,272,512]{2,1,0:T(8,128)(2,1)S(1)}, u32[]{:S(2)}, u32[]{:S(2)}) %collective-permute-start.110) | collective-permute-done | bytes 278560 | tf_op jit(solution)/shard_map/ppermute | solution.py:474
  581.5 3.0 collective-permute-done.102
  (595 shorter events, 236.8 us)
Async XLA Ops:
  7.2 100.8 %all-gather.4.cloned.1.call-start = ((), (), s32[]{:S(2)}) async-start(), calls=%async_computation | async-start | bytes 12435456 | tf_op jit(solution)/shard_map/all_gather | solution.py:884
  9.2 181.1 %all-gather.6.cloned.1.call-start = ((), (), s32[]{:S(2)}) async-start(), calls=%async_computation.1 | async-start | bytes 9191424 | tf_op jit(solution)/shard_map/all_gather | solution.py:884
  11.1 262.2 %all-gather.8.cloned.1.call-start = ((), (), s32[]{:S(2)}) async-start(), calls=%async_computation.2 | async-start | bytes 9191424 | tf_op jit(solution)/shard_map/all_gather | solution.py:884
  120.1 8.8 %collective-permute-start.6 = (f32[2,512]{1,0:T(2,128)S(1)}, f32[2,512]{1,0:T(2,128)S(1)}, u32[]{:S(2)}, u32[]{:S(2)}) collective-permute-start(f32[2,512]{1,0:T(2,128)S(1)} %add_add_fusion.24), channel_id=1, source_target_pairs={{0,24},{1,25},{2,26},{3,27},{4,28},{5,29},{6,30},{7,31},{8,16},{9,... | collective-permute-start | bytes 12296 | tf_op jit(solution)/shard_map/ppermute | solution.py:30
  121.8 7.1 %collective-permute-start.5 = (f32[2,512]{1,0:T(2,128)S(1)}, f32[2,512]{1,0:T(2,128)S(1)}, u32[]{:S(2)}, u32[]{:S(2)}) collective-permute-start(f32[2,512]{1,0:T(2,128)S(1)} %add_add_fusion.24), channel_id=1, source_target_pairs={{0,16},{1,17},{2,18},{3,19},{4,20},{5,21},{6,22},{7,23},{8,24},{9,... | collective-permute-start | bytes 12296 | tf_op jit(solution)/shard_map/ppermute | solution.py:30
  122.7 6.2 %collective-permute-start.4 = (f32[2,512]{1,0:T(2,128)S(1)}, f32[2,512]{1,0:T(2,128)S(1)}, u32[]{:S(2)}, u32[]{:S(2)}) collective-permute-start(f32[2,512]{1,0:T(2,128)S(1)} %add_add_fusion.24), channel_id=1, source_target_pairs={{0,8},{1,9},{2,10},{3,11},{4,12},{5,13},{6,14},{7,15},{8,0},{9,1},... | collective-permute-start | bytes 12296 | tf_op jit(solution)/shard_map/ppermute | solution.py:30
  162.1 6.8 %collective-permute-start.20 = (f32[4,2048]{1,0:T(4,128)S(1)}, f32[4,2048]{1,0:T(4,128)S(1)}, u32[]{:S(2)}, u32[]{:S(2)}) collective-permute-start(f32[4,2048]{1,0:T(4,128)S(1)} %add_add_fusion.4), channel_id=1, source_target_pairs={{0,24},{1,25},{2,26},{3,27},{4,28},{5,29},{6,30},{7,31},{8,16},{9,... | collective-permute-start | bytes 98312 | tf_op jit(solution)/shard_map/ppermute | solution.py:30
  164.4 7.7 %collective-permute-start.19 = (f32[4,2048]{1,0:T(4,128)S(1)}, f32[4,2048]{1,0:T(4,128)S(1)}, u32[]{:S(2)}, u32[]{:S(2)}) collective-permute-start(f32[4,2048]{1,0:T(4,128)S(1)} %add_add_fusion.4), channel_id=1, source_target_pairs={{0,16},{1,17},{2,18},{3,19},{4,20},{5,21},{6,22},{7,23},{8,24},{9,... | collective-permute-start | bytes 98312 | tf_op jit(solution)/shard_map/ppermute | solution.py:30
  165.4 6.7 %collective-permute-start.18 = (f32[4,2048]{1,0:T(4,128)S(1)}, f32[4,2048]{1,0:T(4,128)S(1)}, u32[]{:S(2)}, u32[]{:S(2)}) collective-permute-start(f32[4,2048]{1,0:T(4,128)S(1)} %add_add_fusion.4), channel_id=1, source_target_pairs={{0,8},{1,9},{2,10},{3,11},{4,12},{5,13},{6,14},{7,15},{8,0},{9,1},... | collective-permute-start | bytes 98312 | tf_op jit(solution)/shard_map/ppermute | solution.py:30
  201.6 7.1 %collective-permute-start.27 = (f32[2,512]{1,0:T(2,128)S(1)}, f32[2,512]{1,0:T(2,128)S(1)}, u32[]{:S(2)}, u32[]{:S(2)}) collective-permute-start(f32[2,512]{1,0:T(2,128)S(1)} %add_add_fusion.20), channel_id=1, source_target_pairs={{0,24},{1,25},{2,26},{3,27},{4,28},{5,29},{6,30},{7,31},{8,16},{9,... | collective-permute-start | bytes 12296 | tf_op jit(solution)/shard_map/ppermute | solution.py:30
  250.2 6.4 %collective-permute-start.43 = (bf16[1,6,2176]{2,1,0:T(8,128)(2,1)S(1)}, bf16[1,6,2176]{2,1,0:T(8,128)(2,1)S(1)}, u32[]{:S(2)}, u32[]{:S(2)}) collective-permute-start(bf16[1,6,2176]{2,1,0:T(8,128)(2,1)S(1)} %get-tuple-element.212), channel_id=1, source_target_pairs={{0,16},{1,17},{2,18},{3,19},{4,20},{5,21},{6,22},{7,23},{8,24},{9,... | collective-permute-start | bytes 78344 | tf_op jit(solution)/shard_map/ppermute | solution.py:30
  253.4 6.5 %collective-permute-start.44 = (bf16[1,6,2176]{2,1,0:T(8,128)(2,1)S(1)}, bf16[1,6,2176]{2,1,0:T(8,128)(2,1)S(1)}, u32[]{:S(2)}, u32[]{:S(2)}) collective-permute-start(bf16[1,6,2176]{2,1,0:T(8,128)(2,1)S(1)} %get-tuple-element.212), channel_id=1, source_target_pairs={{0,24},{1,25},{2,26},{3,27},{4,28},{5,29},{6,30},{7,31},{8,16},{9,... | collective-permute-start | bytes 78344 | tf_op jit(solution)/shard_map/ppermute | solution.py:30
  259.9 8.9 %collective-permute-start.47 = (bf16[4,6,2176]{2,1,0:T(8,128)(2,1)S(1)}, bf16[4,6,2176]{2,1,0:T(8,128)(2,1)S(1)}, u32[]{:S(2)}, u32[]{:S(2)}) collective-permute-start(bf16[4,6,2176]{2,1,0:T(8,128)(2,1)S(1)} %pad_maximum_fusion), channel_id=1, source_target_pairs={{0,6},{1,7},{2,4},{3,5},{4,2},{5,3},{6,0},{7,1},{8,14},{9,15},{10,... | collective-permute-start | bytes 313352 | tf_op jit(solution)/shard_map/ppermute | solution.py:30
  260.6 7.6 %collective-permute-start.46 = (bf16[4,6,2176]{2,1,0:T(8,128)(2,1)S(1)}, bf16[4,6,2176]{2,1,0:T(8,128)(2,1)S(1)}, u32[]{:S(2)}, u32[]{:S(2)}) collective-permute-start(bf16[4,6,2176]{2,1,0:T(8,128)(2,1)S(1)} %pad_maximum_fusion), channel_id=1, source_target_pairs={{0,4},{1,5},{2,6},{3,7},{4,0},{5,1},{6,2},{7,3},{8,12},{9,13},{10,... | collective-permute-start | bytes 313352 | tf_op jit(solution)/shard_map/ppermute | solution.py:30
  325.9 6.8 %collective-permute-start.62 = (f32[2,512]{1,0:T(2,128)S(1)}, f32[2,512]{1,0:T(2,128)S(1)}, u32[]{:S(2)}, u32[]{:S(2)}) collective-permute-start(f32[2,512]{1,0:T(2,128)S(1)} %add_add_fusion.16), channel_id=1, source_target_pairs={{0,24},{1,25},{2,26},{3,27},{4,28},{5,29},{6,30},{7,31},{8,16},{9,... | collective-permute-start | bytes 12296 | tf_op jit(solution)/shard_map/ppermute | solution.py:30
  337.7 7.7 %collective-permute-start.65 = (f32[2,512]{1,0:T(2,128)S(1)}, f32[2,512]{1,0:T(2,128)S(1)}, u32[]{:S(2)}, u32[]{:S(2)}) collective-permute-start(f32[2,512]{1,0:T(2,128)S(1)} %fusion.59), channel_id=1, source_target_pairs={{0,4},{1,5},{2,6},{3,7},{4,0},{5,1},{6,2},{7,3},{8,12},{9,13},{10,... | collective-permute-start | bytes 12296 | tf_op jit(solution)/shard_map/ppermute | solution.py:30
  338.9 6.5 %collective-permute-start.66 = (f32[2,512]{1,0:T(2,128)S(1)}, f32[2,512]{1,0:T(2,128)S(1)}, u32[]{:S(2)}, u32[]{:S(2)}) collective-permute-start(f32[2,512]{1,0:T(2,128)S(1)} %fusion.59), channel_id=1, source_target_pairs={{0,6},{1,7},{2,4},{3,5},{4,2},{5,3},{6,0},{7,1},{8,14},{9,15},{10,... | collective-permute-start | bytes 12296 | tf_op jit(solution)/shard_map/ppermute | solution.py:30
  361.3 6.8 %collective-permute-start.72 = (f32[3,2048]{1,0:T(4,128)S(1)}, f32[3,2048]{1,0:T(4,128)S(1)}, u32[]{:S(2)}, u32[]{:S(2)}) collective-permute-start(f32[3,2048]{1,0:T(4,128)S(1)} %fusion.67), channel_id=1, source_target_pairs={{0,4},{1,5},{2,6},{3,7},{4,0},{5,1},{6,2},{7,3},{8,12},{9,13},{10,... | collective-permute-start | bytes 73736 | tf_op jit(solution)/shard_map/ppermute | solution.py:30
  368.4 15.6 %collective-permute-start.77 = (bf16[16,272,512]{2,1,0:T(8,128)(2,1)S(1)}, bf16[16,272,512]{2,1,0:T(8,128)(2,1)S(1)}, u32[]{:S(2)}, u32[]{:S(2)}) collective-permute-start(bf16[16,272,512]{2,1,0:T(8,128)(2,1)S(1)} %shard_map.152), channel_id=1, source_target_pairs={{0,1},{1,0},{2,3},{3,2},{4,5},{5,4},{6,7},{7,6},{8,9},{9,8},{10,11... | collective-permute-start | bytes 13369352 | tf_op jit(solution)/shard_map/ppermute | solution.py:474
  387.4 37.1 %collective-permute-start.85 = (bf16[8,272,512]{2,1,0:T(8,128)(2,1)}, bf16[8,272,512]{2,1,0:T(8,128)(2,1)}, u32[]{:S(2)}, u32[]{:S(2)}) collective-permute-start(bf16[8,272,512]{2,1,0:T(8,128)(2,1)} %get-tuple-element.108), channel_id=1, source_target_pairs={{0,2},{1,5},{2,0},{3,7},{4,6},{5,1},{6,4},{7,3},{8,10},{9,13},{10,... | collective-permute-start | bytes 6684680 | tf_op jit(solution)/shard_map/ppermute | solution.py:474
  394.3 10.2 %collective-permute-start.78 = (f32[2,512]{1,0:T(2,128)S(1)}, f32[2,512]{1,0:T(2,128)S(1)}, u32[]{:S(2)}, u32[]{:S(2)}) collective-permute-start(f32[2,512]{1,0:T(2,128)S(1)} %pad_maximum_fusion.12), channel_id=1, source_target_pairs={{0,1},{1,0},{2,3},{3,2},{4,5},{5,4},{6,7},{7,6},{8,9},{9,8},{10,11... | collective-permute-start | bytes 12296 | tf_op jit(solution)/shard_map/ppermute | solution.py:30
  404.6 11.1 %collective-permute-start.81 = (f32[2,512]{1,0:T(2,128)S(1)}, f32[2,512]{1,0:T(2,128)S(1)}, u32[]{:S(2)}, u32[]{:S(2)}) collective-permute-start(f32[2,512]{1,0:T(2,128)S(1)} %add.870), channel_id=1, source_target_pairs={{0,6},{1,7},{2,4},{3,5},{4,2},{5,3},{6,0},{7,1},{8,14},{9,15},{10,... | collective-permute-start | bytes 12296 | tf_op jit(solution)/shard_map/ppermute | solution.py:30
  405.7 9.9 %collective-permute-start.80 = (f32[2,512]{1,0:T(2,128)S(1)}, f32[2,512]{1,0:T(2,128)S(1)}, u32[]{:S(2)}, u32[]{:S(2)}) collective-permute-start(f32[2,512]{1,0:T(2,128)S(1)} %add.870), channel_id=1, source_target_pairs={{0,4},{1,5},{2,6},{3,7},{4,0},{5,1},{6,2},{7,3},{8,12},{9,13},{10,... | collective-permute-start | bytes 12296 | tf_op jit(solution)/shard_map/ppermute | solution.py:30
  406.7 8.9 %collective-permute-start.79 = (f32[2,512]{1,0:T(2,128)S(1)}, f32[2,512]{1,0:T(2,128)S(1)}, u32[]{:S(2)}, u32[]{:S(2)}) collective-permute-start(f32[2,512]{1,0:T(2,128)S(1)} %add.870), channel_id=1, source_target_pairs={{0,2},{1,3},{2,0},{3,1},{4,6},{5,7},{6,4},{7,5},{8,10},{9,11},{10,... | collective-permute-start | bytes 12296 | tf_op jit(solution)/shard_map/ppermute | solution.py:30
  415.7 8.8 %collective-permute-start.84 = (f32[2,512]{1,0:T(2,128)S(1)}, f32[2,512]{1,0:T(2,128)S(1)}, u32[]{:S(2)}, u32[]{:S(2)}) collective-permute-start(f32[2,512]{1,0:T(2,128)S(1)} %add_add_fusion.12), channel_id=1, source_target_pairs={{0,24},{1,25},{2,26},{3,27},{4,28},{5,29},{6,30},{7,31},{8,16},{9,... | collective-permute-start | bytes 12296 | tf_op jit(solution)/shard_map/ppermute | solution.py:30
  417.7 6.8 %collective-permute-start.83 = (f32[2,512]{1,0:T(2,128)S(1)}, f32[2,512]{1,0:T(2,128)S(1)}, u32[]{:S(2)}, u32[]{:S(2)}) collective-permute-start(f32[2,512]{1,0:T(2,128)S(1)} %add_add_fusion.12), channel_id=1, source_target_pairs={{0,16},{1,17},{2,18},{3,19},{4,20},{5,21},{6,22},{7,23},{8,24},{9,... | collective-permute-start | bytes 12296 | tf_op jit(solution)/shard_map/ppermute | solution.py:30
  427.4 7.1 %collective-permute-start.86 = (bf16[8,368,512]{2,1,0:T(8,128)(2,1)S(1)}, bf16[8,368,512]{2,1,0:T(8,128)(2,1)S(1)}, u32[]{:S(2)}, u32[]{:S(2)}) collective-permute-start(bf16[8,368,512]{2,1,0:T(8,128)(2,1)S(1)} %copy-done.15), channel_id=1, source_target_pairs={{0,1},{1,0},{2,3},{3,2},{4,5},{5,4},{6,7},{7,6},{8,9},{9,8},{10,11... | collective-permute-start | bytes 9043976 | tf_op jit(solution)/shard_map/ppermute | solution.py:474
  438.4 10.0 %collective-permute-start.87 = (f32[2,512]{1,0:T(2,128)S(1)}, f32[2,512]{1,0:T(2,128)S(1)}, u32[]{:S(2)}, u32[]{:S(2)}) collective-permute-start(f32[2,512]{1,0:T(2,128)S(1)} %pad_maximum_fusion.13), channel_id=1, source_target_pairs={{0,1},{1,0},{2,3},{3,2},{4,5},{5,4},{6,7},{7,6},{8,9},{9,8},{10,11... | collective-permute-start | bytes 12296 | tf_op jit(solution)/shard_map/ppermute | solution.py:30
  447.3 39.7 %collective-permute-start.95 = (bf16[4,368,512]{2,1,0:T(8,128)(2,1)S(1)}, bf16[4,368,512]{2,1,0:T(8,128)(2,1)S(1)}, u32[]{:S(2)}, u32[]{:S(2)}) collective-permute-start(bf16[4,368,512]{2,1,0:T(8,128)(2,1)S(1)} %get-tuple-element.121), channel_id=1, source_target_pairs={{0,2},{1,5},{2,0},{3,7},{4,6},{5,1},{6,4},{7,3},{8,10},{9,13},{10,... | collective-permute-start | bytes 4521992 | tf_op jit(solution)/shard_map/ppermute | solution.py:474
  449.9 17.8 %collective-permute-start.90 = (f32[2,512]{1,0:T(2,128)S(1)}, f32[2,512]{1,0:T(2,128)S(1)}, u32[]{:S(2)}, u32[]{:S(2)}) collective-permute-start(f32[2,512]{1,0:T(2,128)S(1)} %fusion.58), channel_id=1, source_target_pairs={{0,6},{1,7},{2,4},{3,5},{4,2},{5,3},{6,0},{7,1},{8,14},{9,15},{10,... | collective-permute-start | bytes 12296 | tf_op jit(solution)/shard_map/ppermute | solution.py:30
  450.9 16.8 %collective-permute-start.88 = (f32[2,512]{1,0:T(2,128)S(1)}, f32[2,512]{1,0:T(2,128)S(1)}, u32[]{:S(2)}, u32[]{:S(2)}) collective-permute-start(f32[2,512]{1,0:T(2,128)S(1)} %fusion.58), channel_id=1, source_target_pairs={{0,2},{1,3},{2,0},{3,1},{4,6},{5,7},{6,4},{7,5},{8,10},{9,11},{10,... | collective-permute-start | bytes 12296 | tf_op jit(solution)/shard_map/ppermute | solution.py:30
  467.7 19.7 %collective-permute-start.94 = (bf16[4,368,512]{2,1,0:T(8,128)(2,1)S(1)}, bf16[4,368,512]{2,1,0:T(8,128)(2,1)S(1)}, u32[]{:S(2)}, u32[]{:S(2)}) collective-permute-start(bf16[4,368,512]{2,1,0:T(8,128)(2,1)S(1)} %shard_map.159), channel_id=1, source_target_pairs={{0,1},{1,0},{2,3},{3,2},{4,5},{5,4},{6,7},{7,6},{8,9},{9,8},{10,11... | collective-permute-start | bytes 4521992 | tf_op jit(solution)/shard_map/ppermute | solution.py:474
  467.8 15.6 %collective-permute-start.97 = (bf16[4,272,512]{2,1,0:T(8,128)(2,1)S(1)}, bf16[4,272,512]{2,1,0:T(8,128)(2,1)S(1)}, u32[]{:S(2)}, u32[]{:S(2)}) collective-permute-start(bf16[4,272,512]{2,1,0:T(8,128)(2,1)S(1)} %get-tuple-element.129), channel_id=1, source_target_pairs={{0,4},{1,3},{2,6},{3,1},{4,0},{5,7},{6,2},{7,5},{8,12},{9,11},{10,... | collective-permute-start | bytes 3342344 | tf_op jit(solution)/shard_map/ppermute | solution.py:474
  468.8 16.1 %collective-permute-start.93 = (f32[2,512]{1,0:T(2,128)S(1)}, f32[2,512]{1,0:T(2,128)S(1)}, u32[]{:S(2)}, u32[]{:S(2)}) collective-permute-start(f32[2,512]{1,0:T(2,128)S(1)} %add_add_fusion.10), channel_id=1, source_target_pairs={{0,24},{1,25},{2,26},{3,27},{4,28},{5,29},{6,30},{7,31},{8,16},{9,... | collective-permute-start | bytes 12296 | tf_op jit(solution)/shard_map/ppermute | solution.py:30
  470.7 14.2 %collective-permute-start.92 = (f32[2,512]{1,0:T(2,128)S(1)}, f32[2,512]{1,0:T(2,128)S(1)}, u32[]{:S(2)}, u32[]{:S(2)}) collective-permute-start(f32[2,512]{1,0:T(2,128)S(1)} %add_add_fusion.10), channel_id=1, source_target_pairs={{0,16},{1,17},{2,18},{3,19},{4,20},{5,21},{6,22},{7,23},{8,24},{9,... | collective-permute-start | bytes 12296 | tf_op jit(solution)/shard_map/ppermute | solution.py:30
  490.0 11.6 %collective-permute-start.96 = (bf16[2,368,512]{2,1,0:T(8,128)(2,1)S(1)}, bf16[2,368,512]{2,1,0:T(8,128)(2,1)S(1)}, u32[]{:S(2)}, u32[]{:S(2)}) collective-permute-start(bf16[2,368,512]{2,1,0:T(8,128)(2,1)S(1)} %get-tuple-element.126), channel_id=1, source_target_pairs={{0,4},{1,3},{2,6},{3,1},{4,0},{5,7},{6,2},{7,5},{8,12},{9,11},{10,... | collective-permute-start | bytes 2261000 | tf_op jit(solution)/shard_map/ppermute | solution.py:474
  504.3 11.9 %collective-permute-start.103 = (bf16[2,368,512]{2,1,0:T(8,128)(2,1)}, bf16[2,368,512]{2,1,0:T(8,128)(2,1)S(1)}, u32[]{:S(2)}, u32[]{:S(2)}) collective-permute-start(bf16[2,368,512]{2,1,0:T(8,128)(2,1)} %copy-done.22), channel_id=1, source_target_pairs={{0,2},{1,5},{2,0},{3,7},{4,6},{5,1},{6,4},{7,3},{8,10},{9,13},{10,... | collective-permute-start | bytes 2261000 | tf_op jit(solution)/shard_map/ppermute | solution.py:474
  508.3 20.1 %collective-permute-start.99 = (bf16[2,368,512]{2,1,0:T(8,128)(2,1)S(1)}, bf16[2,368,512]{2,1,0:T(8,128)(2,1)S(1)}, u32[]{:S(2)}, u32[]{:S(2)}) collective-permute-start(bf16[2,368,512]{2,1,0:T(8,128)(2,1)S(1)} %get-tuple-element.135), channel_id=1, source_target_pairs={{0,2},{1,5},{2,0},{3,7},{4,6},{5,1},{6,4},{7,3},{8,10},{9,13},{10,... | collective-permute-start | bytes 2261000 | tf_op jit(solution)/shard_map/ppermute | solution.py:474
  516.4 15.5 %collective-permute-start.104 = (bf16[1,368,512]{2,1,0:T(8,128)(2,1)S(1)}, bf16[1,368,512]{2,1,0:T(8,128)(2,1)S(1)}, u32[]{:S(2)}, u32[]{:S(2)}) collective-permute-start(bf16[1,368,512]{2,1,0:T(8,128)(2,1)S(1)} %get-tuple-element.141), channel_id=1, source_target_pairs={{0,4},{1,3},{2,6},{3,1},{4,0},{5,7},{6,2},{7,5},{8,12},{9,11},{10,... | collective-permute-start | bytes 1130504 | tf_op jit(solution)/shard_map/ppermute | solution.py:474
  528.6 7.7 %collective-permute-start.100 = (bf16[1,368,512]{2,1,0:T(8,128)(2,1)S(1)}, bf16[1,368,512]{2,1,0:T(8,128)(2,1)S(1)}, u32[]{:S(2)}, u32[]{:S(2)}) collective-permute-start(bf16[1,368,512]{2,1,0:T(8,128)(2,1)S(1)} %get-tuple-element.137), channel_id=1, source_target_pairs={{0,4},{1,3},{2,6},{3,1},{4,0},{5,7},{6,2},{7,5},{8,12},{9,11},{10,... | collective-permute-start | bytes 1130504 | tf_op jit(solution)/shard_map/ppermute | solution.py:474
  529.8 19.8 %collective-permute-start.107 = (bf16[1,368,512]{2,1,0:T(8,128)(2,1)S(1)}, bf16[1,368,512]{2,1,0:T(8,128)(2,1)S(1)}, u32[]{:S(2)}, u32[]{:S(2)}) collective-permute-start(bf16[1,368,512]{2,1,0:T(8,128)(2,1)S(1)} %get-tuple-element.145), channel_id=1, source_target_pairs={{0,8},{1,9},{2,10},{3,11},{4,12},{5,13},{6,14},{7,15},{8,0},{9,1},... | collective-permute-start | bytes 1130504 | tf_op jit(solution)/shard_map/ppermute | solution.py:474
  530.3 29.7 %collective-permute-start.109 = (bf16[2,272,512]{2,1,0:T(8,128)(2,1)S(1)}, bf16[2,272,512]{2,1,0:T(8,128)(2,1)S(1)}, u32[]{:S(2)}, u32[]{:S(2)}) collective-permute-start(bf16[2,272,512]{2,1,0:T(8,128)(2,1)S(1)} %copy-done.24), channel_id=1, source_target_pairs={{0,8},{1,9},{2,10},{3,11},{4,12},{5,13},{6,14},{7,15},{8,0},{9,1},... | collective-permute-start | bytes 1671176 | tf_op jit(solution)/shard_map/ppermute | solution.py:474
  532.0 28.3 %collective-permute-start.105 = (bf16[1,368,512]{2,1,0:T(8,128)(2,1)S(1)}, bf16[1,368,512]{2,1,0:T(8,128)(2,1)S(1)}, u32[]{:S(2)}, u32[]{:S(2)}) collective-permute-start(bf16[1,368,512]{2,1,0:T(8,128)(2,1)S(1)} %add_convert_fusion.2), channel_id=1, source_target_pairs={{0,8},{2,10},{4,12},{6,14},{16,24},{17,1},{18,26},{19,3},{20,28},{... | collective-permute-start | bytes 1130504 | tf_op jit(solution)/shard_map/ppermute | solution.py:474
  536.3 27.9 %collective-permute-start.101 = (bf16[1,368,512]{2,1,0:T(8,128)(2,1)S(1)}, bf16[1,368,512]{2,1,0:T(8,128)(2,1)S(1)}, u32[]{:S(2)}, u32[]{:S(2)}) collective-permute-start(bf16[1,368,512]{2,1,0:T(8,128)(2,1)S(1)} %add_convert_fusion.4), channel_id=1, source_target_pairs={{8,0},{10,2},{12,4},{14,6},{17,1},{19,3},{21,5},{23,7},{24,16},{25... | collective-permute-start | bytes 1130504 | tf_op jit(solution)/shard_map/ppermute | solution.py:474
  549.8 31.7 %collective-permute-start.108 = (bf16[1,368,512]{2,1,0:T(8,128)(2,1)S(1)}, bf16[1,368,512]{2,1,0:T(8,128)(2,1)S(1)}, u32[]{:S(2)}, u32[]{:S(2)}) collective-permute-start(bf16[1,368,512]{2,1,0:T(8,128)(2,1)S(1)} %add_convert_fusion), channel_id=1, source_target_pairs={{0,16},{1,17},{2,18},{3,19},{4,20},{5,21},{6,22},{7,23},{8,24},{9,... | collective-permute-start | bytes 1130504 | tf_op jit(solution)/shard_map/ppermute | solution.py:474
  560.2 20.2 %collective-permute-start.110 = (bf16[1,272,512]{2,1,0:T(8,128)(2,1)S(1)}, bf16[1,272,512]{2,1,0:T(8,128)(2,1)S(1)}, u32[]{:S(2)}, u32[]{:S(2)}) collective-permute-start(bf16[1,272,512]{2,1,0:T(8,128)(2,1)S(1)} %get-tuple-element.149), channel_id=1, source_target_pairs={{0,16},{1,17},{2,18},{3,19},{4,20},{5,21},{6,22},{7,23},{8,24},{9,... | collective-permute-start | bytes 835592 | tf_op jit(solution)/shard_map/ppermute | solution.py:474
  560.4 21.1 %collective-permute-start.106 = (bf16[1,368,512]{2,1,0:T(8,128)(2,1)S(1)}, bf16[1,368,512]{2,1,0:T(8,128)(2,1)S(1)}, u32[]{:S(2)}, u32[]{:S(2)}) collective-permute-start(bf16[1,368,512]{2,1,0:T(8,128)(2,1)S(1)} %add_convert_fusion.1), channel_id=1, source_target_pairs={{1,9},{3,11},{5,13},{7,15},{24,8},{26,10},{28,12},{30,14}} | collective-permute-start | bytes 1130504 | tf_op jit(solution)/shard_map/ppermute | solution.py:474
  564.3 20.2 %collective-permute-start.102 = (bf16[1,368,512]{2,1,0:T(8,128)(2,1)S(1)}, bf16[1,368,512]{2,1,0:T(8,128)(2,1)S(1)}, u32[]{:S(2)}, u32[]{:S(2)}) collective-permute-start(bf16[1,368,512]{2,1,0:T(8,128)(2,1)S(1)} %add_convert_fusion.3), channel_id=1, source_target_pairs={{9,1},{11,3},{13,5},{15,7},{16,0},{18,2},{20,4},{22,6}} | collective-permute-start | bytes 1130504 | tf_op jit(solution)/shard_map/ppermute | solution.py:474
  (178 other events, 1093.3 us)
Sparse Core Ops, SparseCore 0:
  11.4 96.4 all-gather.3
  111.4 78.9 all-gather.5
  193.2 80.1 all-gather.7
